TPU v7x, 128 devices: a whole 4x4x4 slice. The times are simulated.
128 devices in a mesh: grp: 4 (over z_hi, core), seq: 32 (over x, y, z_lo).
Axes of the slice: x: 4, y: 4, z: 4 (z_hi: 2, z_lo: 2; z = z_hi * 2 + z_lo), core: 2. Of those that a mesh axis runs over, the one named last changes fastest.
Arguments:
- inputs: bfloat16 [16, 4096, 512], P('grp', 'seq'), may hold values from -6 to 6
- history: int32 [16, 4096], P('grp', 'seq'), may hold values from 0 to 65535
- lengths: int32 [16], replicated, may hold values from 1024 to 4096
- w_joined: bfloat16 [512, 2048], replicated, may hold values from -0.25 to 0.25
- w_out: bfloat16 [512, 512], replicated, may hold values from -0.25 to 0.25
- neg_emb: bfloat16 [65536, 512], P(('grp', 'seq')), may hold values from -6 to 6
- neg_ids: int32 [65536], P(('grp', 'seq')), may hold values from 0 to 65535
Outputs:
- grad_joined: float32 [512, 2048], replicated
- grad_out: float32 [512, 512], replicated
- loss: float32 [], replicated
All inputs are finite; a program needn't handle non-finite values.
Results may differ from a plain program's by a relative error of at most 0.013.
Values may be sent and summed in bfloat16 or wider, within the bound.
A program may use at most 128 MiB of HBM per device.

v0:
```python
import jax
import jax.numpy as jnp
from jax import lax
from jax.sharding import PartitionSpec as P

HEADS = 8


eps_norm = 1e-06
logit_scale = 64.0


def passed_along(value, axis, steps):
    count = lax.axis_size(axis)
    initial, last = (max(0, -steps), min(count, count - steps))
    return lax.ppermute(value, axis, [(source, source + steps) for source in range(initial, last)])


def rounded(values):
    return lax.optimization_barrier(values.astype(jnp.bfloat16))


def layer_norm(values):
    centered = values - jnp.mean(values, axis=-1, keepdims=True)
    inv_std = lax.rsqrt(jnp.mean(centered * centered, axis=-1, keepdims=True) + eps_norm)
    return (centered * inv_std, inv_std)


def unit_rows(values):
    return values * lax.rsqrt(jnp.sum(values * values, axis=-1, keepdims=True) + eps_norm)


def silu_slope(values):
    sig_part = jax.nn.sigmoid(values)
    return sig_part * (1.0 + values * (1.0 - sig_part))


def local(inputs, history, lengths, w_joined, w_out, neg_emb, neg_ids):
    seqs_here, block, width = inputs.shape
    n_seq = lax.axis_size("seq")
    head_dim = width // HEADS
    rows = seqs_here * block
    length = block * n_seq
    seq_me = lax.axis_index("seq")
    grp_me = lax.axis_index("grp")
    x_float = inputs.reshape(rows, width).astype(jnp.float32)
    normed_in, _ = layer_norm(x_float)
    x_normed = normed_in.astype(jnp.bfloat16)
    pre_act = jnp.dot(x_normed, w_joined, preferred_element_type=jnp.float32)
    activated = jax.nn.silu(pre_act)
    u_part = rounded(activated[:, :width])
    packed = activated[:, width:].astype(jnp.bfloat16).reshape(seqs_here, block, 3, HEADS, head_dim)
    packed = packed.transpose(0, 3, 1, 2, 4).reshape(seqs_here * HEADS, block * 3 * head_dim)
    arrived = lax.all_to_all(packed, "seq", split_axis=0, concat_axis=0, tiled=True).reshape(
        length, 3, head_dim
    )
    v_head = arrived[:, 0]
    q_head = arrived[:, 1]
    k_head = arrived[:, 2]
    my_seq = grp_me * seqs_here + seq_me // HEADS
    seq_len = lax.dynamic_slice_in_dim(lengths, my_seq, 1)[0]
    len_float = seq_len.astype(jnp.float32)
    q_block = min(512, length)
    n_blocks = length // q_block
    key_pos = jnp.arange(length, dtype=jnp.int32)

    def block_scores(start):
        q_rows = lax.dynamic_slice_in_dim(q_head, start, q_block, 0)
        q_pos = start + jnp.arange(q_block, dtype=jnp.int32)
        key_mask = (key_pos[None, :] <= q_pos[:, None]) & (key_pos[None, :] < seq_len)
        scores = jnp.dot(q_rows, k_head.T, preferred_element_type=jnp.float32)
        att_probs = rounded(jnp.where(key_mask, jax.nn.silu(scores), 0.0) / len_float)
        return (q_rows, key_mask, scores, att_probs)

    def forward_block(index):
        _, _, _, att_probs = block_scores(index * q_block)
        return jnp.dot(att_probs, v_head, preferred_element_type=jnp.float32).astype(jnp.bfloat16)

    attended = lax.map(forward_block, jnp.arange(n_blocks, dtype=jnp.int32)).reshape(
        length, head_dim
    )
    returned = lax.all_to_all(
        attended.reshape(n_seq, block * head_dim), "seq", split_axis=0, concat_axis=0, tiled=True
    )
    returned = (
        returned.reshape(seqs_here, HEADS, block, head_dim)
        .transpose(0, 2, 1, 3)
        .reshape(rows, width)
    )
    normed, inv_att = layer_norm(returned.astype(jnp.float32))
    gated = (normed * u_part.astype(jnp.float32)).astype(jnp.bfloat16)
    out_rows = x_float + jnp.dot(gated, w_out, preferred_element_type=jnp.float32)
    inv_y = lax.rsqrt(jnp.sum(out_rows * out_rows, axis=-1, keepdims=True) + eps_norm)
    unit_y = out_rows * inv_y
    unit_b = rounded(unit_y)
    next_first, next_first_id = passed_along((inputs[:, 0, :], history[:, 0]), "seq", -1)
    x_next = (
        jnp.concatenate([inputs[:, 1:, :], next_first[:, None, :]], axis=1)
        .reshape(rows, width)
        .astype(jnp.float32)
    )
    id_next = jnp.concatenate([history[:, 1:], next_first_id[:, None]], axis=1).reshape(rows)
    pos_unit = rounded(unit_rows(x_next))
    neg_unit = rounded(unit_rows(neg_emb.astype(jnp.float32)))
    all_neg, all_ids = (
        lax.all_gather(neg_unit, "grp", axis=0, tiled=True),
        lax.all_gather(neg_ids, "grp", axis=0, tiled=True),
    )
    pos_logit = logit_scale * jnp.sum(
        unit_b.astype(jnp.float32) * pos_unit.astype(jnp.float32), axis=-1
    )
    neg_logit = logit_scale * jnp.dot(unit_b, all_neg.T, preferred_element_type=jnp.float32)
    hit_mask = all_ids[None, :] == id_next[:, None]
    neg_exp = jnp.where(hit_mask, 0.0, jnp.exp(neg_logit))
    pos_exp = jnp.exp(pos_logit)
    denom_sum = pos_exp + jnp.sum(neg_exp, axis=-1)
    group_lens = lax.dynamic_slice_in_dim(lengths, grp_me * seqs_here, seqs_here)
    row_len = jnp.repeat(group_lens, block)
    row_pos = seq_me * block + jnp.tile(jnp.arange(block, dtype=jnp.int32), seqs_here)
    valid = row_pos + 1 < row_len
    target_count = jnp.sum(lengths - 1).astype(jnp.float32)
    loss_sum = jnp.sum(jnp.where(valid, jnp.log(denom_sum) - pos_logit, 0.0))
    row_weight = jnp.where(valid, 1.0 / target_count, 0.0)
    d_pos = row_weight * (pos_exp / denom_sum - 1.0)
    d_neg = (row_weight[:, None] * neg_exp / denom_sum[:, None]).astype(jnp.bfloat16)
    neg_back = jnp.dot(d_neg, all_neg, preferred_element_type=jnp.float32)
    d_unit = logit_scale * (d_pos[:, None] * pos_unit.astype(jnp.float32) + neg_back)
    d_out = ((d_unit - unit_y * jnp.sum(unit_y * d_unit, axis=-1, keepdims=True)) * inv_y).astype(
        jnp.bfloat16
    )
    d_gate = jnp.dot(d_out, w_out.T, preferred_element_type=jnp.float32)
    grad_out_part = jnp.dot(gated.T, d_out, preferred_element_type=jnp.float32)
    d_u = d_gate * normed
    d_norm = d_gate * u_part.astype(jnp.float32)
    d_att = inv_att * (
        d_norm
        - jnp.mean(d_norm, axis=-1, keepdims=True)
        - normed * jnp.mean(d_norm * normed, axis=-1, keepdims=True)
    )
    d_att_send = (
        d_att.astype(jnp.bfloat16).reshape(seqs_here, block, HEADS, head_dim).transpose(0, 2, 1, 3)
    )
    d_att_head = lax.all_to_all(
        d_att_send.reshape(n_seq, block * head_dim), "seq", split_axis=0, concat_axis=0, tiled=True
    ).reshape(length, head_dim)

    def backward_block(carry, index):
        d_k_sum, d_v_sum = carry
        start = index * q_block
        q_rows, key_mask, scores, att_probs = block_scores(start)
        d_rows = lax.dynamic_slice_in_dim(d_att_head, start, q_block, 0)
        d_probs = jnp.dot(d_rows, v_head.T, preferred_element_type=jnp.float32)
        d_v_sum = d_v_sum + jnp.dot(att_probs.T, d_rows, preferred_element_type=jnp.float32)
        d_scores = (jnp.where(key_mask, d_probs * silu_slope(scores), 0.0) / len_float).astype(
            jnp.bfloat16
        )
        d_q_rows = jnp.dot(d_scores, k_head, preferred_element_type=jnp.float32).astype(
            jnp.bfloat16
        )
        d_k_sum = d_k_sum + jnp.dot(d_scores.T, q_rows, preferred_element_type=jnp.float32)
        return ((d_k_sum, d_v_sum), d_q_rows)

    zero_grad = jnp.zeros((length, head_dim), jnp.float32)
    (d_k_head, d_v_head), d_q_blocks = lax.scan(
        backward_block, (zero_grad, zero_grad), jnp.arange(n_blocks, dtype=jnp.int32)
    )
    d_q_head = d_q_blocks.reshape(length, head_dim)
    stacked = jnp.stack(
        [d_v_head.astype(jnp.bfloat16), d_q_head, d_k_head.astype(jnp.bfloat16)], axis=1
    )
    d_vqk = lax.all_to_all(
        stacked.reshape(n_seq, block * 3 * head_dim), "seq", split_axis=0, concat_axis=0, tiled=True
    )
    d_vqk = (
        d_vqk.reshape(seqs_here, HEADS, block, 3, head_dim)
        .transpose(0, 2, 3, 1, 4)
        .reshape(rows, 3 * width)
    )
    d_act = jnp.concatenate([d_u, d_vqk.astype(jnp.float32)], axis=-1)
    d_pre = (d_act * silu_slope(pre_act)).astype(jnp.bfloat16)
    grad_joined_part = jnp.dot(x_normed.T, d_pre, preferred_element_type=jnp.float32)
    grad_joined, grad_out, loss_total = lax.psum(
        (grad_joined_part, grad_out_part, loss_sum), ("grp", "seq")
    )
    return (grad_joined, grad_out, loss_total / target_count)


def solution(mesh):
    placed = (
        P("grp", "seq", None),
        P("grp", "seq"),
        P(),
        P(),
        P(),
        P(("grp", "seq"), None),
        P(("grp", "seq")),
    )
    return jax.shard_map(
        local, mesh=mesh, in_specs=placed, out_specs=(P(), P(), P()), check_vma=False
    )
```

profile of v0, /device:TPU:1, one launch (start us, length us, event | category | flops | bytes accessed | tf_op | source)
XLA Modules:
  0.0 738.2 jit_solution(7396211202704488660)
XLA Ops:
  22.0 7.5 %copy.61 = bf16[4,8,128,3,64]{4,3,2,1,0:T(4,128)(2,1)} copy(bf16[4,8,128,3,64]{2,0,4,1,3:T(4,128)(2,1)} %bitcast.122) | data formatting | bytes 3145728 | tf_op jit(solution)/shard_map/transpose | solution.py:53
  29.4 11.1 %all_to_all.32 = bf16[32,1,24576]{2,1,0:T(2,128)(2,1)} reshape(bf16[4,8,128,3,64]{4,3,2,1,0:T(4,128)(2,1)} %copy.61) | data formatting | bytes 3145728 | tf_op jit(solution)/shard_map/all_to_all | solution.py:54
  41.0 11.8 %reduce.17 = bf16[32,24576]{1,0:T(8,128)(2,1)S(1)} reduce(bf16[32,1,24576]{2,1,0:T(2,128)(2,1)} %all_to_all.32, bf16[]{:T(256)} %broadcast.241), dimensions={1}, to_apply=%all_to_all.32.reduce_sub_computation | reduce | bytes 3145730 | tf_op jit(solution)/shard_map/all_to_all | solution.py:54
  54.9 9.3 %all-to-all-start = ((bf16[32,2,12288]{2,1,0:T(2,128)(2,1)}), bf16[32,2,12288]{2,1,0:T(2,128)(2,1)S(1)}, u32[]{:S(2)}, u32[]{:S(2)}) async-start(bf16[32,2,12288]{2,1,0:T(2,128)(2,1)} %reshape.249), calls=%async_computation | async-start | bytes 3145728 | tf_op jit(solution)/shard_map/all_to_all | solution.py:54
  73.6 7.9 %all-gather = s32[4,1,512]{2,1,0:T(1,128)} all-gather(s32[1,1,512]{2,1,0:T(1,128)S(1)} %bitcast.128), channel_id=1, replica_groups=mesh['grp'=4,'seq'=32] {'grp'}, dimensions={0}, use_global_device_ids=true | all-gather | bytes 10240 | tf_op jit(solution)/shard_map/all_gather | solution.py:107
  91.1 11.2 %reduce.9 = bf16[32,24576]{1,0:T(8,128)(2,1)S(1)} reduce(bf16[32,1,24576]{2,1,0:T(2,128)(2,1)} %reshape.250, bf16[]{:T(256)} %constant.97), dimensions={1}, to_apply=%all_to_all.25.reduce_sub_computation | reduce | bytes 3145730 | tf_op jit(solution)/shard_map/all_to_all | solution.py:54
  107.1 10.3 %fusion.38 = (bf16[4096,1,64]{2,1,0:T(2,128)(2,1)S(1)}, bf16[4096,1,64]{2,1,0:T(2,128)(2,1)S(1)}, bf16[4096,1,64]{2,1,0:T(2,128)(2,1)S(1)}) fusion(bf16[4096,3,64]{2,1,0:T(4,128)(2,1)} %reshape.230), kind=kLoop, calls=%fused_computation.103 | loop fusion | bytes 3145728 | tf_op jit(solution)/shard_map/slice | solution.py:57
  118.8 64.0 %while.28 = (s32[]{:T(128)}, bf16[8,512,64]{1,2,0:T(8,128)(2,1)S(1)}, s32[8]{0:T(128)S(1)}, s32[]{:T(128)}, bf16[4096,64]{1,0:T(8,128)(2,1)}, /*index=5*/bf16[40...) while((s32[]{:T(128)}, ...), condition=%wide.region_4.5_spmd.clone.clone, body=%wide.region_3.4_spmd.clone.clone.sunk | while | flops 555782656 | bytes 10171071 | solution.py:79
  194.9 13.3 %all-to-all-start.1 = ((bf16[32,2,4096]{2,1,0:T(2,128)(2,1)}), bf16[32,2,4096]{2,1,0:T(2,128)(2,1)S(1)}, u32[]{:S(2)}, u32[]{:S(2)}) async-start(bf16[32,2,4096]{2,1,0:T(2,128)(2,1)} %reshape.251), calls=%async_computation.1 | async-start | bytes 1048576 | tf_op jit(solution)/shard_map/all_to_all | solution.py:82
  210.6 8.6 %all-to-all-done.1 = bf16[32,2,4096]{2,1,0:T(2,128)(2,1)S(1)} async-done(((bf16[32,2,4096]{2,1,0:T(2,128)(2,1)}), bf16[32,2,4096]{2,1,0:T(2,128)(2,1)S(1)}, u32[]{:S(2)}, u32[]{:S(2)}) %all-to-all-start.1) | async-done | bytes 524320 | tf_op jit(solution)/shard_map/all_to_all | solution.py:82
  252.7 9.8 %all-to-all-done.2 = bf16[32,2,4096]{2,1,0:T(2,128)(2,1)} async-done(((bf16[32,2,4096]{2,1,0:T(2,128)(2,1)}), bf16[32,2,4096]{2,1,0:T(2,128)(2,1)}, u32[]{:S(2)}, u32[]{:S(2)}) %all-to-all-start.2) | async-done | bytes 524320 | tf_op jit(solution)/shard_map/all_to_all | solution.py:143
  275.7 187.6 %while.29 = (s32[]{:T(128)}, f32[4096,64]{0,1:T(8,128)S(1)}, f32[4096,64]{0,1:T(8,128)S(1)}, bf16[8,512,64]{1,2,0:T(8,128)(2,1)}, s32[8]{0:T(128)S(1)}, /*index=...) while((s32[]{:T(128)}, f32[4096,64]{0,1:T(8,128)S(1)}, ...), condition=%wide.region_16.17_spmd.clone.clone, body=%wide.region_15.16_spmd.clone.clone.sunk | while | flops 1389400576 | bytes 80301880 | solution.py:164
  284.2 7.2 divide_convert_fusion.14
  307.7 7.2 divide_convert_fusion.14
  331.1 7.2 divide_convert_fusion.14
  425.0 7.2 divide_convert_fusion.14
  470.0 11.3 %all_to_all.35 = bf16[32,1,24576]{2,1,0:T(2,128)(2,1)} reshape(bf16[4096,3,64]{2,1,0:T(4,128)(2,1)} %copy.85) | data formatting | bytes 3145728 | tf_op jit(solution)/shard_map/all_to_all | solution.py:171
  481.3 11.8 %reduce.20 = bf16[32,24576]{1,0:T(8,128)(2,1)S(1)} reduce(bf16[32,1,24576]{2,1,0:T(2,128)(2,1)} %all_to_all.35, bf16[]{:T(256)} %broadcast.241), dimensions={1}, to_apply=%all_to_all.35.reduce_sub_computation | reduce | bytes 3145730 | tf_op jit(solution)/shard_map/all_to_all | solution.py:171
  500.7 18.1 %all-to-all-done.3 = bf16[32,2,12288]{2,1,0:T(2,128)(2,1)S(1)} async-done(((bf16[32,2,12288]{2,1,0:T(2,128)(2,1)}), bf16[32,2,12288]{2,1,0:T(2,128)(2,1)S(1)}, u32[]{:S(2)}, u32[]{:S(2)}) %all-to-all-start.3) | async-done | bytes 1572896 | tf_op jit(solution)/shard_map/all_to_all | solution.py:171
  523.1 12.8 %convert_reduce_fusion = f32[32,24576]{1,0:T(8,128)} fusion(bf16[32,1,24576]{2,1,0:T(2,128)(2,1)} %reshape.256), kind=kLoop, calls=%fused_computation.39 | loop fusion | flops 786432 | bytes 4718592 | tf_op jit(solution)/shard_map/convert_element_type | solution.py:179
  535.9 8.1 %reshape.239 = f32[4,8,128,3,64]{4,3,2,1,0:T(4,128)} reshape(f32[32,24576]{1,0:T(8,128)} %convert_reduce_fusion) | data formatting | bytes 6291456 | tf_op jit(solution)/shard_map/convert_element_type | solution.py:179
  544.0 9.7 %copy.99 = f32[4,128,3,8,64]{4,3,2,1,0:T(8,128)} copy(f32[4,128,3,8,64]{4,2,1,3,0:T(4,128)} %bitcast.119) | data formatting | bytes 6291456 | tf_op jit(solution)/shard_map/convert_element_type | solution.py:179
  567.2 66.0 %psum.23 = f32[]{:T(128)} all-reduce(f32[]{:T(128)} %get-tuple-element.317), channel_id=1, replica_groups=mesh['grp'=4,'seq'=32] {'grp','seq'}, use_global_device_ids=true, to_apply=%region_20.21 | all-reduce | flops 1 | bytes 8 | tf_op jit(solution)/shard_map/psum | solution.py:182
  633.9 90.4 %all-reduce.3.cloned.1.call-done = (f32[512,2048]{1,0:T(8,128)}, f32[512,512]{1,0:T(8,128)}) async-done(((f32[512,2048]{1,0:T(8,128)}, f32[512,512]{1,0:T(8,128)}), (f32[512,2048]{1,0:T(8,128)}, f32[512,512]{1,0:T(8,128)})) %all-reduce.3.cloned.1.call-update) | async-done | bytes 5242896 | tf_op jit(solution)/shard_map/psum | solution.py:182
  (335 shorter events, 351.0 us)
Async XLA Ops:
  52.8 12.1 %copy-start.21 = (bf16[512,512]{1,0:T(8,128)(2,1)S(1)}, bf16[512,512]{1,0:T(8,128)(2,1)}, u32[]{:S(2)}) copy-start(bf16[512,512]{1,0:T(8,128)(2,1)} %param.16) | copy-start | bytes 1572868
  52.8 13.3 %copy-start.32 = (s32[4,128]{1,0:T(4,128)S(1)}, s32[4,128]{1,0:T(4,128)}, u32[]{:S(2)}) copy-start(s32[4,128]{1,0:T(4,128)} %param.12) | copy-start | bytes 6148
  52.8 14.7 %copy-start.8 = (bf16[4,128,512]{2,1,0:T(8,128)(2,1)S(1)}, bf16[4,128,512]{2,1,0:T(8,128)(2,1)}, u32[]{:S(2)}) copy-start(bf16[4,128,512]{2,1,0:T(8,128)(2,1)} %param.11) | copy-start | bytes 1572868
  54.9 16.0 %copy-start.44 = (s32[16]{0:T(128)S(1)}, s32[16]{0:T(128)}, u32[]{:S(2)}) copy-start(s32[16]{0:T(128)} %param.13) | copy-start | bytes 196
  54.9 18.6 %copy-start.33 = (s32[512]{0:T(512)S(1)}, s32[512]{0:T(512)}, u32[]{:S(2)}) copy-start(s32[512]{0:T(512)} %param.17) | copy-start | bytes 6148
  54.9 32.2 %all-to-all-start = ((bf16[32,2,12288]{2,1,0:T(2,128)(2,1)}), bf16[32,2,12288]{2,1,0:T(2,128)(2,1)S(1)}, u32[]{:S(2)}, u32[]{:S(2)}) async-start(bf16[32,2,12288]{2,1,0:T(2,128)(2,1)} %reshape.249), calls=%async_computation | async-start | bytes 3145728 | tf_op jit(solution)/shard_map/all_to_all | solution.py:54
  64.3 166.6 %all-gather.3.cloned.1.call-start = ((), (), s32[]{:S(2)}) async-start(), calls=%async_computation.4 | async-start | bytes 2621440 | tf_op jit(solution)/shard_map/all_gather | solution.py:106
  66.2 16.5 %collective-permute-start.1 = (s32[4]{0:T(128)S(1)}, s32[4]{0:T(128)S(1)}, u32[]{:S(2)}, u32[]{:S(2)}) collective-permute-start(s32[4]{0:T(128)S(1)} %slice_reduce_fusion), channel_id=1, source_target_pairs={{1,0},{2,1},{3,2},{4,3},{5,4},{6,5},{7,6},{8,7},{9,8},{10,9},{11,1... | collective-permute-start | bytes 56 | tf_op jit(solution)/shard_map/ppermute | solution.py:16
  67.6 15.9 %collective-permute-start = (bf16[4,512]{1,0:T(4,128)(2,1)S(1)}, bf16[4,512]{1,0:T(4,128)(2,1)S(1)}, u32[]{:S(2)}, u32[]{:S(2)}) collective-permute-start(bf16[4,512]{1,0:T(4,128)(2,1)S(1)} %bitcast.126), channel_id=1, source_target_pairs={{1,0},{2,1},{3,2},{4,3},{5,4},{6,5},{7,6},{8,7},{9,8},{10,9},{11,1... | collective-permute-start | bytes 12296 | tf_op jit(solution)/shard_map/ppermute | solution.py:16
  70.9 20.2 %copy-start.11 = (bf16[4,127,512]{2,1,0:T(8,128)(2,1)}, bf16[4,127,512]{2,1,0:T(8,128)(2,1)S(1)}, u32[]{:S(2)}) copy-start(bf16[4,127,512]{2,1,0:T(8,128)(2,1)S(1)} %slice.34) | copy-start | bytes 1560580
  72.2 18.9 %copy-start.40 = (s32[4]{0:T(128)}, s32[4]{0:T(128)S(1)}, u32[]{:S(2)}) copy-start(s32[4]{0:T(128)S(1)} %dynamic_slice.22) | copy-start | bytes 52
  182.8 27.7 %copy-start.4 = (bf16[4096,64]{1,0:T(8,128)(2,1)}, bf16[4096,64]{1,0:T(8,128)(2,1)S(1)}, u32[]{:S(2)}) copy-start(bf16[4096,64]{1,0:T(8,128)(2,1)S(1)} %get-tuple-element.544) | copy-start | bytes 1572868
  182.9 27.7 %copy-start.6 = (bf16[4096,64]{1,0:T(8,128)(2,1)}, bf16[4096,64]{1,0:T(8,128)(2,1)S(1)}, u32[]{:S(2)}) copy-start(bf16[4096,64]{1,0:T(8,128)(2,1)S(1)} %get-tuple-element.545) | copy-start | bytes 1572868
  182.9 25.3 %copy-start.12 = (bf16[4,127,512]{2,1,0:T(8,128)(2,1)S(1)}, bf16[4,127,512]{2,1,0:T(8,128)(2,1)}, u32[]{:S(2)}) copy-start(bf16[4,127,512]{2,1,0:T(8,128)(2,1)} %copy-done.11) | copy-start | bytes 1560580
  182.9 25.3 %copy-start.30 = (bf16[4,1,512]{2,1,0:T(2,128)(2,1)S(1)}, bf16[4,1,512]{2,1,0:T(2,128)(2,1)}, u32[]{:S(2)}) copy-start(bf16[4,1,512]{2,1,0:T(2,128)(2,1)} %copy-done.29) | copy-start | bytes 12292
  194.9 24.3 %all-to-all-start.1 = ((bf16[32,2,4096]{2,1,0:T(2,128)(2,1)}), bf16[32,2,4096]{2,1,0:T(2,128)(2,1)S(1)}, u32[]{:S(2)}, u32[]{:S(2)}) async-start(bf16[32,2,4096]{2,1,0:T(2,128)(2,1)} %reshape.251), calls=%async_computation.1 | async-start | bytes 1048576 | tf_op jit(solution)/shard_map/all_to_all | solution.py:82
  242.9 32.8 %copy-start.5 = (bf16[4096,64]{1,0:T(8,128)(2,1)S(1)}, bf16[4096,64]{1,0:T(8,128)(2,1)}, u32[]{:S(2)}) copy-start(bf16[4096,64]{1,0:T(8,128)(2,1)} %copy-done.4) | copy-start | bytes 1572868
  247.9 14.7 %all-to-all-start.2 = ((bf16[32,2,4096]{2,1,0:T(2,128)(2,1)}), bf16[32,2,4096]{2,1,0:T(2,128)(2,1)}, u32[]{:S(2)}, u32[]{:S(2)}) async-start(bf16[32,2,4096]{2,1,0:T(2,128)(2,1)} %reshape.253), calls=%async_computation.2 | async-start | bytes 1048576 | tf_op jit(solution)/shard_map/all_to_all | solution.py:143
  495.2 23.6 %all-to-all-start.3 = ((bf16[32,2,12288]{2,1,0:T(2,128)(2,1)}), bf16[32,2,12288]{2,1,0:T(2,128)(2,1)S(1)}, u32[]{:S(2)}, u32[]{:S(2)}) async-start(bf16[32,2,12288]{2,1,0:T(2,128)(2,1)} %reshape.255), calls=%async_computation.3 | async-start | bytes 3145728 | tf_op jit(solution)/shard_map/all_to_all | solution.py:171
  499.2 225.1 %all-reduce.3.cloned.1.call-start = ((), (), s32[]{:S(2)}) async-start(), calls=%async_computation.5 | async-start | bytes 10485760 | tf_op jit(solution)/shard_map/psum | solution.py:182
  553.7 6.4 copy-start.19
  553.7 6.4 copy-start.28
  553.7 6.4 copy-start.35
  553.7 6.4 copy-start.39
  (50 other events, 169.9 us)
Sparse Core Ops, SparseCore 0:
  66.8 34.9 all-gather.2
  567.4 156.8 all-reduce.2
where the time goes:
time: 744 us; the launch traced here: 738 us
  matrix products  236 us (32%)
  local copies, waits for them, and re-layouts  149 us (20%)
  waiting for transfers between devices  127 us (17%)
  other arithmetic  87.6 us (12%)
  blocking collectives  73.9 us (10%)
  starting transfers between devices  34.7 us (5%)
  between operations  18.1 us (2%)
  loops' own time  11.5 us (2%)
    dot_general x16, matrix products, block_scores(): scores = jnp.dot(q_rows, k_head.T, preferred_element_type=jnp.float32)  90.5 us
    psum x1, waiting for transfers between devices, local(): lax.psum((grad_joined_part, grad_out_part, loss_sum), ('grp', 'seq'))  90.4 us
    psum x1, blocking collectives, local(): lax.psum((grad_joined_part, grad_out_part, loss_sum), ('grp', 'seq'))  66 us
    dot_general x8, matrix products, backward_block(): d_probs = jnp.dot(d_rows, v_head.T, preferred_element_type=jnp.float32)  57.6 us
    unnamed x96, local copies, waits for them, and re-layouts  28.6 us
    dot_general x8, matrix products, backward_block(): jnp.dot(d_scores.T, q_rows, preferred_element_type=jnp.float32)  26.7 us
    convert_element_type x3, local copies, waits for them, and re-layouts, local(): d_act = jnp.concatenate([d_u, d_vqk.astype(jnp.float32)], axis=-1)  24.1 us
    all_to_all x2, other arithmetic, local(): lax.all_to_all(packed, 'seq', split_axis=0, concat_axis=0, tiled=True)  23 us
  transfers between devices with their start and end apart: 8, of which 4 were waited for; matrix products, arithmetic and copies ran while one was open for 17% of the time, Pallas kernels for 0%

commit v1 on v0

v1 whole, which is shorter than its diff:
```python
import functools

import jax
import jax.numpy as jnp
from jax import lax
from jax.experimental import pallas as pl
from jax.experimental.pallas import tpu as pltpu
from jax.sharding import PartitionSpec as P

HEADS = 8
HEAD = 64
WIDTH = 512
PAIRS = 4
BLOCK = 128
TILE = 512
eps_norm = 1e-06
logit_scale = 64.0

MESH = pl.DeviceIdType.MESH
F32 = jnp.float32
BF16 = jnp.bfloat16
VMEM = pl.BlockSpec(memory_space=pltpu.VMEM)
SMEM = pl.BlockSpec(memory_space=pltpu.SMEM)


def dot_nn(a, b):
    return lax.dot_general(a, b, (((1,), (0,)), ((), ())), preferred_element_type=F32)


def dot_nt(a, b):
    return lax.dot_general(a, b, (((1,), (1,)), ((), ())), preferred_element_type=F32)


def dot_tn(a, b):
    return lax.dot_general(a, b, (((0,), (0,)), ((), ())), preferred_element_type=F32)


def low_lanes(shape):
    return lax.broadcasted_iota(jnp.int32, shape, 1) < HEAD


def turned(a):
    return pltpu.roll(a, HEAD, axis=1)


def swapped(a, b):
    low = low_lanes(a.shape)
    return jnp.where(low, a, turned(b)), jnp.where(low, turned(a), b)


def seq_barrier(me, n_seq):
    barrier = pltpu.get_barrier_semaphore()

    @pl.loop(1, n_seq)
    def _(step):
        pl.semaphore_signal(
            barrier, inc=1, device_id={"seq": lax.rem(me + step, n_seq)}, device_id_type=MESH
        )

    pl.semaphore_wait(barrier, n_seq - 1)


def push(src, dst, send_sem, recv_sem, where):
    pltpu.make_async_remote_copy(
        src_ref=src, dst_ref=dst, send_sem=send_sem, recv_sem=recv_sem,
        device_id=where, device_id_type=MESH,
    ).start()


def await_bytes(ref, sem):
    pltpu.make_async_copy(ref, ref, sem).wait()


def project_kernel(n_seq, x_ref, w_ref, xn_ref, u_ref, slope_ref, got_ref, send_ref, send_sem, recv_sem):
    me = lax.axis_index("seq")
    n_here = x_ref.shape[0]
    seq_barrier(me, n_seq)

    @pl.loop(0, n_here)
    def _(step):
        b = lax.rem(me // HEADS + step, n_here)
        x = x_ref[b].astype(F32)
        centered = x - jnp.mean(x, axis=-1, keepdims=True)
        var = jnp.mean(centered * centered, axis=-1, keepdims=True)
        xn = (centered * lax.rsqrt(var + eps_norm)).astype(BF16)
        xn_ref[b] = xn

        def activated(part):
            half = 0.5 * dot_nn(xn, w_ref[:, part * WIDTH:(part + 1) * WIDTH])
            th = jnp.tanh(half)
            slope = (0.5 + 0.5 * th) * (1.0 + half * (1.0 - th))
            slope_ref[b, :, part * WIDTH:(part + 1) * WIDTH] = slope.astype(BF16)
            return half + half * th

        v = activated(1)
        q = activated(2)
        k = activated(3)
        for pair in range(PAIRS):
            cols = slice(pair * 2 * HEAD, (pair + 1) * 2 * HEAD)
            kv = swapped(k[:, cols], v[:, cols])
            qs = swapped(q[:HEAD, cols], q[HEAD:, cols])
            for odd in range(2):
                j = b * HEADS + 2 * pair + odd
                send_ref[j, :BLOCK] = kv[odd].astype(BF16)
                send_ref[j, BLOCK:] = qs[odd].astype(BF16)

        @pl.loop(0, HEADS)
        def _(turn):
            j = b * HEADS + lax.rem(me + turn, HEADS)

            @pl.when(j != me)
            def _():
                push(send_ref.at[j], got_ref.at[me], send_sem, recv_sem, {"seq": j})

            @pl.when(j == me)
            def _():
                got_ref[me] = send_ref[me]

        u_ref[b] = activated(0).astype(BF16)

    await_bytes(send_ref.at[pl.ds(0, n_seq - 1)], send_sem)
    await_bytes(got_ref.at[pl.ds(0, n_seq - 1)], recv_sem)


def own_length(lens_ref, me, n_here):
    return lens_ref[lax.axis_index("grp") * n_here + me // HEADS]


def forward_kernel(n_seq, n_here, lens_ref, got_ref, back_ref, kv_ref, q_ref, acc_ref, send_ref, send_sem, recv_sem):
    me = lax.axis_index("seq")
    seq_barrier(me, n_seq)
    length = own_length(lens_ref, me, n_here)
    n_tiles = n_seq * BLOCK // TILE
    per_tile = TILE // BLOCK

    @pl.loop(0, n_seq)
    def _(i):
        rows = pl.ds(pl.multiple_of(i * BLOCK, BLOCK), BLOCK)
        pos = i * BLOCK + lax.broadcasted_iota(jnp.int32, (BLOCK, 2 * HEAD), 0)
        kv = got_ref[i, :BLOCK].astype(F32)
        kv_ref[rows] = jnp.where(pos < length, kv, 0.0).astype(BF16)
        q = got_ref[i, BLOCK:].astype(F32) * 0.5
        low = low_lanes(q.shape)
        q_ref[rows] = jnp.concatenate(
            [jnp.where(low, q, 0.0), jnp.where(low, turned(q), 0.0)], axis=0
        ).astype(BF16)

    inv_len = 1.0 / jnp.full((1, 2 * HEAD), length, jnp.int32).astype(F32)

    def probs(half):
        return (half + half * jnp.tanh(half)).astype(BF16)

    sub = TILE // 2

    @pl.loop(0, n_tiles)
    def _(step):
        c = lax.rem(me // per_tile + step, n_tiles)
        start = pl.multiple_of(c * TILE, TILE)
        q = q_ref[pl.ds(start, TILE)]
        kv_a = kv_ref[pl.ds(start, sub)]
        kv_b = kv_ref[pl.ds(start + sub, sub)]
        seen = lax.broadcasted_iota(jnp.int32, (sub, sub), 1) <= lax.broadcasted_iota(
            jnp.int32, (sub, sub), 0
        )
        acc_ref[:sub] = dot_nn(probs(jnp.where(seen, dot_nt(q[:sub], kv_a), 0.0)), kv_a)
        acc_ref[sub:] = dot_nn(probs(dot_nt(q[sub:], kv_a)), kv_a) + dot_nn(
            probs(jnp.where(seen, dot_nt(q[sub:], kv_b), 0.0)), kv_b
        )

        @pl.loop(0, c)
        def _(other):
            kv = kv_ref[pl.ds(pl.multiple_of(other * TILE, TILE), TILE)]
            acc_ref[...] += dot_nn(probs(dot_nt(q, kv)), kv)

        for u in range(per_tile):
            out = acc_ref[u * BLOCK:(u + 1) * BLOCK] * inv_len
            top, bottom = out[:HEAD], out[HEAD:]
            send_ref[c * per_tile + u] = jnp.where(
                low_lanes(top.shape), turned(top), bottom
            ).astype(BF16)

        @pl.loop(0, per_tile)
        def _(turn):
            i = c * per_tile + lax.rem(me + turn, per_tile)

            @pl.when(i != me)
            def _():
                push(send_ref.at[i], back_ref.at[me], send_sem, recv_sem, {"seq": i})

            @pl.when(i == me)
            def _():
                back_ref[me] = send_ref[me]

    await_bytes(send_ref.at[pl.ds(0, n_seq - 1)], send_sem)
    await_bytes(back_ref.at[pl.ds(0, n_seq - 1)], recv_sem)


def middle_kernel(
    n_seq, lens_ref, back_ref, x_ref, first_ref, id_next_ref, neg_ref, neg_ids_ref, w_out_ref, u_ref,
    slope_ref, got_ref, d_pre_ref, grad_ref, loss_ref, att_ref, exp_ref, send_ref, send_sem, recv_sem,
):
    me = lax.axis_index("seq")
    grp = lax.axis_index("grp")
    seq_barrier(me, n_seq)
    n_here = x_ref.shape[0]
    both = 2
    rows = both * BLOCK
    n_neg = neg_ref.shape[0]
    n_halves = n_here // both

    total = lens_ref[0] - 1
    for at in range(1, lens_ref.shape[0]):
        total = total + (lens_ref[at] - 1)
    weight = 1.0 / jnp.full((rows, 1), total, jnp.int32).astype(F32)
    grad_ref[...] = jnp.zeros_like(grad_ref)
    loss_ref[...] = jnp.zeros_like(loss_ref)

    @pl.loop(0, n_halves)
    def _(step):
        first_b = both * lax.rem(me // (both * HEADS) + step, n_halves)
        for e in range(both):
            for pair in range(PAIRS):
                j = (first_b + e) * HEADS + 2 * pair
                top, bottom = swapped(back_ref[j].astype(F32), back_ref[j + 1].astype(F32))
                cols = slice(pair * 2 * HEAD, (pair + 1) * 2 * HEAD)
                att_ref[e * BLOCK:e * BLOCK + HEAD, cols] = top
                att_ref[e * BLOCK + HEAD:(e + 1) * BLOCK, cols] = bottom

        def joined(make):
            return jnp.concatenate([make(e) for e in range(both)], axis=0)

        att = att_ref[...]
        centered = att - jnp.mean(att, axis=-1, keepdims=True)
        inv_att = lax.rsqrt(jnp.mean(centered * centered, axis=-1, keepdims=True) + eps_norm)
        normed = centered * inv_att
        u = joined(lambda e: u_ref[first_b + e]).astype(F32)
        gated = (normed * u).astype(BF16)
        x = joined(lambda e: x_ref[first_b + e]).astype(F32)
        out_rows = x + dot_nn(gated, w_out_ref[...])
        inv_y = lax.rsqrt(jnp.sum(out_rows * out_rows, axis=-1, keepdims=True) + eps_norm)
        unit_y = out_rows * inv_y
        unit_b = unit_y.astype(BF16)

        def next_rows(e):
            mine = x_ref[first_b + e].astype(F32)
            shifted = pltpu.roll(mine, BLOCK - 1, axis=0)
            is_last = lax.broadcasted_iota(jnp.int32, mine.shape, 0) == BLOCK - 1
            return jnp.where(is_last, first_ref[first_b + e].astype(F32)[:1], shifted)

        x_next = joined(next_rows)
        pos_unit = (
            x_next * lax.rsqrt(jnp.sum(x_next * x_next, axis=-1, keepdims=True) + eps_norm)
        ).astype(BF16).astype(F32)
        pos_logit = logit_scale * jnp.sum(unit_b.astype(F32) * pos_unit, axis=-1, keepdims=True)

        def row_ids(e):
            ids = id_next_ref[first_b + e][:1]
            return jnp.transpose(jnp.broadcast_to(ids, (BLOCK, BLOCK)))

        ids = joined(row_ids)
        lane_sum = jnp.zeros((rows, BLOCK), F32)
        for part in range(n_neg // WIDTH):
            neg_logit = logit_scale * dot_nt(unit_b, neg_ref[part * WIDTH:(part + 1) * WIDTH])
            for sub in range(WIDTH // BLOCK):
                at = part * (WIDTH // BLOCK) + sub
                hit = neg_ids_ref[at:at + 1] == ids
                exps = jnp.where(hit, 0.0, jnp.exp(neg_logit[:, sub * BLOCK:(sub + 1) * BLOCK]))
                exp_ref[:, at * BLOCK:(at + 1) * BLOCK] = exps
                lane_sum = lane_sum + exps
        pos_exp = jnp.exp(pos_logit)
        denom = pos_exp + jnp.sum(lane_sum, axis=-1, keepdims=True)

        def row_valid(e):
            seq_len = lens_ref[grp * n_here + first_b + e]
            pos = me * BLOCK + lax.broadcasted_iota(jnp.int32, (BLOCK, 1), 0)
            return jnp.where(pos + 1 < seq_len, 1.0, 0.0)

        valid = joined(row_valid)
        row_loss = jnp.where(valid > 0.0, jnp.log(denom) - pos_logit, 0.0)
        loss_ref[...] += jnp.broadcast_to(jnp.sum(row_loss, axis=0, keepdims=True), loss_ref.shape)
        row_weight = valid * weight
        d_pos = row_weight * (pos_exp / denom - 1.0)
        scale = row_weight / denom
        neg_back = jnp.zeros((rows, WIDTH), F32)
        for part in range(n_neg // WIDTH):
            d_neg = (scale * exp_ref[:, part * WIDTH:(part + 1) * WIDTH]).astype(BF16)
            neg_back = neg_back + dot_nn(d_neg, neg_ref[part * WIDTH:(part + 1) * WIDTH])
        d_unit = logit_scale * (d_pos * pos_unit + neg_back)
        d_out = (
            (d_unit - unit_y * jnp.sum(unit_y * d_unit, axis=-1, keepdims=True)) * inv_y
        ).astype(BF16)
        d_gate = dot_nt(d_out, w_out_ref[...])
        d_norm = d_gate * u
        d_att = inv_att * (
            d_norm
            - jnp.mean(d_norm, axis=-1, keepdims=True)
            - normed * jnp.mean(d_norm * normed, axis=-1, keepdims=True)
        )
        for e in range(both):
            mine = d_att[e * BLOCK:(e + 1) * BLOCK]
            for pair in range(PAIRS):
                cols = slice(pair * 2 * HEAD, (pair + 1) * 2 * HEAD)
                packed = swapped(mine[:HEAD, cols], mine[HEAD:, cols])
                for odd in range(2):
                    send_ref[(first_b + e) * HEADS + 2 * pair + odd] = packed[odd].astype(BF16)

        @pl.loop(0, both * HEADS)
        def _(turn):
            j = first_b * HEADS + lax.rem(me + turn, both * HEADS)

            @pl.when(j != me)
            def _():
                push(send_ref.at[j], got_ref.at[me], send_sem, recv_sem, {"seq": j})

            @pl.when(j == me)
            def _():
                got_ref[me] = send_ref[me]

        grad_ref[...] += dot_tn(gated, d_out)
        d_u = d_gate * normed
        for e in range(both):
            slope = slope_ref[first_b + e, :, :WIDTH].astype(F32)
            d_pre_ref[first_b + e] = (d_u[e * BLOCK:(e + 1) * BLOCK] * slope).astype(BF16)

    await_bytes(send_ref.at[pl.ds(0, n_seq - 1)], send_sem)
    await_bytes(got_ref.at[pl.ds(0, n_seq - 1)], recv_sem)


def backward_kernel(
    n_seq, n_here, lens_ref, got_ref, datt_ref, back_ref, qa_ref, lhs_ref, kt_ref, dq_ref, dkv_ref,
    send_ref, kv_send_sem, q_send_sem, kv_recv_sem, q_recv_sem,
):
    me = lax.axis_index("seq")
    seq_barrier(me, n_seq)
    length = own_length(lens_ref, me, n_here)
    n_tiles = n_seq * BLOCK // TILE
    per_tile = TILE // BLOCK

    @pl.loop(0, n_seq)
    def _(i):
        rows = pl.ds(pl.multiple_of(i * BLOCK, BLOCK), BLOCK)
        pos = i * BLOCK + lax.broadcasted_iota(jnp.int32, (BLOCK, 2 * HEAD), 0)
        kv = jnp.where(pos < length, got_ref[i, :BLOCK].astype(F32), 0.0)
        low = low_lanes(kv.shape)
        tile = i // per_tile
        at = pl.multiple_of(lax.rem(i, per_tile) * BLOCK, BLOCK)
        lhs_ref[tile, pl.ds(at, BLOCK)] = jnp.where(low, 0.5 * kv, 0.0).astype(BF16)
        lhs_ref[tile, pl.ds(TILE + at, BLOCK)] = jnp.where(low, 0.0, kv).astype(BF16)
        kt_ref[tile, :, pl.ds(at, BLOCK)] = jnp.transpose(kv)[:HEAD].astype(BF16)
        top, bottom = swapped(got_ref[i, BLOCK:].astype(F32), datt_ref[i].astype(F32))
        qa_ref[rows] = jnp.concatenate([top, bottom], axis=0).astype(BF16)

    dq_ref[...] = jnp.zeros_like(dq_ref)
    inv_len = 1.0 / jnp.full((1, 2 * HEAD), length, jnp.int32).astype(F32)
    low_row = low_lanes((1, 2 * HEAD))
    kv_scale = jnp.where(low_row, 0.5 * inv_len, inv_len)
    low = low_lanes((TILE, 2 * HEAD))

    def tile_grads(c, other, masked):
        qa = qa_ref[pl.ds(pl.multiple_of(other * TILE, TILE), TILE)]
        both = dot_nt(lhs_ref[c], qa)
        half, d_probs = both[:TILE], both[TILE:]
        if masked:
            seen = lax.broadcasted_iota(jnp.int32, (TILE, TILE), 0) <= lax.broadcasted_iota(
                jnp.int32, (TILE, TILE), 1
            )
            half = jnp.where(seen, half, 0.0)
            d_probs = jnp.where(seen, d_probs, 0.0)
        up = 1.0 + jnp.tanh(half)
        probs = half * up
        d_scores = (d_probs * up * (1.0 + (half + half) - probs)).astype(BF16)
        dq_ref[other] += dot_nn(kt_ref[c], d_scores)
        return jnp.where(low, dot_nn(d_scores, qa), dot_nn(probs.astype(BF16), qa))

    @pl.loop(0, n_tiles)
    def _(step):
        c = lax.rem(me // per_tile + step, n_tiles)
        dkv_ref[...] = tile_grads(c, c, True)

        @pl.loop(c + 1, n_tiles)
        def _(other):
            dkv_ref[...] += tile_grads(c, other, False)

        for u in range(per_tile):
            send_ref[c * per_tile + u, :BLOCK] = (
                dkv_ref[u * BLOCK:(u + 1) * BLOCK] * kv_scale
            ).astype(BF16)

        @pl.loop(0, per_tile)
        def _(turn):
            i = c * per_tile + lax.rem(me + turn, per_tile)

            @pl.when(i != me)
            def _():
                push(
                    send_ref.at[i, pl.ds(0, BLOCK)], back_ref.at[me, pl.ds(0, BLOCK)],
                    kv_send_sem, kv_recv_sem, {"seq": i},
                )

    @pl.loop(0, n_tiles)
    def _(step):
        c = lax.rem(me // per_tile + step, n_tiles)
        for u in range(per_tile):
            d_q = dq_ref[c, :, u * BLOCK:(u + 1) * BLOCK] * (0.5 * inv_len)
            send_ref[c * per_tile + u, BLOCK:] = d_q.astype(BF16)

        @pl.loop(0, per_tile)
        def _(turn):
            i = c * per_tile + lax.rem(me + turn, per_tile)

            @pl.when(i != me)
            def _():
                push(
                    send_ref.at[i, pl.ds(BLOCK, HEAD)], back_ref.at[me, pl.ds(BLOCK, HEAD)],
                    q_send_sem, q_recv_sem, {"seq": i},
                )

            @pl.when(i == me)
            def _():
                back_ref[me] = send_ref[me]

    others = pl.ds(0, n_seq - 1)
    await_bytes(send_ref.at[others, pl.ds(0, BLOCK)], kv_send_sem)
    await_bytes(send_ref.at[others, pl.ds(BLOCK, HEAD)], q_send_sem)
    await_bytes(back_ref.at[others, pl.ds(0, BLOCK)], kv_recv_sem)
    await_bytes(back_ref.at[others, pl.ds(BLOCK, HEAD)], q_recv_sem)


def gradient_kernel(
    n_seq, back_ref, xn_ref, slope_ref, d_pre_u_ref, grad_out_ref, joined_ref, out_ref,
    d_pre_ref, part_ref, core_ref, sum_ref, got_ref, red_ref, full_ref, send_sem, recv_sem,
):
    me = lax.axis_index("seq")
    grp = lax.axis_index("grp")
    core, z_hi = lax.rem(grp, 2), grp // 2
    n_here = xn_ref.shape[0]
    rows = n_here * BLOCK
    group = part_ref.shape[-1]
    per = BLOCK // HEAD * 8
    mate = {"grp": grp + 1 - 2 * core}

    barrier = pltpu.get_barrier_semaphore()
    pl.semaphore_signal(barrier, inc=1, device_id=mate, device_id_type=MESH)

    @pl.loop(1, 2 * n_seq)
    def _(step):
        slot = lax.rem(z_hi * n_seq + me + step, 2 * n_seq)
        pl.semaphore_signal(
            barrier, inc=1, device_id_type=MESH,
            device_id={"grp": slot // n_seq * 2 + core, "seq": lax.rem(slot, n_seq)},
        )

    for b in range(n_here):
        at = slice(b * BLOCK, (b + 1) * BLOCK)
        d_pre_ref[at, :WIDTH] = d_pre_u_ref[b]
        for pair in range(PAIRS):
            j = b * HEADS + 2 * pair
            d_k, d_v = swapped(back_ref[j, :BLOCK].astype(F32), back_ref[j + 1, :BLOCK].astype(F32))
            d_q = jnp.transpose(
                jnp.concatenate(
                    [back_ref[j, BLOCK:].astype(F32), back_ref[j + 1, BLOCK:].astype(F32)], axis=0
                )
            )
            for part, grad in ((1, d_v), (2, d_q), (3, d_k)):
                low = part * WIDTH + pair * 2 * HEAD
                slope = slope_ref[b, :, low:low + 2 * HEAD].astype(F32)
                d_pre_ref[at, low:low + 2 * HEAD] = (grad * slope).astype(BF16)

    xn = jnp.concatenate([xn_ref[b] for b in range(n_here)], axis=0)
    total_cols = 4 * WIDTH
    for g in range(4):
        low, high = g * group, (g + 1) * group
        if high <= total_cols:
            part = dot_tn(xn, d_pre_ref[:, low:high])
            part_ref[g % 2, g // 2] = part.astype(BF16)
        else:
            split = total_cols - low
            part_ref[g % 2, g // 2, :, :split] = dot_tn(xn, d_pre_ref[:, low:total_cols]).astype(BF16)
            part_ref[g % 2, g // 2, :, split:] = grad_out_ref[...].astype(BF16)

    pl.semaphore_wait(barrier, 2 * n_seq)
    push(part_ref.at[1 - core], core_ref, send_sem.at[0], recv_sem.at[0], mate)
    await_bytes(part_ref.at[0], send_sem.at[0])
    await_bytes(core_ref, recv_sem.at[0])

    @pl.loop(0, n_seq)
    def _(i):
        at = pl.ds(pl.multiple_of(i * per, per), per)
        for z in range(2):
            sum_ref[z * n_seq + i] = (
                part_ref[core, z, at].astype(F32) + core_ref[z, at].astype(F32)
            ).astype(BF16)

    mine = z_hi * n_seq + me

    @pl.loop(1, 2 * n_seq)
    def _(step):
        slot = lax.rem(mine + step, 2 * n_seq)
        push(
            sum_ref.at[slot], got_ref.at[mine], send_sem.at[1], recv_sem.at[1],
            {"grp": slot // n_seq * 2 + core, "seq": lax.rem(slot, n_seq)},
        )

    got_ref[mine] = sum_ref[mine]
    others = pl.ds(0, 2 * n_seq - 1)
    await_bytes(sum_ref.at[others], send_sem.at[1])
    await_bytes(got_ref.at[others], recv_sem.at[1])

    red_ref[...] = lax.fori_loop(
        0, 2 * n_seq, lambda at, total: total + got_ref[at].astype(F32),
        jnp.zeros(red_ref.shape, F32),
    ).astype(BF16)

    @pl.loop(1, 2 * n_seq)
    def _(step):
        slot = lax.rem(mine + step, 2 * n_seq)
        push(
            red_ref, full_ref.at[core, mine], send_sem.at[2], recv_sem.at[2],
            {"grp": slot // n_seq * 2 + core, "seq": lax.rem(slot, n_seq)},
        )

    full_ref[core, mine] = red_ref[...]
    await_bytes(full_ref.at[0, others], send_sem.at[2])
    await_bytes(full_ref.at[0, others], recv_sem.at[2])
    push(full_ref.at[core], full_ref.at[core], send_sem.at[3], recv_sem.at[3], mate)
    await_bytes(full_ref.at[0], send_sem.at[3])
    await_bytes(full_ref.at[0], recv_sem.at[3])

    @pl.loop(0, n_seq)
    def _(i):
        at = pl.ds(pl.multiple_of(i * per, per), per)
        for g in range(4):
            block = full_ref[g % 2, g // 2 * n_seq + i].astype(F32)
            low, high = g * group, (g + 1) * group
            if high <= total_cols:
                joined_ref[at, low:high] = block
            else:
                split = total_cols - low
                joined_ref[at, low:total_cols] = block[:, :split]
                out_ref[at] = block[:, split:]


def call(body, out_shape, in_specs, scratch, collective, cost=None):
    return pl.pallas_call(
        body,
        out_shape=out_shape,
        in_specs=in_specs,
        out_specs=jax.tree.map(lambda _: VMEM, out_shape),
        scratch_shapes=scratch,
        cost_estimate=cost,
        compiler_params=pltpu.CompilerParams(
            collective_id=collective, has_side_effects=True, vmem_limit_bytes=56 * 1024 * 1024
        ),
    )


def shaped(shape, dtype):
    return jax.ShapeDtypeStruct(shape, dtype)


def unit_rows(values):
    return values * lax.rsqrt(jnp.sum(values * values, axis=-1, keepdims=True) + eps_norm)


def local(inputs, history, lengths, w_joined, w_out, neg_emb, neg_ids):
    n_here, block, width = inputs.shape
    n_seq = lax.axis_size("seq")
    length = n_seq * block
    n_tiles = length // TILE
    lanes = 2 * HEAD
    dma = pltpu.SemaphoreType.DMA

    neg_unit = unit_rows(neg_emb.astype(F32)).astype(BF16)
    all_neg = lax.all_gather(neg_unit, "grp", axis=0, tiled=True)
    all_ids = lax.all_gather(neg_ids, "grp", axis=0, tiled=True).reshape(-1, BLOCK)
    passes = [(source, source - 1) for source in range(1, n_seq)]
    next_first = lax.ppermute(inputs[:, :1, :], "seq", passes)
    next_first_id = lax.ppermute(history[:, :1], "seq", passes)
    id_next = jnp.concatenate([history[:, 1:], next_first_id], axis=1)

    rows3 = (n_here, block, width)
    pack3 = (n_seq, BLOCK + HEAD, lanes)
    pack1 = (n_seq, HEAD, lanes)
    xn, u, slope, got = call(
        functools.partial(project_kernel, n_seq),
        [shaped(rows3, BF16), shaped(rows3, BF16), shaped((n_here, block, 4 * width), BF16), shaped(pack3, BF16)],
        [VMEM, VMEM],
        [pltpu.VMEM(pack3, BF16), dma, dma],
        0,
    )(inputs, w_joined)

    back = call(
        functools.partial(forward_kernel, n_seq, n_here),
        [shaped(pack1, BF16)],
        [SMEM, VMEM],
        [
            pltpu.VMEM((length, lanes), BF16), pltpu.VMEM((length, lanes), BF16),
            pltpu.VMEM((TILE, lanes), F32), pltpu.VMEM(pack1, BF16), dma, dma,
        ],
        1,
    )(lengths, got)[0]

    n_neg = all_neg.shape[0]
    d_att, d_pre_u, grad_out, loss = call(
        functools.partial(middle_kernel, n_seq),
        [shaped(pack1, BF16), shaped(rows3, BF16), shaped((width, width), F32), shaped((8, BLOCK), F32)],
        [SMEM] + [VMEM] * 9,
        [
            pltpu.VMEM((2 * BLOCK, width), F32), pltpu.VMEM((2 * BLOCK, n_neg), F32),
            pltpu.VMEM(pack1, BF16), dma, dma,
        ],
        2,
    )(lengths, back, inputs, next_first, id_next[:, None, :], all_neg, all_ids, w_out, u, slope)

    grads = call(
        functools.partial(backward_kernel, n_seq, n_here),
        [shaped(pack3, BF16)],
        [SMEM, VMEM, VMEM],
        [
            pltpu.VMEM((length, lanes), BF16), pltpu.VMEM((n_tiles, 2 * TILE, lanes), BF16),
            pltpu.VMEM((n_tiles, HEAD, TILE), BF16), pltpu.VMEM((n_tiles, HEAD, TILE), F32),
            pltpu.VMEM((TILE, lanes), F32), pltpu.VMEM(pack3, BF16), dma, dma, dma, dma,
        ],
        3,
    )(lengths, got, d_att)[0]

    group = 5 * width // 4
    strip = (2 * n_seq, width // n_seq, group)
    grad_joined, grad_total = call(
        functools.partial(gradient_kernel, n_seq),
        [shaped((width, 4 * width), F32), shaped((width, width), F32)],
        [VMEM] * 5,
        [
            pltpu.VMEM((n_here * block, 4 * width), BF16), pltpu.VMEM((2, 2, width, group), BF16),
            pltpu.VMEM((2, width, group), BF16), pltpu.VMEM(strip, BF16), pltpu.VMEM(strip, BF16),
            pltpu.VMEM(strip[1:], BF16), pltpu.VMEM((2,) + strip, BF16), dma((4,)), dma((4,)),
        ],
        4,
    )(grads, xn, slope, d_pre_u, grad_out)

    target_count = jnp.sum(lengths - 1).astype(F32)
    loss_total = lax.psum(loss[0, 0], ("grp", "seq"))
    return (grad_joined, grad_total, loss_total / target_count)


def solution(mesh):
    placed = (
        P("grp", "seq", None),
        P("grp", "seq"),
        P(),
        P(),
        P(),
        P(("grp", "seq"), None),
        P(("grp", "seq")),
    )
    return jax.shard_map(
        local, mesh=mesh, in_specs=placed, out_specs=(P(), P(), P()), check_vma=False
    )
```

time: 744 us -> 319 us (0.43)
  matrix products: 236 us -> 0 us
  Pallas kernels: 0 us -> 209 us
  local copies, waits for them, and re-layouts: 149 us -> 8.41 us
  waiting for transfers between devices: 127 us -> 0.02 us
  other arithmetic: 87.6 us -> 4.47 us
  starting transfers between devices: 34.7 us -> 2.61 us
  loops' own time: 11.5 us -> 0 us
    dot_general x63 -> x0, matrix products: 236 us -> none  [the longest x16 90.5 us: block_scores(): scores = jnp.dot(q_rows, k_head.T, preferred_element_type=jnp.float32)]
    pallas_call x0 -> x5, Pallas kernels: none -> 209 us  [the longest x1 62.7 us: local(): call(functools.partial(gradient_kernel, n_seq), [shaped((width, 4 * width...]
    psum x1 -> x0, waiting for transfers between devices: 90.4 us -> none  [local(): lax.psum((grad_joined_part, grad_out_part, loss_sum), ('grp', 'seq'))]
    all_to_all x6 -> x0, other arithmetic: 48.6 us -> none  [the longest x2 23 us: local(): lax.all_to_all(packed, 'seq', split_axis=0, concat_axis=0, tiled=True)]
    all_to_all x4 -> x0, waiting for transfers between devices: 36.5 us -> none  [the longest x1 18.1 us: local(): lax.all_to_all(stacked.reshape(n_seq, block * 3 * head_dim), 'seq', split...]
    convert_element_type x9 -> x0, local copies, waits for them, and re-layouts: 34.9 us -> none  [the longest x3 24.1 us: local(): d_act = jnp.concatenate([d_u, d_vqk.astype(jnp.float32)], axis=-1)]
    all_to_all x4 -> x0, starting transfers between devices: 31.4 us -> none  [the longest x1 13.3 us: local(): lax.all_to_all(attended.reshape(n_seq, block * head_dim), 'seq', split_ax...]
    all_to_all x5 -> x0, local copies, waits for them, and re-layouts: 28.1 us -> none  [the longest x2 11.6 us: local(): lax.all_to_all(packed, 'seq', split_axis=0, concat_axis=0, tiled=True)]
  transfers between devices with their start and end apart: 8 -> 3, of which waited for: 4 -> 0; matrix products, arithmetic and copies ran while one was open for 17% -> 1% of each run, Pallas kernels for 0% -> 22%
where the time goes in v1:
time: 319 us
  Pallas kernels  209 us (66%)
  blocking collectives  77.9 us (24%)
  between operations  16.6 us (5%)
  local copies, waits for them, and re-layouts  8.41 us (3%)
  other arithmetic  4.47 us (1%)
    psum x1, blocking collectives, local(): loss_total = lax.psum(loss[0, 0], ('grp', 'seq'))  68.2 us
    pallas_call x1, Pallas kernels, local(): call(functools.partial(gradient_kernel, n_seq), [shaped((width, 4 * width...  62.7 us
    pallas_call x1, Pallas kernels, local(): call(functools.partial(backward_kernel, n_seq, n_here), [shaped(pack3, BF...  55.1 us
    pallas_call x1, Pallas kernels, local(): call(functools.partial(project_kernel, n_seq), [shaped(rows3, BF16), shap...  35.6 us
    pallas_call x1, Pallas kernels, local(): call(functools.partial(forward_kernel, n_seq, n_here), [shaped(pack1, BF1...  34.1 us
    pallas_call x1, Pallas kernels, local(): call(functools.partial(middle_kernel, n_seq), [shaped(pack1, BF16), shape...  21.4 us
    all_gather x1, blocking collectives, local(): lax.all_gather(neg_ids, 'grp', axis=0, tiled=True).reshape(-1, BLOCK)  9.71 us
  transfers between devices with their start and end apart: 3, of which 0 were waited for; matrix products, arithmetic and copies ran while one was open for 1% of the time, Pallas kernels for 22%

profile of v1, /device:TPU:1, one launch (start us, length us, event | category | flops | bytes accessed | tf_op | source)
XLA Modules:
  0.0 318.8 jit_solution(17863713046164827091)
XLA Ops:
  7.2 0.0 copy-start.2
  7.2 0.0 all-gather.3.cloned.1.call-start
  7.2 1.2 fusion
  8.5 2.0 fusion.1
  10.5 0.0 all-gather.3.cloned.1.call-update
  10.5 1.3 collective-permute-start.1
  11.8 0.8 slice.12
  12.6 1.3 collective-permute-start
  13.9 0.1 slice.13
  13.9 0.6 add_reduce_fusion
  15.2 0.0 copy-start.3
  15.2 35.6 %shard_map.94 = (bf16[4,128,512]{2,1,0:T(8,128)(2,1)}, bf16[4,128,512]{2,1,0:T(8,128)(2,1)}, bf16[4,128,2048]{2,1,0:T(8,128)(2,1)}, bf16[32,192,128]{2,1,0:T(8,128)(2,1)}) custom-call(bf16[4,128,512]{2,1,0:T(8,128)(2,1)} %x_ref.3, bf16[512,2048]{1,0:T(8,128)(2,1)} %w_ref.1), custom_call_target="tpu_custom_call" | custom-call | tf_op jit(solution)/shard_map/pallas_call | solution.py:584
  50.8 34.1 %shard_map.95.back_ref = bf16[32,64,128]{2,1,0:T(8,128)(2,1)} custom-call(s32[16]{0:T(128)} %lens_ref.5, bf16[32,192,128]{2,1,0:T(8,128)(2,1)} %get-tuple-element.13.got_ref), custom_call_target="tpu_custom_call" | custom-call | tf_op jit(solution)/shard_map/pallas_call | solution.py:592
  84.9 9.7 %all-gather = s32[4,1,512]{2,1,0:T(1,128)} all-gather(s32[1,1,512]{2,1,0:T(1,128)S(1)} %bitcast.7), channel_id=1, replica_groups=mesh['grp'=4,'seq'=32] {'grp'}, dimensions={0}, use_global_device_ids=true | all-gather | bytes 10240 | tf_op jit(solution)/shard_map/all_gather | solution.py:575
  94.6 0.0 collective-permute-done.1
  94.6 0.6 pad_add_fusion
  95.2 0.6 copy-done.1
  95.8 21.4 %shard_map.96 = (bf16[32,64,128]{2,1,0:T(8,128)(2,1)}, bf16[4,128,512]{2,1,0:T(8,128)(2,1)}, f32[512,512]{1,0:T(8,128)}, f32[8,128]{1,0:T(8,128)}) custom-call(s32[16]{0:T(128)} %lens_ref.5, bf16[32,64,128]{2,1,0:T(8,128)(2,1)} %shard_map.95.back_ref, bf16[4,128,512]{2,1,0:T(8,128)(2,1)} %x_ref.3, bf16[4,1,512]{2,1,0:T(2,128)(2,1)} %copy-done.1, ...), custom_call_target="tpu_custom_call" | custom-call | tf_op jit(solution)/shard_map/pallas_call | solution.py:604
  117.2 1.2 slice.15
  118.4 68.2 %psum.7 = f32[]{:T(128)} all-reduce(f32[]{:T(128)} %bitcast.3), channel_id=1, replica_groups=mesh['grp'=4,'seq'=32] {'grp','seq'}, use_global_device_ids=true, to_apply=%region_1.0 | all-reduce | flops 1 | bytes 8 | tf_op jit(solution)/shard_map/psum | solution.py:642
  186.6 55.1 %shard_map.97.back_ref = bf16[32,192,128]{2,1,0:T(8,128)(2,1)} custom-call(s32[16]{0:T(128)} %lens_ref.5, bf16[32,192,128]{2,1,0:T(8,128)(2,1)} %get-tuple-element.13.got_ref, bf16[32,64,128]{2,1,0:T(8,128)(2,1)} %get-tuple-element.16.datt_ref), custom_call_target="tpu_custom_call" | custom-call | tf_op jit(solution)/shard_map/pallas_call | solution.py:615
  241.7 62.7 %shard_map.98 = (f32[512,2048]{1,0:T(8,128)}, f32[512,512]{1,0:T(8,128)}) custom-call(bf16[32,192,128]{2,1,0:T(8,128)(2,1)} %shard_map.97.back_ref, bf16[4,128,512]{2,1,0:T(8,128)(2,1)} %get-tuple-element.17.xn_ref, bf16[4,128,2048]{2,1,0:T(8,128)(2,1)} %get-tuple-element.15.slope_ref, bf16[4,128,512]{2,1,0:T(8,128)(2,1)} %get-tuple-element.18.d_pre_u_ref, ...), custom_call_target="tpu_custom_call" | custom-call | tf_op jit(solution)/shard_map/pallas_call | solution.py:629
  305.0 4.8 %copy.12 = f32[512,2048]{1,0:T(8,128)} copy(f32[512,2048]{1,0:T(8,128)} %get-tuple-element.26) | data formatting | bytes 8388608
  309.8 1.0 copy.13
  (10 shorter events, 0.0 us)
Async XLA Ops:
  7.2 3.3 %copy-start.4 = (s32[4,128]{1,0:T(4,128)S(1)}, s32[4,128]{1,0:T(4,128)}, u32[]{:S(2)}) copy-start(s32[4,128]{1,0:T(4,128)} %param.8) | copy-start | bytes 6148
  7.2 6.8 %copy-start.2 = (s32[16]{0:T(128)S(1)}, s32[16]{0:T(128)}, u32[]{:S(2)}) copy-start(s32[16]{0:T(128)} %lens_ref.5) | copy-start | bytes 196
  7.2 88.0 %all-gather.3.cloned.1.call-start = ((), (), s32[]{:S(2)}) async-start(), calls=%async_computation | async-start | bytes 2621440 | tf_op jit(solution)/shard_map/all_gather | solution.py:574
  10.5 84.1 %collective-permute-start.1 = (s32[4,1]{1,0:T(4,128)S(1)}, s32[4,1]{1,0:T(4,128)S(1)}, u32[]{:S(2)}, u32[]{:S(2)}) collective-permute-start(s32[4,1]{1,0:T(4,128)S(1)} %bitcast.8), channel_id=1, source_target_pairs={{1,0},{2,1},{3,2},{4,3},{5,4},{6,5},{7,6},{8,7},{9,8},{10,9},{11,1... | collective-permute-start | bytes 56 | tf_op jit(solution)/shard_map/ppermute | solution.py:578
  12.6 82.6 %collective-permute-start = (bf16[4,1,512]{2,1,0:T(2,128)(2,1)S(1)}, bf16[4,1,512]{2,1,0:T(2,128)(2,1)S(1)}, u32[]{:S(2)}, u32[]{:S(2)}) collective-permute-start(bf16[4,1,512]{2,1,0:T(2,128)(2,1)S(1)} %slice.12), channel_id=1, source_target_pairs={{1,0},{2,1},{3,2},{4,3},{5,4},{6,5},{7,6},{8,7},{9,8},{10,9},{11,1... | collective-permute-start | bytes 12296 | tf_op jit(solution)/shard_map/ppermute | solution.py:577
  15.2 69.7 %copy-start.3 = (s32[512]{0:T(512)S(1)}, s32[512]{0:T(512)}, u32[]{:S(2)}) copy-start(s32[512]{0:T(512)} %param.13) | copy-start | bytes 6148
  95.2 0.6 copy-start.1
  305.0 4.8 %copy-start = (f32[512,512]{1,0:T(8,128)S(1)}, f32[512,512]{1,0:T(8,128)}, u32[]{:S(2)}) copy-start(f32[512,512]{1,0:T(8,128)} %get-tuple-element.27) | copy-start | bytes 3145732
Sparse Core Ops, SparseCore 0:
  10.6 47.2 all-gather.2

commit v2 on v0

v2 whole, which is shorter than its diff:
```python
import functools
import types

import jax
import jax.numpy as jnp
from jax import lax
from jax.experimental import pallas as pl
from jax.experimental.pallas import tpu as pltpu
from jax.sharding import PartitionSpec as P

HEADS = 8
HEAD = 64
WIDTH = 512
PAIRS = 4
BLOCK = 128
FQ = 512
FK = 2048
BM = 512
BT = 1024
eps_norm = 1e-06
logit_scale = 64.0

MESH = pl.DeviceIdType.MESH
F32 = jnp.float32
BF16 = jnp.bfloat16
VMEM = pl.BlockSpec(memory_space=pltpu.VMEM)
SMEM = pl.BlockSpec(memory_space=pltpu.SMEM)


def dot_nn(a, b):
    return lax.dot_general(a, b, (((1,), (0,)), ((), ())), preferred_element_type=F32)


def dot_nt(a, b):
    return lax.dot_general(a, b, (((1,), (1,)), ((), ())), preferred_element_type=F32)


def dot_tn(a, b):
    return lax.dot_general(a, b, (((0,), (0,)), ((), ())), preferred_element_type=F32)


def low_lanes(shape):
    return lax.broadcasted_iota(jnp.int32, shape, 1) < HEAD


def turned(a):
    return pltpu.roll(a, HEAD, axis=1)


def swapped(a, b):
    low = low_lanes(a.shape)
    return jnp.where(low, a, turned(b)), jnp.where(low, turned(a), b)


def copy_to(src, dst, send_sem, recv_sem, where):
    pltpu.make_async_remote_copy(
        src_ref=src, dst_ref=dst, send_sem=send_sem, recv_sem=recv_sem,
        device_id=where, device_id_type=MESH,
    ).start()


def await_bytes(ref, sem):
    pltpu.make_async_copy(ref, ref, sem).wait()


def aligned(at, size):
    return pl.ds(pl.multiple_of(at, size), size)


def pair_cols(pair):
    return slice(pair * 2 * HEAD, (pair + 1) * 2 * HEAD)


def kernel(n_seq, names, *refs):
    r = types.SimpleNamespace(**dict(zip(names, refs, strict=True)))
    me = lax.axis_index("seq")
    grp = lax.axis_index("grp")
    core, z_hi = lax.rem(grp, 2), grp // 2
    n_here = r.x.shape[0]
    planes = n_seq // HEADS
    length = n_seq * BLOCK
    n_chips = 2 * n_seq
    mine = z_hi * n_seq + me
    mate = {"grp": grp + 1 - 2 * core}
    other_z = {"grp": (1 - z_hi) * 2 + core}
    others = pl.ds(0, n_seq - 1)

    def chip(slot):
        return {"grp": slot // n_seq * 2 + core, "seq": lax.rem(slot, n_seq)}

    barrier = pltpu.get_barrier_semaphore()
    pl.semaphore_signal(barrier, inc=1, device_id=mate, device_id_type=MESH)

    @pl.loop(1, n_chips)
    def _(step):
        pl.semaphore_signal(
            barrier, inc=1, device_id=chip(lax.rem(mine + step, n_chips)), device_id_type=MESH
        )

    @pl.loop(0, n_here)
    def _(step):
        b = lax.rem(me // HEADS + step, n_here)
        x = r.x[b].astype(F32)
        centered = x - jnp.mean(x, axis=-1, keepdims=True)
        var = jnp.mean(centered * centered, axis=-1, keepdims=True)
        xn = (centered * lax.rsqrt(var + eps_norm)).astype(BF16)
        r.xn[b] = xn
        v, q, k = (activated(r, b, xn, part) for part in (1, 2, 3))
        for pair in range(PAIRS):
            cols = pair_cols(pair)
            kv = swapped(k[:, cols], v[:, cols])
            qs = swapped(q[:HEAD, cols], q[HEAD:, cols])
            for odd in range(2):
                j = b * HEADS + 2 * pair + odd
                r.send[j, :BLOCK] = kv[odd].astype(BF16)
                r.send[j, BLOCK:] = qs[odd].astype(BF16)

        @pl.when(step == 0)
        def _():
            pl.semaphore_wait(barrier, n_chips)

        @pl.loop(0, HEADS)
        def _(turn):
            j = b * HEADS + lax.rem(me + turn, HEADS)

            @pl.when(j != me)
            def _():
                copy_to(r.send.at[j], r.got.at[me], r.send_sem.at[0], r.got_sem.at[me], {"seq": j})

            @pl.when(j == me)
            def _():
                r.got[me] = r.send[me]

    before = {"seq": lax.rem(me + n_seq - 1, n_seq)}
    r.ids[:n_here] = r.history[...]
    r.ids[n_here:] = r.neg_ids[...]
    copy_to(r.x.at[:, pl.ds(0, 16)], r.first, r.send_sem.at[1], r.one_sem.at[0], before)
    copy_to(r.ids, r.next_ids, r.send_sem.at[2], r.one_sem.at[1], before)

    @pl.loop(0, n_here)
    def _(b):
        xn = r.xn[b]
        r.u[b] = activated(r, b, xn, 0).astype(BF16)
        r.xnt[:, aligned(b * BLOCK, BLOCK)] = jnp.transpose(xn.astype(F32)).astype(BF16)
        rows = aligned(b * BLOCK, BLOCK)
        emb = r.neg_emb[rows].astype(F32)
        r.negs[grp, rows] = (
            emb * lax.rsqrt(jnp.sum(emb * emb, axis=-1, keepdims=True) + eps_norm)
        ).astype(BF16)

    r.all_ids[grp] = r.ids[...]
    copy_to(r.negs.at[grp], r.negs.at[grp], r.send_sem.at[3], r.one_sem.at[2], mate)
    copy_to(r.all_ids.at[grp], r.all_ids.at[grp], r.send_sem.at[4], r.one_sem.at[3], mate)
    copy_to(r.negs.at[grp], r.negs.at[grp], r.send_sem.at[5], r.one_sem.at[4], other_z)
    copy_to(r.all_ids.at[grp], r.all_ids.at[grp], r.send_sem.at[6], r.one_sem.at[5], other_z)

    seq_len = r.lens[grp * n_here + me // HEADS]
    low = low_lanes((HEAD, 2 * HEAD))
    low_block = low_lanes((BLOCK, 2 * HEAD))

    @pl.loop(0, planes)
    def _(step):
        first = lax.rem(me // HEADS + planes - step, planes) * HEADS

        @pl.loop(0, HEADS)
        def _(turn):
            i = first + turn

            @pl.when(i != me)
            def _():
                await_bytes(r.got.at[0], r.got_sem.at[i])

        @pl.loop(0, HEADS, unroll=4)
        def _(turn):
            i = first + turn
            rows = aligned(i * BLOCK, BLOCK)
            pos = i * BLOCK + lax.broadcasted_iota(jnp.int32, (BLOCK, 2 * HEAD), 0)
            kv = jnp.where(pos < seq_len, r.got[i, :BLOCK].astype(F32), 0.0)
            r.k0[rows] = jnp.where(low_block, 0.5 * kv, 0.0).astype(BF16)
            r.v0[rows] = jnp.where(low_block, 0.0, kv).astype(BF16)
            r.kt[:, rows] = jnp.transpose(kv)[:HEAD].astype(BF16)
            q = r.got[i, BLOCK:].astype(F32)
            r.qa[rows] = jnp.concatenate(
                [jnp.where(low, q, 0.0), jnp.where(low, turned(q), 0.0)], axis=0
            ).astype(BF16)

    await_bytes(r.send.at[others], r.send_sem.at[0])
    inv_len = 1.0 / jnp.full((1, 2 * HEAD), seq_len, jnp.int32).astype(F32)

    f_tiles = length // FQ
    f_per = FQ // BLOCK

    @pl.loop(0, f_tiles)
    def _(step):
        c = lax.rem(me // f_per + step, f_tiles)
        q = r.qa[aligned(c * FQ, FQ)]
        r.acc[...] = jnp.zeros_like(r.acc)
        n_full = c * FQ // FK

        def piece(at, masked):
            rows = aligned(at * FK, FK)
            half = dot_nt(q, r.k0[rows])
            if masked:
                ahead = at * FK - c * FQ + lax.broadcasted_iota(
                    jnp.int32, (FQ, FK), 1
                ) - lax.broadcasted_iota(jnp.int32, (FQ, FK), 0)
                half = jnp.where(ahead <= 0, half, 0.0)
            probs = (half + half * jnp.tanh(half)).astype(BF16)
            r.acc[...] += dot_nn(probs, r.v0[rows])

        @pl.loop(0, n_full)
        def _(at):
            piece(at, False)

        piece(n_full, True)
        for u in range(f_per):
            out = r.acc[u * BLOCK:(u + 1) * BLOCK] * inv_len
            top, bottom = out[:HEAD], out[HEAD:]
            r.att_send[c * f_per + u] = jnp.where(low, turned(top), bottom).astype(BF16)

        @pl.loop(0, f_per)
        def _(turn):
            i = c * f_per + lax.rem(me + turn, f_per)

            @pl.when(i != me)
            def _():
                copy_to(
                    r.att_send.at[i], r.att_got.at[me], r.send_sem.at[7], r.att_sem.at[me], {"seq": i}
                )

            @pl.when(i == me)
            def _():
                r.att_got[me] = r.att_send[me]

    far = (1 - z_hi) * 2 + core
    await_bytes(r.negs.at[0], r.one_sem.at[4])
    await_bytes(r.all_ids.at[0], r.one_sem.at[5])
    copy_to(r.negs.at[far], r.negs.at[far], r.send_sem.at[8], r.one_sem.at[6], mate)
    copy_to(r.all_ids.at[far], r.all_ids.at[far], r.send_sem.at[9], r.one_sem.at[7], mate)

    total = r.lens[0] - 1
    for at in range(1, r.lens.shape[0]):
        total = total + (r.lens[at] - 1)
    both = 2
    half_rows = both * BLOCK
    weight = 1.0 / jnp.full((half_rows, 1), total, jnp.int32).astype(F32)
    r.grad_out[...] = jnp.zeros_like(r.grad_out)
    r.loss[...] = jnp.zeros_like(r.loss)
    await_bytes(r.first, r.one_sem.at[0])
    await_bytes(r.ids, r.one_sem.at[1])
    await_bytes(r.negs.at[0], r.one_sem.at[2])
    await_bytes(r.all_ids.at[0], r.one_sem.at[3])
    await_bytes(r.negs.at[0], r.one_sem.at[6])
    await_bytes(r.all_ids.at[0], r.one_sem.at[7])
    n_halves = n_here // both

    @pl.loop(0, n_halves)
    def _(step):
        middle(r, n_seq, me, grp, both * lax.rem(me // (both * HEADS) + step, n_halves), weight)

    r.e_part[0, 0] = dot_nn(r.xnt[...], r.d_pre[:, :WIDTH // 2]).astype(BF16)
    r.e_part[1, 0] = dot_nn(r.xnt[...], r.d_pre[:, WIDTH // 2:WIDTH]).astype(BF16)
    r.e_part[0, 1] = r.grad_out[:, :WIDTH // 2].astype(BF16)
    r.e_part[1, 1] = r.grad_out[:, WIDTH // 2:].astype(BF16)

    def reduction(name, sem_at):
        part, got_core, sums, got, red, full = (
            getattr(r, name + tail) for tail in ("_part", "_core", "_sum", "_got", "_red", "_full")
        )
        send = [r.red_send.at[sem_at + k] for k in range(4)]
        recv = [r.red_recv.at[sem_at + k] for k in range(4)]
        rest = pl.ds(0, n_chips - 1)
        height = sums.shape[1]

        def to_core():
            copy_to(part.at[1 - core], got_core, send[0], recv[0], mate)

        def spread():
            await_bytes(got_core, recv[0])

            @pl.loop(0, n_seq, unroll=4)
            def _(i):
                at = aligned(i * height, height)
                for z in range(2):
                    sums[z * n_seq + i] = (
                        part[core, z, at].astype(F32) + got_core[z, at].astype(F32)
                    ).astype(BF16)

            @pl.loop(1, n_chips)
            def _(step):
                slot = lax.rem(mine + step, n_chips)
                copy_to(sums.at[slot], got.at[mine], send[1], recv[1], chip(slot))

            got[mine] = sums[mine]

        def collect():
            await_bytes(got.at[rest], recv[1])
            red[...] = jnp.sum(got[...].astype(F32), axis=0).astype(BF16)

            @pl.loop(1, n_chips)
            def _(step):
                slot = lax.rem(mine + step, n_chips)
                copy_to(red, full.at[core, mine], send[2], recv[2], chip(slot))

            full[core, mine] = red[...]

        def share():
            await_bytes(full.at[0, rest], recv[2])
            copy_to(full.at[core], full.at[core], send[3], recv[3], mate)

        def finish():
            await_bytes(full.at[0], recv[3])
            await_bytes(part.at[0], send[0])
            await_bytes(sums.at[rest], send[1])
            await_bytes(full.at[0, rest], send[2])
            await_bytes(full.at[0], send[3])

        def written(at, ref, col):
            width = full.shape[-1]
            ref[:, col:col + width] = full[
                at % 2, at // 2 * n_seq:(at // 2 + 1) * n_seq
            ].reshape(n_seq * height, width)

        return types.SimpleNamespace(
            to_core=to_core, spread=spread, collect=collect, share=share, finish=finish, written=written
        )

    early = reduction("e", 0)
    early.to_core()
    copy_to(r.loss, r.loss_core, r.loss_sem.at[0], r.loss_sem.at[1], mate)

    @pl.loop(0, n_seq)
    def _(step):
        i = lax.rem(me + step, n_seq)

        @pl.when(i != me)
        def _():
            await_bytes(r.datt_got.at[0], r.datt_sem.at[i])

    @pl.loop(0, n_seq, unroll=4)
    def _(i):
        d_att = r.datt_got[i].astype(F32)
        rows = aligned(i * BLOCK, BLOCK)
        qa = r.qa[rows].astype(F32)
        r.qa[rows] = jnp.where(
            low_block, qa, jnp.concatenate([turned(d_att), d_att], axis=0)
        ).astype(BF16)

    r.dq[...] = jnp.zeros_like(r.dq)
    b_tiles = length // BM
    b_per = BM // BLOCK
    t_tiles = length // BT
    kv_scale = jnp.where(low_lanes((1, 2 * HEAD)), 0.5 * inv_len, inv_len)

    @pl.loop(0, b_tiles)
    def _(step):
        c = lax.rem(me // b_per + step, b_tiles)
        m_rows = aligned(c * BM, BM)
        low_tile = low_lanes((BM, 2 * HEAD))

        def piece(at, masked):
            t_rows = aligned(at * BT, BT)
            qa = r.qa[t_rows]
            half = dot_nt(r.k0[m_rows], qa)
            d_probs = dot_nt(r.v0[m_rows], qa)
            if masked:
                ahead = c * BM - at * BT + lax.broadcasted_iota(
                    jnp.int32, (BM, BT), 0
                ) - lax.broadcasted_iota(jnp.int32, (BM, BT), 1)
                half = jnp.where(ahead <= 0, half, 0.0)
                d_probs = jnp.where(ahead <= 0, d_probs, 0.0)
            up = 1.0 + jnp.tanh(half)
            probs = half * up
            d_scores = (d_probs * up * (1.0 + (half + half) - probs)).astype(BF16)
            r.dq[:, t_rows] += dot_nn(r.kt[:, m_rows], d_scores)
            return jnp.where(low_tile, dot_nn(d_scores, qa), dot_nn(probs.astype(BF16), qa))

        first = c * BM // BT
        r.dkv[...] = piece(first, True)

        @pl.loop(first + 1, t_tiles)
        def _(at):
            r.dkv[...] += piece(at, False)

        for u in range(b_per):
            r.grad_send[c * b_per + u, :BLOCK] = (
                r.dkv[u * BLOCK:(u + 1) * BLOCK] * kv_scale
            ).astype(BF16)

        @pl.loop(0, b_per)
        def _(turn):
            i = c * b_per + lax.rem(me + turn, b_per)

            @pl.when(i != me)
            def _():
                copy_to(
                    r.grad_send.at[i, pl.ds(0, BLOCK)], r.grad_got.at[me, pl.ds(0, BLOCK)],
                    r.send_sem.at[10], r.grad_sem.at[0], {"seq": i},
                )

            @pl.when(i == me)
            def _():
                r.grad_got[me, :BLOCK] = r.grad_send[me, :BLOCK]

        @pl.when(step == 0)
        def _():
            early.spread()
            await_bytes(r.loss_core, r.loss_sem.at[1])
            r.loss_sum[...] = r.loss[...] + r.loss_core[...]
            r.loss_all[mine] = r.loss_sum[...]

            @pl.loop(1, n_chips)
            def _(turn):
                slot = lax.rem(mine + turn, n_chips)
                copy_to(
                    r.loss_sum, r.loss_all.at[mine], r.loss_sem.at[2], r.loss_sem.at[3], chip(slot)
                )

        @pl.when(step == b_tiles // 2)
        def _():
            early.collect()

    @pl.loop(0, b_tiles)
    def _(step):
        c = lax.rem(me // b_per + step, b_tiles)
        for u in range(b_per):
            d_q = r.dq[:, aligned((c * b_per + u) * BLOCK, BLOCK)] * (0.5 * inv_len)
            r.grad_send[c * b_per + u, BLOCK:] = d_q.astype(BF16)

        @pl.loop(0, b_per)
        def _(turn):
            i = c * b_per + lax.rem(me + turn, b_per)

            @pl.when(i != me)
            def _():
                copy_to(
                    r.grad_send.at[i, pl.ds(BLOCK, HEAD)], r.grad_got.at[me, pl.ds(BLOCK, HEAD)],
                    r.send_sem.at[11], r.grad_sem.at[1], {"seq": i},
                )

            @pl.when(i == me)
            def _():
                r.grad_got[me, BLOCK:] = r.grad_send[me, BLOCK:]

    later = reduction("l", 4)
    last = reduction("q", 8)
    await_bytes(r.grad_got.at[others, pl.ds(0, BLOCK)], r.grad_sem.at[0])

    @pl.loop(0, n_here)
    def _(b):
        rows = aligned(b * BLOCK, BLOCK)
        for pair in range(PAIRS):
            j = b * HEADS + 2 * pair
            d_k, d_v = swapped(r.grad_got[j, :BLOCK].astype(F32), r.grad_got[j + 1, :BLOCK].astype(F32))
            for part, grad in ((1, d_v), (3, d_k)):
                at = part * WIDTH + pair * 2 * HEAD
                slope = r.slope[b, :, at:at + 2 * HEAD].astype(F32)
                r.d_pre[rows, at:at + 2 * HEAD] = (grad * slope).astype(BF16)

    for at, low_col in enumerate((1, 1.5, 3, 3.5)):
        col = int(low_col * WIDTH)
        r.l_part[at % 2, at // 2] = dot_nn(r.xnt[...], r.d_pre[:, col:col + WIDTH // 2]).astype(BF16)
    later.to_core()
    await_bytes(r.grad_got.at[others, pl.ds(BLOCK, HEAD)], r.grad_sem.at[1])

    @pl.loop(0, n_here)
    def _(b):
        rows = aligned(b * BLOCK, BLOCK)
        for pair in range(PAIRS):
            j = b * HEADS + 2 * pair
            at = 2 * WIDTH + pair * 2 * HEAD
            grad = jnp.transpose(
                jnp.concatenate([r.grad_got[j + e, BLOCK:].astype(F32) for e in range(2)], axis=0)
            )
            slope = r.slope[b, :, at:at + 2 * HEAD].astype(F32)
            r.d_pre[rows, at:at + 2 * HEAD] = (grad * slope).astype(BF16)

    later.spread()
    q_grad = dot_nn(r.xnt[...], r.d_pre[:, 2 * WIDTH:3 * WIDTH]).astype(BF16)
    for at in range(4):
        r.q_part[at % 2, at // 2] = q_grad[:, at * BLOCK:(at + 1) * BLOCK]
    last.to_core()
    early.share()
    last.spread()
    later.collect()
    last.collect()

    await_bytes(r.loss_all.at[pl.ds(0, n_chips - 1)], r.loss_sem.at[3])
    r.loss_out[...] = jnp.sum(r.loss_all[...], axis=0)
    early.finish()
    for at in range(2):
        early.written(at, r.joined, at * WIDTH // 2)
        early.written(2 + at, r.out, at * WIDTH // 2)
    later.share()
    last.share()
    later.finish()
    for at, low_col in enumerate((1, 1.5, 3, 3.5)):
        later.written(at, r.joined, int(low_col * WIDTH))
    last.finish()
    for at in range(4):
        last.written(at, r.joined, 2 * WIDTH + at * BLOCK)

    await_bytes(r.first, r.send_sem.at[1])
    await_bytes(r.ids, r.send_sem.at[2])
    for at in (3, 5, 8):
        await_bytes(r.negs.at[0], r.send_sem.at[at])
        await_bytes(r.all_ids.at[0], r.send_sem.at[at + 1])
    await_bytes(r.att_send.at[others], r.send_sem.at[7])
    await_bytes(r.datt_send.at[others], r.send_sem.at[12])
    await_bytes(r.grad_send.at[others, pl.ds(0, BLOCK)], r.send_sem.at[10])
    await_bytes(r.grad_send.at[others, pl.ds(BLOCK, HEAD)], r.send_sem.at[11])
    await_bytes(r.loss, r.loss_sem.at[0])
    await_bytes(r.loss_all.at[pl.ds(0, n_chips - 1)], r.loss_sem.at[2])


def activated(r, b, xn, part):
    half = 0.5 * dot_nn(xn, r.w_joined[:, part * WIDTH:(part + 1) * WIDTH])
    th = jnp.tanh(half)
    slope = (0.5 + 0.5 * th) * (1.0 + half * (1.0 - th))
    r.slope[b, :, part * WIDTH:(part + 1) * WIDTH] = slope.astype(BF16)
    return half + half * th


def middle(r, n_seq, me, grp, first_b, weight):
    both = 2
    rows = both * BLOCK
    n_here = r.x.shape[0]
    n_grp, n_neg = r.negs.shape[:2]

    def joined(make):
        return jnp.concatenate([make(e) for e in range(both)], axis=0)

    @pl.loop(0, both * HEADS)
    def _(turn):
        j = first_b * HEADS + turn

        @pl.when(j != me)
        def _():
            await_bytes(r.att_got.at[0], r.att_sem.at[j])

    for e in range(both):
        for pair in range(PAIRS):
            j = (first_b + e) * HEADS + 2 * pair
            top, bottom = swapped(r.att_got[j].astype(F32), r.att_got[j + 1].astype(F32))
            r.att[e * BLOCK:e * BLOCK + HEAD, pair_cols(pair)] = top
            r.att[e * BLOCK + HEAD:(e + 1) * BLOCK, pair_cols(pair)] = bottom

    att = r.att[...]
    centered = att - jnp.mean(att, axis=-1, keepdims=True)
    inv_att = lax.rsqrt(jnp.mean(centered * centered, axis=-1, keepdims=True) + eps_norm)
    normed = centered * inv_att
    u = joined(lambda e: r.u[first_b + e]).astype(F32)
    gated = (normed * u).astype(BF16)
    x = joined(lambda e: r.x[first_b + e]).astype(F32)
    out_rows = x + dot_nn(gated, r.w_out[...])
    inv_y = lax.rsqrt(jnp.sum(out_rows * out_rows, axis=-1, keepdims=True) + eps_norm)
    unit_y = out_rows * inv_y
    unit_b = unit_y.astype(BF16)
    more = jnp.where(me == n_seq - 1, 0, 1)
    last_row = lax.broadcasted_iota(jnp.int32, (BLOCK, WIDTH), 0) == BLOCK - 1
    last_lane = lax.broadcasted_iota(jnp.int32, (1, BLOCK), 1) == BLOCK - 1

    def next_rows(e):
        shifted = pltpu.roll(r.x[first_b + e].astype(F32), BLOCK - 1, axis=0)
        return jnp.where(last_row, r.first[first_b + e].astype(F32)[:1] * more.astype(F32), shifted)

    x_next = joined(next_rows)
    pos_unit = (
        x_next * lax.rsqrt(jnp.sum(x_next * x_next, axis=-1, keepdims=True) + eps_norm)
    ).astype(BF16).astype(F32)
    pos_logit = logit_scale * jnp.sum(unit_b.astype(F32) * pos_unit, axis=-1, keepdims=True)

    def row_ids(e):
        shifted = pltpu.roll(r.ids[pl.ds(first_b + e, 1)], BLOCK - 1, axis=1)
        coming = pltpu.roll(r.next_ids[pl.ds(first_b + e, 1)], BLOCK - 1, axis=1) * more
        return jnp.transpose(jnp.broadcast_to(jnp.where(last_lane, coming, shifted), (BLOCK, BLOCK)))

    ids = joined(row_ids)
    lane_sum = jnp.zeros((rows, BLOCK), F32)
    for g in range(n_grp):
        neg_logit = logit_scale * dot_nt(unit_b, r.negs[g])
        for sub in range(n_neg // BLOCK):
            at = (g * n_neg) + sub * BLOCK
            hit = r.all_ids[g, n_here + sub:n_here + sub + 1] == ids
            exps = jnp.where(hit, 0.0, jnp.exp(neg_logit[:, sub * BLOCK:(sub + 1) * BLOCK]))
            r.exps[:, at:at + BLOCK] = exps
            lane_sum = lane_sum + exps
    pos_exp = jnp.exp(pos_logit)
    denom = pos_exp + jnp.sum(lane_sum, axis=-1, keepdims=True)

    def row_valid(e):
        pos = me * BLOCK + lax.broadcasted_iota(jnp.int32, (BLOCK, 1), 0)
        return jnp.where(pos + 1 < r.lens[grp * n_here + first_b + e], 1.0, 0.0)

    valid = joined(row_valid)
    row_loss = jnp.where(valid > 0.0, jnp.log(denom) - pos_logit, 0.0)
    r.loss[...] += jnp.broadcast_to(jnp.sum(row_loss, axis=0, keepdims=True), r.loss.shape)
    row_weight = valid * weight
    d_pos = row_weight * (pos_exp / denom - 1.0)
    scale = row_weight / denom
    neg_back = jnp.zeros((rows, WIDTH), F32)
    for g in range(n_grp):
        d_neg = (scale * r.exps[:, g * n_neg:(g + 1) * n_neg]).astype(BF16)
        neg_back = neg_back + dot_nn(d_neg, r.negs[g])
    d_unit = logit_scale * (d_pos * pos_unit + neg_back)
    d_out = (
        (d_unit - unit_y * jnp.sum(unit_y * d_unit, axis=-1, keepdims=True)) * inv_y
    ).astype(BF16)
    d_gate = dot_nt(d_out, r.w_out[...])
    d_norm = d_gate * u
    d_att = inv_att * (
        d_norm
        - jnp.mean(d_norm, axis=-1, keepdims=True)
        - normed * jnp.mean(d_norm * normed, axis=-1, keepdims=True)
    )
    for e in range(both):
        rows_e = d_att[e * BLOCK:(e + 1) * BLOCK]
        for pair in range(PAIRS):
            cols = pair_cols(pair)
            packed = swapped(rows_e[:HEAD, cols], rows_e[HEAD:, cols])
            for odd in range(2):
                r.datt_send[(first_b + e) * HEADS + 2 * pair + odd] = packed[odd].astype(BF16)

    @pl.loop(0, both * HEADS)
    def _(turn):
        j = first_b * HEADS + lax.rem(me + turn, both * HEADS)

        @pl.when(j != me)
        def _():
            copy_to(
                r.datt_send.at[j], r.datt_got.at[me], r.send_sem.at[12], r.datt_sem.at[me], {"seq": j}
            )

        @pl.when(j == me)
        def _():
            r.datt_got[me] = r.datt_send[me]

    r.grad_out[...] += dot_tn(gated, d_out)
    d_u = d_gate * normed
    for e in range(both):
        slope = r.slope[first_b + e, :, :WIDTH].astype(F32)
        r.d_pre[aligned((first_b + e) * BLOCK, BLOCK), :WIDTH] = (
            d_u[e * BLOCK:(e + 1) * BLOCK] * slope
        ).astype(BF16)


def local(inputs, history, lengths, w_joined, w_out, neg_emb, neg_ids):
    n_here, block, width = inputs.shape
    n_seq = lax.axis_size("seq")
    length = n_seq * block
    lanes = 2 * HEAD
    rows = n_here * block
    n_neg = neg_emb.shape[0]
    chips = 2 * n_seq
    strip = width // n_seq
    dma = pltpu.SemaphoreType.DMA
    buffers = dict(
        xn=((n_here, block, width), BF16), xnt=((width, rows), BF16), u=((n_here, block, width), BF16),
        slope=((n_here, block, 4 * width), BF16), d_pre=((rows, 4 * width), BF16),
        send=((n_seq, BLOCK + HEAD, lanes), BF16), got=((n_seq, BLOCK + HEAD, lanes), BF16),
        att_send=((n_seq, HEAD, lanes), BF16), att_got=((n_seq, HEAD, lanes), BF16),
        datt_send=((n_seq, HEAD, lanes), BF16), datt_got=((n_seq, HEAD, lanes), BF16),
        grad_send=((n_seq, BLOCK + HEAD, lanes), BF16), grad_got=((n_seq, BLOCK + HEAD, lanes), BF16),
        first=((n_here, 16, width), BF16), ids=((2 * n_here, block), jnp.int32),
        next_ids=((2 * n_here, block), jnp.int32), negs=((4, n_neg, width), BF16),
        all_ids=((4, 2 * n_here, block), jnp.int32),
        k0=((length, lanes), BF16), v0=((length, lanes), BF16), qa=((length, lanes), BF16),
        kt=((HEAD, length), BF16), acc=((FQ, lanes), F32), dq=((HEAD, length), F32), dkv=((BM, lanes), F32),
        att=((2 * block, width), F32), exps=((2 * block, 4 * n_neg), F32), grad_out=((width, width), F32),
        loss=((8, block), F32), loss_core=((8, block), F32), loss_sum=((8, block), F32),
        loss_all=((chips, 8, block), F32),
    )
    for name, cols in (("e", 2 * width // 4), ("l", 2 * width // 4), ("q", width // 4)):
        buffers[name + "_part"] = ((2, 2, width, cols), BF16)
        buffers[name + "_core"] = ((2, width, cols), BF16)
        buffers[name + "_sum"] = ((chips, strip, cols), BF16)
        buffers[name + "_got"] = ((chips, strip, cols), BF16)
        buffers[name + "_red"] = ((strip, cols), BF16)
        buffers[name + "_full"] = ((2, chips, strip, cols), BF16)
    sems = dict(
        send_sem=13, one_sem=8, got_sem=n_seq, att_sem=n_seq, datt_sem=n_seq, grad_sem=2, loss_sem=4,
        red_send=12, red_recv=12,
    )
    takes = ("lens", "x", "history", "neg_ids", "w_joined", "w_out", "neg_emb")
    gives = dict(
        joined=((width, 4 * width), BF16), out=((width, width), BF16), loss_out=((8, block), F32)
    )
    names = takes + tuple(gives) + tuple(buffers) + tuple(sems)
    joined, out, loss = pl.pallas_call(
        functools.partial(kernel, n_seq, names),
        out_shape=[jax.ShapeDtypeStruct(*kind) for kind in gives.values()],
        in_specs=[SMEM] + [VMEM] * (len(takes) - 1),
        out_specs=[VMEM] * len(gives),
        scratch_shapes=[pltpu.VMEM(*kind) for kind in buffers.values()]
        + [dma((count,)) for count in sems.values()],
        compiler_params=pltpu.CompilerParams(
            collective_id=0, has_side_effects=True, vmem_limit_bytes=60 * 1024 * 1024
        ),
    )(lengths, inputs, history, neg_ids.reshape(-1, block), w_joined, w_out, neg_emb)
    target_count = jnp.sum(lengths - 1).astype(F32)
    return (joined.astype(F32), out.astype(F32), loss[0, 0] / target_count)


def solution(mesh):
    placed = (
        P("grp", "seq", None),
        P("grp", "seq"),
        P(),
        P(),
        P(),
        P(("grp", "seq"), None),
        P(("grp", "seq")),
    )
    return jax.shard_map(
        local, mesh=mesh, in_specs=placed, out_specs=(P(), P(), P()), check_vma=False
    )
```

time: 744 us -> 171 us (0.23)
  matrix products: 236 us -> 0 us
  Pallas kernels: 0 us -> 160 us
  local copies, waits for them, and re-layouts: 149 us -> 1.2 us
  waiting for transfers between devices: 127 us -> 0 us
  other arithmetic: 87.6 us -> 5.91 us
  blocking collectives: 73.9 us -> 0 us
  starting transfers between devices: 34.7 us -> 0 us
  between operations: 18.1 us -> 3 us
  loops' own time: 11.5 us -> 0 us
    dot_general x63 -> x0, matrix products: 236 us -> none  [the longest x16 90.5 us: block_scores(): scores = jnp.dot(q_rows, k_head.T, preferred_element_type=jnp.float32)]
    pallas_call x0 -> x1, Pallas kernels: none -> 160 us  [local(): pl.pallas_call(functools.partial(kernel, n_seq, names), out_shape=[jax.Sh...]
    psum x1 -> x0, waiting for transfers between devices: 90.4 us -> none  [local(): lax.psum((grad_joined_part, grad_out_part, loss_sum), ('grp', 'seq'))]
    psum x1 -> x0, blocking collectives: 66 us -> none  [local(): lax.psum((grad_joined_part, grad_out_part, loss_sum), ('grp', 'seq'))]
    all_to_all x6 -> x0, other arithmetic: 48.6 us -> none  [the longest x2 23 us: local(): lax.all_to_all(packed, 'seq', split_axis=0, concat_axis=0, tiled=True)]
    all_to_all x4 -> x0, waiting for transfers between devices: 36.5 us -> none  [the longest x1 18.1 us: local(): lax.all_to_all(stacked.reshape(n_seq, block * 3 * head_dim), 'seq', split...]
    convert_element_type x9 -> x0, local copies, waits for them, and re-layouts: 34.9 us -> none  [the longest x3 24.1 us: local(): d_act = jnp.concatenate([d_u, d_vqk.astype(jnp.float32)], axis=-1)]
    all_to_all x4 -> x0, starting transfers between devices: 31.4 us -> none  [the longest x1 13.3 us: local(): lax.all_to_all(attended.reshape(n_seq, block * head_dim), 'seq', split_ax...]
  transfers between devices with their start and end apart: 8 -> 0, of which waited for: 4 -> 0; matrix products, arithmetic and copies ran while one was open for 17% -> 0% of each run, Pallas kernels for 0% -> 0%
where the time goes in v2:
time: 171 us
  Pallas kernels  160 us (94%)
  other arithmetic  5.91 us (3%)
  between operations  3 us (2%)
    pallas_call x1, Pallas kernels, local(): pl.pallas_call(functools.partial(kernel, n_seq, names), out_shape=[jax.Sh...  160 us
    convert_element_type x2, other arithmetic, local(): return (joined.astype(F32), out.astype(F32), loss[0, 0] / target_count)  5.29 us

profile of v2, /device:TPU:1, one launch (start us, length us, event | category | flops | bytes accessed | tf_op | source)
XLA Modules:
  0.0 170.6 jit_solution(10575894815501703381)
XLA Ops:
  0.6 160.5 %shard_map.94 = (bf16[512,2048]{1,0:T(8,128)(2,1)}, bf16[512,512]{1,0:T(8,128)(2,1)}, f32[8,128]{1,0:T(8,128)}) custom-call(s32[16]{0:T(128)} %refs_0_.1, bf16[4,128,512]{2,1,0:T(8,128)(2,1)} %refs_1_.1, s32[4,128]{1,0:T(4,128)} %refs_2_.1, s32[4,128]{1,0:T(4,128)} %bitcast.2, bf16[512,2048]{1,0:T(8,128)(2,1)} %refs_4_.1, bf16[512,512]{1,0:T(8,128)(2,1)} %refs_5_.1, ...), custom_call_target="tpu_custom_call" | custom-call | tf_op jit(solution)/shard_map/pallas_call | solution.py:689
  161.1 0.0 copy-start
  161.1 0.0 copy-start.1
  161.2 4.2 %convert_element_type.9 = f32[512,2048]{1,0:T(8,128)} convert(bf16[512,2048]{1,0:T(8,128)(2,1)} %get-tuple-element.6) | non-fusion elementwise | flops 1048576 | bytes 6291456 | tf_op jit(solution)/shard_map/convert_element_type | solution.py:701
  165.3 0.0 copy-done
  165.3 1.1 convert_element_type.10
  166.4 1.2 slice.3
  167.6 0.0 copy-done.1
  167.6 0.6 add_reduce_fusion
Async XLA Ops:
  161.1 4.2 %copy-start = (bf16[512,512]{1,0:T(8,128)(2,1)S(1)}, bf16[512,512]{1,0:T(8,128)(2,1)}, u32[]{:S(2)}) copy-start(bf16[512,512]{1,0:T(8,128)(2,1)} %get-tuple-element.7) | copy-start | bytes 1572868
  161.1 6.5 %copy-start.1 = (s32[16]{0:T(128)S(1)}, s32[16]{0:T(128)}, u32[]{:S(2)}) copy-start(s32[16]{0:T(128)} %refs_0_.1) | copy-start | bytes 196

commit v3 on v2

--- a/solution.py
+++ b/solution.py
@@ -13,10 +13,9 @@
 WIDTH = 512
 PAIRS = 4
 BLOCK = 128
-FQ = 512
-FK = 2048
-BM = 512
-BT = 1024
+TILE = 512
+FQ = TILE
+BM = TILE
 eps_norm = 1e-06
 logit_scale = 64.0
 
@@ -69,6 +68,29 @@
 
 def pair_cols(pair):
     return slice(pair * 2 * HEAD, (pair + 1) * 2 * HEAD)
+
+
+def shifts(n_seq):
+    side = int((n_seq // 2) ** 0.5)
+    steps = [(x, y, z) for x in range(side) for y in range(side) for z in range(2)]
+    return sorted(steps[1:], key=lambda at: -(min(at[0], side - at[0]) + min(at[1], side - at[1]) + at[2]))
+
+
+def peer(me, shift):
+    x, y, z = me // HEADS, lax.rem(me // 2, 4), lax.rem(me, 2)
+    return (lax.rem(x + shift[0], 4) * 4 + lax.rem(y + shift[1], 4)) * 2 + lax.rem(z + shift[2], 2)
+
+
+def cover(first, count, body):
+    done = 0
+    for tiles in (4, 2, 1):
+        n = count // tiles if tiles == 4 else lax.rem(count // tiles, 2)
+
+        @pl.loop(0, n)
+        def _(at, done=done, tiles=tiles):
+            body((first + done + at * tiles) * TILE, tiles * TILE)
+
+        done = done + n * tiles
 
 
 def kernel(n_seq, names, *refs):
@@ -98,8 +120,7 @@
         )
 
     @pl.loop(0, n_here)
-    def _(step):
-        b = lax.rem(me // HEADS + step, n_here)
+    def _(b):
         x = r.x[b].astype(F32)
         centered = x - jnp.mean(x, axis=-1, keepdims=True)
         var = jnp.mean(centered * centered, axis=-1, keepdims=True)
@@ -115,21 +136,11 @@
                 r.send[j, :BLOCK] = kv[odd].astype(BF16)
                 r.send[j, BLOCK:] = qs[odd].astype(BF16)
 
-        @pl.when(step == 0)
-        def _():
-            pl.semaphore_wait(barrier, n_chips)
-
-        @pl.loop(0, HEADS)
-        def _(turn):
-            j = b * HEADS + lax.rem(me + turn, HEADS)
-
-            @pl.when(j != me)
-            def _():
-                copy_to(r.send.at[j], r.got.at[me], r.send_sem.at[0], r.got_sem.at[me], {"seq": j})
-
-            @pl.when(j == me)
-            def _():
-                r.got[me] = r.send[me]
+    pl.semaphore_wait(barrier, n_chips)
+    for shift in shifts(n_seq):
+        j = peer(me, shift)
+        copy_to(r.send.at[j], r.got.at[me], r.send_sem.at[0], r.got_sem.at[me], {"seq": j})
+    r.got[me] = r.send[me]
 
     before = {"seq": lax.rem(me + n_seq - 1, n_seq)}
     r.ids[:n_here] = r.history[...]
@@ -149,10 +160,6 @@
         ).astype(BF16)
 
     r.all_ids[grp] = r.ids[...]
-    copy_to(r.negs.at[grp], r.negs.at[grp], r.send_sem.at[3], r.one_sem.at[2], mate)
-    copy_to(r.all_ids.at[grp], r.all_ids.at[grp], r.send_sem.at[4], r.one_sem.at[3], mate)
-    copy_to(r.negs.at[grp], r.negs.at[grp], r.send_sem.at[5], r.one_sem.at[4], other_z)
-    copy_to(r.all_ids.at[grp], r.all_ids.at[grp], r.send_sem.at[6], r.one_sem.at[5], other_z)
 
     seq_len = r.lens[grp * n_here + me // HEADS]
     low = low_lanes((HEAD, 2 * HEAD))
@@ -160,7 +167,7 @@
 
     @pl.loop(0, planes)
     def _(step):
-        first = lax.rem(me // HEADS + planes - step, planes) * HEADS
+        first = lax.rem(me // HEADS + planes // 2 + step, planes) * HEADS
 
         @pl.loop(0, HEADS)
         def _(turn):
@@ -184,6 +191,10 @@
                 [jnp.where(low, q, 0.0), jnp.where(low, turned(q), 0.0)], axis=0
             ).astype(BF16)
 
+    copy_to(r.negs.at[grp], r.negs.at[grp], r.send_sem.at[3], r.one_sem.at[2], mate)
+    copy_to(r.all_ids.at[grp], r.all_ids.at[grp], r.send_sem.at[4], r.one_sem.at[3], mate)
+    copy_to(r.negs.at[grp], r.negs.at[grp], r.send_sem.at[5], r.one_sem.at[4], other_z)
+    copy_to(r.all_ids.at[grp], r.all_ids.at[grp], r.send_sem.at[6], r.one_sem.at[5], other_z)
     await_bytes(r.send.at[others], r.send_sem.at[0])
     inv_len = 1.0 / jnp.full((1, 2 * HEAD), seq_len, jnp.int32).astype(F32)
 
@@ -194,25 +205,24 @@
     def _(step):
         c = lax.rem(me // f_per + step, f_tiles)
         q = r.qa[aligned(c * FQ, FQ)]
-        r.acc[...] = jnp.zeros_like(r.acc)
-        n_full = c * FQ // FK
-
-        def piece(at, masked):
-            rows = aligned(at * FK, FK)
+
+        def piece(start, size, masked):
+            rows = pl.ds(pl.multiple_of(start, TILE), size)
             half = dot_nt(q, r.k0[rows])
             if masked:
-                ahead = at * FK - c * FQ + lax.broadcasted_iota(
-                    jnp.int32, (FQ, FK), 1
-                ) - lax.broadcasted_iota(jnp.int32, (FQ, FK), 0)
+                ahead = lax.broadcasted_iota(jnp.int32, (FQ, size), 1) - lax.broadcasted_iota(
+                    jnp.int32, (FQ, size), 0
+                )
                 half = jnp.where(ahead <= 0, half, 0.0)
             probs = (half + half * jnp.tanh(half)).astype(BF16)
-            r.acc[...] += dot_nn(probs, r.v0[rows])
-
-        @pl.loop(0, n_full)
-        def _(at):
-            piece(at, False)
-
-        piece(n_full, True)
+            return dot_nn(probs, r.v0[rows])
+
+        r.acc[...] = piece(c * FQ, FQ, True)
+
+        def more(start, size):
+            r.acc[...] += piece(start, size, False)
+
+        cover(0, c, more)
         for u in range(f_per):
             out = r.acc[u * BLOCK:(u + 1) * BLOCK] * inv_len
             top, bottom = out[:HEAD], out[HEAD:]
@@ -349,7 +359,6 @@
     r.dq[...] = jnp.zeros_like(r.dq)
     b_tiles = length // BM
     b_per = BM // BLOCK
-    t_tiles = length // BT
     kv_scale = jnp.where(low_lanes((1, 2 * HEAD)), 0.5 * inv_len, inv_len)
 
     @pl.loop(0, b_tiles)
@@ -358,15 +367,15 @@
         m_rows = aligned(c * BM, BM)
         low_tile = low_lanes((BM, 2 * HEAD))
 
-        def piece(at, masked):
-            t_rows = aligned(at * BT, BT)
+        def piece(start, size, masked):
+            t_rows = pl.ds(pl.multiple_of(start, TILE), size)
             qa = r.qa[t_rows]
             half = dot_nt(r.k0[m_rows], qa)
             d_probs = dot_nt(r.v0[m_rows], qa)
             if masked:
-                ahead = c * BM - at * BT + lax.broadcasted_iota(
-                    jnp.int32, (BM, BT), 0
-                ) - lax.broadcasted_iota(jnp.int32, (BM, BT), 1)
+                ahead = lax.broadcasted_iota(jnp.int32, (BM, size), 0) - lax.broadcasted_iota(
+                    jnp.int32, (BM, size), 1
+                )
                 half = jnp.where(ahead <= 0, half, 0.0)
                 d_probs = jnp.where(ahead <= 0, d_probs, 0.0)
             up = 1.0 + jnp.tanh(half)
@@ -375,13 +384,12 @@
             r.dq[:, t_rows] += dot_nn(r.kt[:, m_rows], d_scores)
             return jnp.where(low_tile, dot_nn(d_scores, qa), dot_nn(probs.astype(BF16), qa))
 
-        first = c * BM // BT
-        r.dkv[...] = piece(first, True)
-
-        @pl.loop(first + 1, t_tiles)
-        def _(at):
-            r.dkv[...] += piece(at, False)
-
+        r.dkv[...] = piece(c * BM, BM, True)
+
+        def more(start, size):
+            r.dkv[...] += piece(start, size, False)
+
+        cover(c + 1, b_tiles - 1 - c, more)
         for u in range(b_per):
             r.grad_send[c * b_per + u, :BLOCK] = (
                 r.dkv[u * BLOCK:(u + 1) * BLOCK] * kv_scale
@@ -486,7 +494,8 @@
     last.collect()
 
     await_bytes(r.loss_all.at[pl.ds(0, n_chips - 1)], r.loss_sem.at[3])
-    r.loss_out[...] = jnp.sum(r.loss_all[...], axis=0)
+    count = jnp.full((8, BLOCK), total, jnp.int32).astype(F32)
+    r.loss_out[0] = (jnp.sum(r.loss_all[...], axis=0) / count)[0, 0]
     early.finish()
     for at in range(2):
         early.written(at, r.joined, at * WIDTH // 2)
@@ -683,22 +692,21 @@
     )
     takes = ("lens", "x", "history", "neg_ids", "w_joined", "w_out", "neg_emb")
     gives = dict(
-        joined=((width, 4 * width), BF16), out=((width, width), BF16), loss_out=((8, block), F32)
+        joined=((width, 4 * width), BF16), out=((width, width), BF16), loss_out=((1,), F32)
     )
     names = takes + tuple(gives) + tuple(buffers) + tuple(sems)
     joined, out, loss = pl.pallas_call(
         functools.partial(kernel, n_seq, names),
         out_shape=[jax.ShapeDtypeStruct(*kind) for kind in gives.values()],
         in_specs=[SMEM] + [VMEM] * (len(takes) - 1),
-        out_specs=[VMEM] * len(gives),
+        out_specs=[VMEM, VMEM, SMEM],
         scratch_shapes=[pltpu.VMEM(*kind) for kind in buffers.values()]
         + [dma((count,)) for count in sems.values()],
         compiler_params=pltpu.CompilerParams(
             collective_id=0, has_side_effects=True, vmem_limit_bytes=60 * 1024 * 1024
         ),
     )(lengths, inputs, history, neg_ids.reshape(-1, block), w_joined, w_out, neg_emb)
-    target_count = jnp.sum(lengths - 1).astype(F32)
-    return (joined.astype(F32), out.astype(F32), loss[0, 0] / target_count)
+    return (joined.astype(F32), out.astype(F32), loss.reshape(()))
 
 
 def solution(mesh):

time: 171 us -> 158 us (0.924)
  Pallas kernels: 160 us -> 151 us
    pallas_call x1, Pallas kernels: 160 us -> 151 us  [local(): pl.pallas_call(functools.partial(kernel, n_seq, names), out_shape=[jax.Sh...]
where the time goes in v3:
time: 158 us
  Pallas kernels  151 us (96%)
  other arithmetic  5.29 us (3%)
  between operations  2.34 us (1%)
    pallas_call x1, Pallas kernels, local(): pl.pallas_call(functools.partial(kernel, n_seq, names), out_shape=[jax.Sh...  151 us
    convert_element_type x2, other arithmetic, local(): return (joined.astype(F32), out.astype(F32), loss.reshape(()))  5.29 us

profile of v3, /device:TPU:1, one launch (start us, length us, event | category | flops | bytes accessed | tf_op | source)
XLA Modules:
  0.0 158.2 jit_solution(10130780636423348444)
XLA Ops:
  0.6 150.5 %shard_map.94 = (bf16[512,2048]{1,0:T(8,128)(2,1)}, bf16[512,512]{1,0:T(8,128)(2,1)}, f32[1]{0:T(128)}) custom-call(s32[16]{0:T(128)} %refs_0_.1, bf16[4,128,512]{2,1,0:T(8,128)(2,1)} %refs_1_.1, s32[4,128]{1,0:T(4,128)} %refs_2_.1, s32[4,128]{1,0:T(4,128)} %bitcast.2, bf16[512,2048]{1,0:T(8,128)(2,1)} %refs_4_.1, bf16[512,512]{1,0:T(8,128)(2,1)} %refs_5_.1, ...), custom_call_target="tpu_custom_call" | custom-call | tf_op jit(solution)/shard_map/pallas_call | solution.py:698
  151.2 0.0 copy-start
  151.2 4.2 %convert_element_type.6 = f32[512,2048]{1,0:T(8,128)} convert(bf16[512,2048]{1,0:T(8,128)(2,1)} %get-tuple-element.6) | non-fusion elementwise | flops 1048576 | bytes 6291456 | tf_op jit(solution)/shard_map/convert_element_type | solution.py:709
  155.4 0.0 copy-done
  155.4 1.1 convert_element_type.7
Async XLA Ops:
  151.2 4.2 %copy-start = (bf16[512,512]{1,0:T(8,128)(2,1)S(1)}, bf16[512,512]{1,0:T(8,128)(2,1)}, u32[]{:S(2)}) copy-start(bf16[512,512]{1,0:T(8,128)(2,1)} %get-tuple-element.7) | copy-start | bytes 1572868

commit v4 on v3

--- a/solution.py
+++ b/solution.py
@@ -98,26 +98,40 @@
     me = lax.axis_index("seq")
     grp = lax.axis_index("grp")
     core, z_hi = lax.rem(grp, 2), grp // 2
+    loads = [
+        pltpu.make_async_copy(getattr(r, name + "_in"), getattr(r, name), r.load_sem.at[at])
+        for at, name in enumerate(("x", "w_joined", "history", "neg_ids", "neg_emb", "w_out"))
+    ]
+    for load in loads:
+        load.start()
     n_here = r.x.shape[0]
     planes = n_seq // HEADS
     length = n_seq * BLOCK
-    n_chips = 2 * n_seq
-    mine = z_hi * n_seq + me
     mate = {"grp": grp + 1 - 2 * core}
     other_z = {"grp": (1 - z_hi) * 2 + core}
     others = pl.ds(0, n_seq - 1)
-
-    def chip(slot):
-        return {"grp": slot // n_seq * 2 + core, "seq": lax.rem(slot, n_seq)}
+    x_at, y_at, z_at = me // HEADS, lax.rem(me // 2, 4), z_hi * 2 + lax.rem(me, 2)
 
     barrier = pltpu.get_barrier_semaphore()
-    pl.semaphore_signal(barrier, inc=1, device_id=mate, device_id_type=MESH)
-
-    @pl.loop(1, n_chips)
+
+    def greet(where):
+        pl.semaphore_signal(barrier, inc=1, device_id=where, device_id_type=MESH)
+
+    greet(mate)
+
+    @pl.loop(1, n_seq)
     def _(step):
-        pl.semaphore_signal(
-            barrier, inc=1, device_id=chip(lax.rem(mine + step, n_chips)), device_id_type=MESH
-        )
+        greet({"seq": lax.rem(me + step, n_seq)})
+
+    for step in range(4):
+        for z in range(2):
+            greet(dict(other_z, seq=(x_at * 4 + lax.rem(y_at + step, 4)) * 2 + z))
+            if step:
+                greet(dict(other_z, seq=(lax.rem(x_at + step, 4) * 4 + y_at) * 2 + z))
+    n_peers = n_seq + 14
+
+    loads[0].wait()
+    loads[1].wait()
 
     @pl.loop(0, n_here)
     def _(b):
@@ -136,17 +150,22 @@
                 r.send[j, :BLOCK] = kv[odd].astype(BF16)
                 r.send[j, BLOCK:] = qs[odd].astype(BF16)
 
-    pl.semaphore_wait(barrier, n_chips)
+    pl.semaphore_wait(barrier, n_peers)
     for shift in shifts(n_seq):
         j = peer(me, shift)
         copy_to(r.send.at[j], r.got.at[me], r.send_sem.at[0], r.got_sem.at[me], {"seq": j})
     r.got[me] = r.send[me]
 
     before = {"seq": lax.rem(me + n_seq - 1, n_seq)}
+    loads[2].wait()
+    loads[3].wait()
     r.ids[:n_here] = r.history[...]
     r.ids[n_here:] = r.neg_ids[...]
     copy_to(r.x.at[:, pl.ds(0, 16)], r.first, r.send_sem.at[1], r.one_sem.at[0], before)
     copy_to(r.ids, r.next_ids, r.send_sem.at[2], r.one_sem.at[1], before)
+
+    loads[4].wait()
+    loads[5].wait()
 
     @pl.loop(0, n_here)
     def _(b):
@@ -268,76 +287,99 @@
     def _(step):
         middle(r, n_seq, me, grp, both * lax.rem(me // (both * HEADS) + step, n_halves), weight)
 
-    r.e_part[0, 0] = dot_nn(r.xnt[...], r.d_pre[:, :WIDTH // 2]).astype(BF16)
-    r.e_part[1, 0] = dot_nn(r.xnt[...], r.d_pre[:, WIDTH // 2:WIDTH]).astype(BF16)
-    r.e_part[0, 1] = r.grad_out[:, :WIDTH // 2].astype(BF16)
-    r.e_part[1, 1] = r.grad_out[:, WIDTH // 2:].astype(BF16)
-
-    def reduction(name, sem_at):
-        part, got_core, sums, got, red, full = (
-            getattr(r, name + tail) for tail in ("_part", "_core", "_sum", "_got", "_red", "_full")
+    axes = dict(x=x_at, y=y_at, z=z_at)
+    plane_at = dict(x=y_at * 4 + z_at, y=x_at * 4 + z_at, z=x_at * 4 + y_at)
+
+    def chip(axis, along, across):
+        hi, lo = across // 4, lax.rem(across, 4)
+        x, y, z = dict(x=(along, hi, lo), y=(hi, along, lo), z=(hi, lo, along))[axis]
+        return {"grp": z // 2 * 2 + core, "seq": (x * 4 + y) * 2 + lax.rem(z, 2)}
+
+    def reduction(name, axis, at):
+        part, got_core, sums, got, sums2, got2, red, full = (
+            getattr(r, name + tail)
+            for tail in ("_part", "_core", "_sum", "_got", "_sum2", "_got2", "_red", "_full")
         )
-        send = [r.red_send.at[sem_at + k] for k in range(4)]
-        recv = [r.red_recv.at[sem_at + k] for k in range(4)]
-        rest = pl.ds(0, n_chips - 1)
-        height = sums.shape[1]
-
-        def to_core():
+        send = [r.red_send.at[at * 6 + k] for k in range(6)]
+        recv = [r.red_recv.at[at * 6 + k] for k in range(6)]
+        along, across = axes[axis], plane_at[axis]
+        rest = pl.ds(0, 15)
+
+        def to_core(grad):
+            for half in range(4):
+                block = grad[:, half * BLOCK:(half + 1) * BLOCK].astype(BF16)
+                low = half % 2 * 8
+                part[half // 2, :, low:low + 8] = block.reshape(4, 8, 16, BLOCK)
             copy_to(part.at[1 - core], got_core, send[0], recv[0], mate)
 
+        def along_axis(sources, target, sems):
+            for step in range(1, 4):
+                to = lax.rem(along + step, 4)
+                copy_to(sources(to), target, *sems, chip(axis, to, across))
+
+        def over_plane(sources, target, sems):
+            @pl.loop(1, 16)
+            def _(step):
+                to = lax.rem(across + step, 16)
+                copy_to(sources(to), target, *sems, chip(axis, along, to))
+
+        def fold():
+            await_bytes(got_core, recv[0])
+            sums[...] = (part[core].astype(F32) + got_core[...].astype(F32)).astype(BF16)
+            along_axis(lambda to: sums.at[to], got.at[along], (send[1], recv[1]))
+
+        def plane():
+            got[along] = sums[along]
+            await_bytes(got.at[pl.ds(0, 3)], recv[1])
+            sums2[...] = jnp.sum(got[...].astype(F32), axis=0).astype(BF16)
+            over_plane(lambda to: sums2.at[to], got2.at[across], (send[2], recv[2]))
+
+        def gather():
+            got2[across] = sums2[across]
+            await_bytes(got2.at[rest], recv[2])
+            red[...] = jnp.sum(got2[...].astype(F32), axis=0).astype(BF16)
+            full[core, along, across] = red[...]
+            over_plane(lambda to: red, full.at[core, along, across], (send[3], recv[3]))
+
         def spread():
-            await_bytes(got_core, recv[0])
-
-            @pl.loop(0, n_seq, unroll=4)
-            def _(i):
-                at = aligned(i * height, height)
-                for z in range(2):
-                    sums[z * n_seq + i] = (
-                        part[core, z, at].astype(F32) + got_core[z, at].astype(F32)
-                    ).astype(BF16)
-
-            @pl.loop(1, n_chips)
-            def _(step):
-                slot = lax.rem(mine + step, n_chips)
-                copy_to(sums.at[slot], got.at[mine], send[1], recv[1], chip(slot))
-
-            got[mine] = sums[mine]
-
-        def collect():
-            await_bytes(got.at[rest], recv[1])
-            red[...] = jnp.sum(got[...].astype(F32), axis=0).astype(BF16)
-
-            @pl.loop(1, n_chips)
-            def _(step):
-                slot = lax.rem(mine + step, n_chips)
-                copy_to(red, full.at[core, mine], send[2], recv[2], chip(slot))
-
-            full[core, mine] = red[...]
+            await_bytes(got2.at[rest], recv[3])
+            along_axis(lambda to: full.at[core, along], full.at[core, along], (send[4], recv[4]))
 
         def share():
-            await_bytes(full.at[0, rest], recv[2])
-            copy_to(full.at[core], full.at[core], send[3], recv[3], mate)
+            await_bytes(got.at[pl.ds(0, 3)], recv[4])
+            copy_to(full.at[core], full.at[core], send[5], recv[5], mate)
 
         def finish():
-            await_bytes(full.at[0], recv[3])
+            await_bytes(full.at[0], recv[5])
             await_bytes(part.at[0], send[0])
-            await_bytes(sums.at[rest], send[1])
-            await_bytes(full.at[0, rest], send[2])
-            await_bytes(full.at[0], send[3])
-
-        def written(at, ref, col):
-            width = full.shape[-1]
-            ref[:, col:col + width] = full[
-                at % 2, at // 2 * n_seq:(at // 2 + 1) * n_seq
-            ].reshape(n_seq * height, width)
+            await_bytes(got.at[pl.ds(0, 3)], send[1])
+            for k in (2, 3):
+                await_bytes(got2.at[rest], send[k])
+            await_bytes(got.at[pl.ds(0, 3)], send[4])
+            await_bytes(full.at[0], send[5])
 
         return types.SimpleNamespace(
-            to_core=to_core, spread=spread, collect=collect, share=share, finish=finish, written=written
+            to_core=to_core, fold=fold, plane=plane, gather=gather, spread=spread, share=share, finish=finish
         )
 
-    early = reduction("e", 0)
-    early.to_core()
+    early = [reduction("u", "x", 0), reduction("o", "y", 1)]
+    early[0].to_core(dot_nn(r.xnt[...], r.d_pre[:, :WIDTH]))
+    early[1].to_core(r.grad_out[...])
     copy_to(r.loss, r.loss_core, r.loss_sem.at[0], r.loss_sem.at[1], mate)
+
+    def loss_along(axis, value, at):
+        r.loss_all[at, axes[axis]] = value
+        r.loss_sum[at] = value
+        for step in range(1, 4):
+            copy_to(
+                r.loss_sum.at[at], r.loss_all.at[at, axes[axis]],
+                r.loss_sem.at[2 + 2 * at], r.loss_sem.at[3 + 2 * at],
+                chip(axis, lax.rem(axes[axis] + step, 4), plane_at[axis]),
+            )
+
+    def loss_over(at):
+        await_bytes(r.loss_all.at[at, pl.ds(0, 3)], r.loss_sem.at[3 + 2 * at])
+        return jnp.sum(r.loss_all[at], axis=0)
 
     @pl.loop(0, n_seq)
     def _(step):
@@ -410,23 +452,21 @@
             def _():
                 r.grad_got[me, :BLOCK] = r.grad_send[me, :BLOCK]
 
-        @pl.when(step == 0)
-        def _():
-            early.spread()
-            await_bytes(r.loss_core, r.loss_sem.at[1])
-            r.loss_sum[...] = r.loss[...] + r.loss_core[...]
-            r.loss_all[mine] = r.loss_sum[...]
-
-            @pl.loop(1, n_chips)
-            def _(turn):
-                slot = lax.rem(mine + turn, n_chips)
-                copy_to(
-                    r.loss_sum, r.loss_all.at[mine], r.loss_sem.at[2], r.loss_sem.at[3], chip(slot)
-                )
-
-        @pl.when(step == b_tiles // 2)
-        def _():
-            early.collect()
+        for at, stage in enumerate(("fold", "plane", "gather", "spread", "share")):
+            @pl.when(step == at)
+            def _(at=at, stage=stage):
+                for one in early:
+                    getattr(one, stage)()
+                if at == 0:
+                    await_bytes(r.loss_core, r.loss_sem.at[1])
+                    loss_along("x", r.loss[...] + r.loss_core[...], 0)
+                if at == 1:
+                    loss_along("y", loss_over(0), 1)
+                if at == 2:
+                    loss_along("z", loss_over(1), 2)
+                if at == 3:
+                    count = jnp.full((8, BLOCK), total, jnp.int32).astype(F32)
+                    r.loss_out[0] = (loss_over(2) / count)[0, 0]
 
     @pl.loop(0, b_tiles)
     def _(step):
@@ -450,8 +490,7 @@
             def _():
                 r.grad_got[me, BLOCK:] = r.grad_send[me, BLOCK:]
 
-    later = reduction("l", 4)
-    last = reduction("q", 8)
+    late = [reduction("v", "x", 2), reduction("k", "y", 3), reduction("q", "z", 4)]
     await_bytes(r.grad_got.at[others, pl.ds(0, BLOCK)], r.grad_sem.at[0])
 
     @pl.loop(0, n_here)
@@ -465,10 +504,10 @@
                 slope = r.slope[b, :, at:at + 2 * HEAD].astype(F32)
                 r.d_pre[rows, at:at + 2 * HEAD] = (grad * slope).astype(BF16)
 
-    for at, low_col in enumerate((1, 1.5, 3, 3.5)):
-        col = int(low_col * WIDTH)
-        r.l_part[at % 2, at // 2] = dot_nn(r.xnt[...], r.d_pre[:, col:col + WIDTH // 2]).astype(BF16)
-    later.to_core()
+    late[0].to_core(dot_nn(r.xnt[...], r.d_pre[:, WIDTH:2 * WIDTH]))
+    late[1].to_core(dot_nn(r.xnt[...], r.d_pre[:, 3 * WIDTH:]))
+    late[0].fold()
+    late[1].fold()
     await_bytes(r.grad_got.at[others, pl.ds(BLOCK, HEAD)], r.grad_sem.at[1])
 
     @pl.loop(0, n_here)
@@ -483,31 +522,23 @@
             slope = r.slope[b, :, at:at + 2 * HEAD].astype(F32)
             r.d_pre[rows, at:at + 2 * HEAD] = (grad * slope).astype(BF16)
 
-    later.spread()
-    q_grad = dot_nn(r.xnt[...], r.d_pre[:, 2 * WIDTH:3 * WIDTH]).astype(BF16)
-    for at in range(4):
-        r.q_part[at % 2, at // 2] = q_grad[:, at * BLOCK:(at + 1) * BLOCK]
-    last.to_core()
-    early.share()
-    last.spread()
-    later.collect()
-    last.collect()
-
-    await_bytes(r.loss_all.at[pl.ds(0, n_chips - 1)], r.loss_sem.at[3])
-    count = jnp.full((8, BLOCK), total, jnp.int32).astype(F32)
-    r.loss_out[0] = (jnp.sum(r.loss_all[...], axis=0) / count)[0, 0]
-    early.finish()
-    for at in range(2):
-        early.written(at, r.joined, at * WIDTH // 2)
-        early.written(2 + at, r.out, at * WIDTH // 2)
-    later.share()
-    last.share()
-    later.finish()
-    for at, low_col in enumerate((1, 1.5, 3, 3.5)):
-        later.written(at, r.joined, int(low_col * WIDTH))
-    last.finish()
-    for at in range(4):
-        last.written(at, r.joined, 2 * WIDTH + at * BLOCK)
+    late[2].to_core(dot_nn(r.xnt[...], r.d_pre[:, 2 * WIDTH:3 * WIDTH]))
+    late[0].plane()
+    late[1].plane()
+    late[2].fold()
+    late[0].gather()
+    late[1].gather()
+    late[2].plane()
+    late[0].spread()
+    late[1].spread()
+    late[2].gather()
+    late[0].share()
+    late[1].share()
+    late[2].spread()
+    late[2].share()
+
+    for one in early + late:
+        one.finish()
 
     await_bytes(r.first, r.send_sem.at[1])
     await_bytes(r.ids, r.send_sem.at[2])
@@ -519,7 +550,8 @@
     await_bytes(r.grad_send.at[others, pl.ds(0, BLOCK)], r.send_sem.at[10])
     await_bytes(r.grad_send.at[others, pl.ds(BLOCK, HEAD)], r.send_sem.at[11])
     await_bytes(r.loss, r.loss_sem.at[0])
-    await_bytes(r.loss_all.at[pl.ds(0, n_chips - 1)], r.loss_sem.at[2])
+    for at in range(3):
+        await_bytes(r.loss_all.at[at, pl.ds(0, 3)], r.loss_sem.at[2 + 2 * at])
 
 
 def activated(r, b, xn, part):
@@ -653,6 +685,18 @@
         ).astype(BF16)
 
 
+def widen(*refs):
+    *blocks, joined, out = refs
+    for at, block in enumerate(blocks):
+        for half in range(4):
+            low = half % 2 * 8
+            values = block[half // 2, 0, low:low + 8].reshape(BLOCK, BLOCK).astype(F32)
+            if at < 4:
+                joined[:, at * WIDTH + half * BLOCK:at * WIDTH + (half + 1) * BLOCK] = values
+            else:
+                out[:, half * BLOCK:(half + 1) * BLOCK] = values
+
+
 def local(inputs, history, lengths, w_joined, w_out, neg_emb, neg_ids):
     n_here, block, width = inputs.shape
     n_seq = lax.axis_size("seq")
@@ -660,8 +704,6 @@
     lanes = 2 * HEAD
     rows = n_here * block
     n_neg = neg_emb.shape[0]
-    chips = 2 * n_seq
-    strip = width // n_seq
     dma = pltpu.SemaphoreType.DMA
     buffers = dict(
         xn=((n_here, block, width), BF16), xnt=((width, rows), BF16), u=((n_here, block, width), BF16),
@@ -676,37 +718,53 @@
         k0=((length, lanes), BF16), v0=((length, lanes), BF16), qa=((length, lanes), BF16),
         kt=((HEAD, length), BF16), acc=((FQ, lanes), F32), dq=((HEAD, length), F32), dkv=((BM, lanes), F32),
         att=((2 * block, width), F32), exps=((2 * block, 4 * n_neg), F32), grad_out=((width, width), F32),
-        loss=((8, block), F32), loss_core=((8, block), F32), loss_sum=((8, block), F32),
-        loss_all=((chips, 8, block), F32),
+        loss=((8, block), F32), loss_core=((8, block), F32), loss_sum=((3, 8, block), F32),
+        loss_all=((3, 4, 8, block), F32), x=((n_here, block, width), BF16),
+        w_joined=((width, 4 * width), BF16), w_out=((width, width), BF16), neg_emb=((n_neg, width), BF16),
+        history=((n_here, block), jnp.int32), neg_ids=((n_here, block), jnp.int32),
     )
-    for name, cols in (("e", 2 * width // 4), ("l", 2 * width // 4), ("q", width // 4)):
-        buffers[name + "_part"] = ((2, 2, width, cols), BF16)
-        buffers[name + "_core"] = ((2, width, cols), BF16)
-        buffers[name + "_sum"] = ((chips, strip, cols), BF16)
-        buffers[name + "_got"] = ((chips, strip, cols), BF16)
-        buffers[name + "_red"] = ((strip, cols), BF16)
-        buffers[name + "_full"] = ((2, chips, strip, cols), BF16)
+    wide = (4, 16, 16, block)
+    for name in "uovkq":
+        buffers[name + "_part"] = ((2,) + wide, BF16)
+        for tail in ("_core", "_sum", "_got"):
+            buffers[name + tail] = (wide, BF16)
+        for tail in ("_sum2", "_got2"):
+            buffers[name + tail] = (wide[1:], BF16)
+        buffers[name + "_red"] = (wide[2:], BF16)
     sems = dict(
-        send_sem=13, one_sem=8, got_sem=n_seq, att_sem=n_seq, datt_sem=n_seq, grad_sem=2, loss_sem=4,
-        red_send=12, red_recv=12,
+        send_sem=13, one_sem=8, got_sem=n_seq, att_sem=n_seq, datt_sem=n_seq, grad_sem=2, loss_sem=8,
+        red_send=30, red_recv=30, load_sem=6,
     )
-    takes = ("lens", "x", "history", "neg_ids", "w_joined", "w_out", "neg_emb")
-    gives = dict(
-        joined=((width, 4 * width), BF16), out=((width, width), BF16), loss_out=((1,), F32)
-    )
+    takes = ("lens", "x_in", "history_in", "neg_ids_in", "w_joined_in", "w_out_in", "neg_emb_in")
+    gives = {name + "_full": ((2,) + wide, BF16) for name in "uvqko"}
+    gives["loss_out"] = ((1,), F32)
     names = takes + tuple(gives) + tuple(buffers) + tuple(sems)
-    joined, out, loss = pl.pallas_call(
+    *grads, loss = pl.pallas_call(
         functools.partial(kernel, n_seq, names),
         out_shape=[jax.ShapeDtypeStruct(*kind) for kind in gives.values()],
-        in_specs=[SMEM] + [VMEM] * (len(takes) - 1),
-        out_specs=[VMEM, VMEM, SMEM],
+        in_specs=[SMEM] + [pl.BlockSpec(memory_space=pl.ANY)] * (len(takes) - 1),
+        out_specs=[VMEM] * 5 + [SMEM],
         scratch_shapes=[pltpu.VMEM(*kind) for kind in buffers.values()]
         + [dma((count,)) for count in sems.values()],
         compiler_params=pltpu.CompilerParams(
             collective_id=0, has_side_effects=True, vmem_limit_bytes=60 * 1024 * 1024
         ),
     )(lengths, inputs, history, neg_ids.reshape(-1, block), w_joined, w_out, neg_emb)
-    return (joined.astype(F32), out.astype(F32), loss.reshape(()))
+    taken = pl.BlockSpec((2, 1) + wide[1:], lambda at: (0, at, 0, 0, 0))
+    joined, out = pl.pallas_call(
+        widen,
+        grid=(4,),
+        out_shape=[
+            jax.ShapeDtypeStruct((width, 4 * width), F32), jax.ShapeDtypeStruct((width, width), F32)
+        ],
+        in_specs=[taken] * 5,
+        out_specs=[
+            pl.BlockSpec((width // 4, 4 * width), lambda at: (at, 0)),
+            pl.BlockSpec((width // 4, width), lambda at: (at, 0)),
+        ],
+        compiler_params=pltpu.CompilerParams(vmem_limit_bytes=32 * 1024 * 1024),
+    )(*grads)
+    return (joined, out, loss.reshape(()))
 
 
 def solution(mesh):

time: 158 us -> 173 us (1.095)
  Pallas kernels: 151 us -> 165 us
  other arithmetic: 5.29 us -> 0 us
  local copies, waits for them, and re-layouts: 0.01 us -> 5.2 us
    pallas_call x1, Pallas kernels: 151 us -> 162 us  [local(): pl.pallas_call(functools.partial(kernel, n_seq, names), out_shape=[jax.Sh...]
    convert_element_type x2 -> x0, other arithmetic: 5.29 us -> none  [local(): return (joined.astype(F32), out.astype(F32), loss.reshape(()))]
    unnamed x2 -> x10, local copies, waits for them, and re-layouts: 0.01 us -> 5.2 us
    pallas_call x0 -> x1, Pallas kernels: none -> 2.91 us  [local(): pl.pallas_call(widen, grid=(4,), out_shape=[jax.ShapeDtypeStruct((width,...]
where the time goes in v4:
time: 173 us
  Pallas kernels  165 us (95%)
  local copies, waits for them, and re-layouts  5.2 us (3%)
  between operations  2.47 us (1%)
    pallas_call x1, Pallas kernels, local(): pl.pallas_call(functools.partial(kernel, n_seq, names), out_shape=[jax.Sh...  162 us
    unnamed x10, local copies, waits for them, and re-layouts  5.2 us

profile of v4, /device:TPU:1, one launch (start us, length us, event | category | flops | bytes accessed | tf_op | source)
XLA Modules:
  0.0 172.7 jit_solution(8305381466446694845)
XLA Ops:
  0.6 162.1 %shard_map.94 = (bf16[2,4,16,16,128]{4,3,2,1,0:T(8,128)(2,1)}, bf16[2,4,16,16,128]{4,3,2,1,0:T(8,128)(2,1)}, bf16[2,4,16,16,128]{4,3,2,1,0:T(8,128)(2,1)}, bf16[...) custom-call(s32[16]{0:T(128)} %refs_0_.1, bf16[4,128,512]{2,1,0:T(8,128)(2,1)} %refs_1_.1, ...), custom_call_target="tpu_custom_call" | custom-call | tf_op jit(solution)/shard_map/pallas_call | solution.py:742
  162.8 0.0 copy-start
  162.8 1.0 copy-done
  163.8 0.0 copy-start.1
  163.8 1.0 copy-done.1
  164.9 0.0 copy-start.2
  164.9 1.0 copy-done.2
  165.9 0.0 copy-start.3
  165.9 1.0 copy-done.3
  166.9 0.0 copy-start.4
  166.9 1.0 copy-done.4
  168.0 2.9 %shard_map.95 = (f32[512,2048]{1,0:T(8,128)}, f32[512,512]{1,0:T(8,128)}) custom-call(bf16[2,4,16,16,128]{4,3,2,1,0:T(8,128)(2,1)S(1)} %copy-done, bf16[2,4,16,16,128]{4,3,2,1,0:T(8,128)(2,1)S(1)} %copy-done.1, bf16[2,4,16,16,128]{4,3,2,1,0:T(8,128)(2,1)S(1)} %copy-done.2, bf16[2,4,16,16,128]{4,3,2,1,0:T(8,128)(2,1)S(1)} %copy-done.3, ...), custom_call_target="tpu_custom_call" | custom-call | tf_op jit(solution)/shard_map/pallas_call | solution.py:754
Async XLA Ops:
  162.8 1.0 copy-start
  163.8 1.0 copy-start.1
  164.9 1.0 copy-start.2
  165.9 1.0 copy-start.3
  166.9 1.0 copy-start.4

commit v5 on v4

--- a/solution.py
+++ b/solution.py
@@ -91,6 +91,12 @@
             body((first + done + at * tiles) * TILE, tiles * TILE)
 
         done = done + n * tiles
+
+
+def tile_at(first, step, tiles):
+    low = lax.rem(first + step // 2, tiles // 2)
+    odd = lax.rem(step, 2)
+    return low + odd * (tiles - 1 - 2 * low)
 
 
 def kernel(n_seq, names, *refs):
@@ -128,7 +134,15 @@
             greet(dict(other_z, seq=(x_at * 4 + lax.rem(y_at + step, 4)) * 2 + z))
             if step:
                 greet(dict(other_z, seq=(lax.rem(x_at + step, 4) * 4 + y_at) * 2 + z))
-    n_peers = n_seq + 14
+
+    def lane(axis, along):
+        x, y, z = (along if axis == name else at for name, at in (("x", x_at), ("y", y_at), ("z", z_at)))
+        return {"grp": z // 2 * 2 + 1 - core, "seq": (x * 4 + y) * 2 + lax.rem(z, 2)}
+
+    for axis, at in (("x", x_at), ("y", y_at), ("z", z_at)):
+        for step in range(1, 4):
+            greet(lane(axis, lax.rem(at + step, 4)))
+    n_peers = n_seq + 14 + 9
 
     loads[0].wait()
     loads[1].wait()
@@ -222,7 +236,7 @@
 
     @pl.loop(0, f_tiles)
     def _(step):
-        c = lax.rem(me // f_per + step, f_tiles)
+        c = tile_at(me // f_per, f_tiles - 1 - step, f_tiles)
         q = r.qa[aligned(c * FQ, FQ)]
 
         def piece(start, size, masked):
@@ -290,81 +304,69 @@
     axes = dict(x=x_at, y=y_at, z=z_at)
     plane_at = dict(x=y_at * 4 + z_at, y=x_at * 4 + z_at, z=x_at * 4 + y_at)
 
-    def chip(axis, along, across):
+    def chip(axis, along, across, of_core=core):
         hi, lo = across // 4, lax.rem(across, 4)
         x, y, z = dict(x=(along, hi, lo), y=(hi, along, lo), z=(hi, lo, along))[axis]
-        return {"grp": z // 2 * 2 + core, "seq": (x * 4 + y) * 2 + lax.rem(z, 2)}
+        return {"grp": z // 2 * 2 + of_core, "seq": (x * 4 + y) * 2 + lax.rem(z, 2)}
 
     def reduction(name, axis, at):
-        part, got_core, sums, got, sums2, got2, red, full = (
-            getattr(r, name + tail)
-            for tail in ("_part", "_core", "_sum", "_got", "_sum2", "_got2", "_red", "_full")
+        part, got, sums, got2, red, full = (
+            getattr(r, name + tail) for tail in ("_part", "_got", "_sum", "_got2", "_red", "_full")
         )
-        send = [r.red_send.at[at * 6 + k] for k in range(6)]
-        recv = [r.red_recv.at[at * 6 + k] for k in range(6)]
+        send = [r.red_send.at[at * 4 + k] for k in range(4)]
+        recv = [r.red_recv.at[at * 4 + k] for k in range(4)]
         along, across = axes[axis], plane_at[axis]
-        rest = pl.ds(0, 15)
-
-        def to_core(grad):
-            for half in range(4):
-                block = grad[:, half * BLOCK:(half + 1) * BLOCK].astype(BF16)
-                low = half % 2 * 8
-                part[half // 2, :, low:low + 8] = block.reshape(4, 8, 16, BLOCK)
-            copy_to(part.at[1 - core], got_core, send[0], recv[0], mate)
-
-        def along_axis(sources, target, sems):
-            for step in range(1, 4):
-                to = lax.rem(along + step, 4)
-                copy_to(sources(to), target, *sems, chip(axis, to, across))
-
-        def over_plane(sources, target, sems):
+        mine = core * 4 + along
+        seven, fifteen = pl.ds(0, 7), pl.ds(0, 15)
+
+        def along_axis(source, target, sems):
+            @pl.loop(1, 8)
+            def _(step):
+                to = lax.rem(mine + step, 8)
+                copy_to(source(to), target, *sems, chip(axis, lax.rem(to, 4), across, to // 4))
+
+        def over_plane(source, target, sems):
             @pl.loop(1, 16)
             def _(step):
                 to = lax.rem(across + step, 16)
-                copy_to(sources(to), target, *sems, chip(axis, along, to))
-
-        def fold():
-            await_bytes(got_core, recv[0])
-            sums[...] = (part[core].astype(F32) + got_core[...].astype(F32)).astype(BF16)
-            along_axis(lambda to: sums.at[to], got.at[along], (send[1], recv[1]))
+                copy_to(source(to), target, *sems, chip(axis, along, to))
+
+        def scatter(grad):
+            for half in range(4):
+                block = grad[:, half * BLOCK:(half + 1) * BLOCK].astype(BF16)
+                low, first = half % 2 * 8, half // 2 * 4
+                part[first:first + 4, low:low + 8] = block.reshape(4, 8, 16, BLOCK)
+            along_axis(lambda to: part.at[to], got.at[mine], (send[0], recv[0]))
 
         def plane():
-            got[along] = sums[along]
-            await_bytes(got.at[pl.ds(0, 3)], recv[1])
-            sums2[...] = jnp.sum(got[...].astype(F32), axis=0).astype(BF16)
-            over_plane(lambda to: sums2.at[to], got2.at[across], (send[2], recv[2]))
+            got[mine] = part[mine]
+            await_bytes(got.at[seven], recv[0])
+            sums[...] = jnp.sum(got[...].astype(F32), axis=0).astype(BF16)
+            over_plane(lambda to: sums.at[to], got2.at[across], (send[1], recv[1]))
 
         def gather():
-            got2[across] = sums2[across]
-            await_bytes(got2.at[rest], recv[2])
+            got2[across] = sums[across]
+            await_bytes(got2.at[fifteen], recv[1])
             red[...] = jnp.sum(got2[...].astype(F32), axis=0).astype(BF16)
-            full[core, along, across] = red[...]
-            over_plane(lambda to: red, full.at[core, along, across], (send[3], recv[3]))
+            full[mine, across] = red[...]
+            over_plane(lambda to: red, full.at[mine, across], (send[2], recv[2]))
 
         def spread():
-            await_bytes(got2.at[rest], recv[3])
-            along_axis(lambda to: full.at[core, along], full.at[core, along], (send[4], recv[4]))
-
-        def share():
-            await_bytes(got.at[pl.ds(0, 3)], recv[4])
-            copy_to(full.at[core], full.at[core], send[5], recv[5], mate)
+            await_bytes(got2.at[fifteen], recv[2])
+            along_axis(lambda to: full.at[mine], full.at[mine], (send[3], recv[3]))
 
         def finish():
-            await_bytes(full.at[0], recv[5])
-            await_bytes(part.at[0], send[0])
-            await_bytes(got.at[pl.ds(0, 3)], send[1])
-            for k in (2, 3):
-                await_bytes(got2.at[rest], send[k])
-            await_bytes(got.at[pl.ds(0, 3)], send[4])
-            await_bytes(full.at[0], send[5])
-
-        return types.SimpleNamespace(
-            to_core=to_core, fold=fold, plane=plane, gather=gather, spread=spread, share=share, finish=finish
-        )
+            await_bytes(got.at[seven], recv[3])
+            await_bytes(got.at[seven], send[0])
+            await_bytes(got2.at[fifteen], send[1])
+            await_bytes(got2.at[fifteen], send[2])
+            await_bytes(got.at[seven], send[3])
+
+        return types.SimpleNamespace(scatter=scatter, plane=plane, gather=gather, spread=spread, finish=finish)
 
     early = [reduction("u", "x", 0), reduction("o", "y", 1)]
-    early[0].to_core(dot_nn(r.xnt[...], r.d_pre[:, :WIDTH]))
-    early[1].to_core(r.grad_out[...])
+    early[0].scatter(dot_nn(r.xnt[...], r.d_pre[:, :WIDTH]))
+    early[1].scatter(r.grad_out[...])
     copy_to(r.loss, r.loss_core, r.loss_sem.at[0], r.loss_sem.at[1], mate)
 
     def loss_along(axis, value, at):
@@ -403,9 +405,31 @@
     b_per = BM // BLOCK
     kv_scale = jnp.where(low_lanes((1, 2 * HEAD)), 0.5 * inv_len, inv_len)
 
+    def send_d_q(low, high):
+        @pl.loop(low, high)
+        def _(c):
+            for u in range(b_per):
+                d_q = r.dq[:, aligned((c * b_per + u) * BLOCK, BLOCK)] * (0.5 * inv_len)
+                r.grad_send[c * b_per + u, BLOCK:] = d_q.astype(BF16)
+
+            @pl.loop(0, b_per)
+            def _(turn):
+                i = c * b_per + lax.rem(me + turn, b_per)
+
+                @pl.when(i != me)
+                def _():
+                    copy_to(
+                        r.grad_send.at[i, pl.ds(BLOCK, HEAD)], r.grad_got.at[me, pl.ds(BLOCK, HEAD)],
+                        r.send_sem.at[11], r.grad_sem.at[1], {"seq": i},
+                    )
+
+                @pl.when(i == me)
+                def _():
+                    r.grad_got[me, BLOCK:] = r.grad_send[me, BLOCK:]
+
     @pl.loop(0, b_tiles)
     def _(step):
-        c = lax.rem(me // b_per + step, b_tiles)
+        c = tile_at(me // b_per, step, b_tiles)
         m_rows = aligned(c * BM, BM)
         low_tile = low_lanes((BM, 2 * HEAD))
 
@@ -452,11 +476,12 @@
             def _():
                 r.grad_got[me, :BLOCK] = r.grad_send[me, :BLOCK]
 
-        for at, stage in enumerate(("fold", "plane", "gather", "spread", "share")):
-            @pl.when(step == at)
+        for at, stage in enumerate(("plane", "gather", "spread", "")):
+            @pl.when(step == 2 * at + 1)
             def _(at=at, stage=stage):
-                for one in early:
-                    getattr(one, stage)()
+                if stage:
+                    for one in early:
+                        getattr(one, stage)()
                 if at == 0:
                     await_bytes(r.loss_core, r.loss_sem.at[1])
                     loss_along("x", r.loss[...] + r.loss_core[...], 0)
@@ -468,27 +493,15 @@
                     count = jnp.full((8, BLOCK), total, jnp.int32).astype(F32)
                     r.loss_out[0] = (loss_over(2) / count)[0, 0]
 
-    @pl.loop(0, b_tiles)
-    def _(step):
-        c = lax.rem(me // b_per + step, b_tiles)
-        for u in range(b_per):
-            d_q = r.dq[:, aligned((c * b_per + u) * BLOCK, BLOCK)] * (0.5 * inv_len)
-            r.grad_send[c * b_per + u, BLOCK:] = d_q.astype(BF16)
-
-        @pl.loop(0, b_per)
-        def _(turn):
-            i = c * b_per + lax.rem(me + turn, b_per)
-
-            @pl.when(i != me)
-            def _():
-                copy_to(
-                    r.grad_send.at[i, pl.ds(BLOCK, HEAD)], r.grad_got.at[me, pl.ds(BLOCK, HEAD)],
-                    r.send_sem.at[11], r.grad_sem.at[1], {"seq": i},
-                )
-
-            @pl.when(i == me)
-            def _():
-                r.grad_got[me, BLOCK:] = r.grad_send[me, BLOCK:]
+        end = tile_at(me // b_per, b_tiles - 1, b_tiles)
+
+        @pl.when(step == b_tiles - 2)
+        def _():
+            send_d_q(0, end)
+
+        @pl.when(step == b_tiles - 1)
+        def _():
+            send_d_q(end, b_tiles)
 
     late = [reduction("v", "x", 2), reduction("k", "y", 3), reduction("q", "z", 4)]
     await_bytes(r.grad_got.at[others, pl.ds(0, BLOCK)], r.grad_sem.at[0])
@@ -504,10 +517,8 @@
                 slope = r.slope[b, :, at:at + 2 * HEAD].astype(F32)
                 r.d_pre[rows, at:at + 2 * HEAD] = (grad * slope).astype(BF16)
 
-    late[0].to_core(dot_nn(r.xnt[...], r.d_pre[:, WIDTH:2 * WIDTH]))
-    late[1].to_core(dot_nn(r.xnt[...], r.d_pre[:, 3 * WIDTH:]))
-    late[0].fold()
-    late[1].fold()
+    late[0].scatter(dot_nn(r.xnt[...], r.d_pre[:, WIDTH:2 * WIDTH]))
+    late[1].scatter(dot_nn(r.xnt[...], r.d_pre[:, 3 * WIDTH:]))
     await_bytes(r.grad_got.at[others, pl.ds(BLOCK, HEAD)], r.grad_sem.at[1])
 
     @pl.loop(0, n_here)
@@ -522,20 +533,10 @@
             slope = r.slope[b, :, at:at + 2 * HEAD].astype(F32)
             r.d_pre[rows, at:at + 2 * HEAD] = (grad * slope).astype(BF16)
 
-    late[2].to_core(dot_nn(r.xnt[...], r.d_pre[:, 2 * WIDTH:3 * WIDTH]))
-    late[0].plane()
-    late[1].plane()
-    late[2].fold()
-    late[0].gather()
-    late[1].gather()
-    late[2].plane()
-    late[0].spread()
-    late[1].spread()
-    late[2].gather()
-    late[0].share()
-    late[1].share()
-    late[2].spread()
-    late[2].share()
+    late[2].scatter(dot_nn(r.xnt[...], r.d_pre[:, 2 * WIDTH:3 * WIDTH]))
+    for stage in ("plane", "gather", "spread"):
+        for one in late:
+            getattr(one, stage)()
 
     for one in early + late:
         one.finish()
@@ -723,20 +724,17 @@
         w_joined=((width, 4 * width), BF16), w_out=((width, width), BF16), neg_emb=((n_neg, width), BF16),
         history=((n_here, block), jnp.int32), neg_ids=((n_here, block), jnp.int32),
     )
-    wide = (4, 16, 16, block)
+    wide = (8, 16, 16, block)
     for name in "uovkq":
-        buffers[name + "_part"] = ((2,) + wide, BF16)
-        for tail in ("_core", "_sum", "_got"):
-            buffers[name + tail] = (wide, BF16)
-        for tail in ("_sum2", "_got2"):
-            buffers[name + tail] = (wide[1:], BF16)
+        buffers[name + "_part"] = buffers[name + "_got"] = (wide, BF16)
+        buffers[name + "_sum"] = buffers[name + "_got2"] = (wide[1:], BF16)
         buffers[name + "_red"] = (wide[2:], BF16)
     sems = dict(
         send_sem=13, one_sem=8, got_sem=n_seq, att_sem=n_seq, datt_sem=n_seq, grad_sem=2, loss_sem=8,
-        red_send=30, red_recv=30, load_sem=6,
+        red_send=20, red_recv=20, load_sem=6,
     )
     takes = ("lens", "x_in", "history_in", "neg_ids_in", "w_joined_in", "w_out_in", "neg_emb_in")
-    gives = {name + "_full": ((2,) + wide, BF16) for name in "uvqko"}
+    gives = {name + "_full": (wide, BF16) for name in "uvqko"}
     gives["loss_out"] = ((1,), F32)
     names = takes + tuple(gives) + tuple(buffers) + tuple(sems)
     *grads, loss = pl.pallas_call(
@@ -762,8 +760,8 @@
             pl.BlockSpec((width // 4, 4 * width), lambda at: (at, 0)),
             pl.BlockSpec((width // 4, width), lambda at: (at, 0)),
         ],
-        compiler_params=pltpu.CompilerParams(vmem_limit_bytes=32 * 1024 * 1024),
-    )(*grads)
+        compiler_params=pltpu.CompilerParams(vmem_limit_bytes=60 * 1024 * 1024),
+    )(*(grad.reshape((2, 4) + wide[1:]) for grad in grads))
     return (joined, out, loss.reshape(()))
 
 

time: 173 us -> 159 us (0.919)
  Pallas kernels: 165 us -> 156 us
  local copies, waits for them, and re-layouts: 5.2 us -> 0 us
    pallas_call x1, Pallas kernels: 162 us -> 151 us  [local(): pl.pallas_call(functools.partial(kernel, n_seq, names), out_shape=[jax.Sh...]
    unnamed x10 -> x0, local copies, waits for them, and re-layouts: 5.2 us -> none
    pallas_call x1, Pallas kernels: 2.91 us -> 4.77 us  [local(): pl.pallas_call(widen, grid=(4,), out_shape=[jax.ShapeDtypeStruct((width,...]
where the time goes in v5:
time: 159 us; the launch traced here: 158 us
  Pallas kernels  156 us (98%)
  between operations  2.33 us (1%)
    pallas_call x1, Pallas kernels, local(): pl.pallas_call(functools.partial(kernel, n_seq, names), out_shape=[jax.Sh...  151 us
    pallas_call x1, Pallas kernels, local(): pl.pallas_call(widen, grid=(4,), out_shape=[jax.ShapeDtypeStruct((width,...  4.77 us

profile of v5, /device:TPU:1, one launch (start us, length us, event | category | flops | bytes accessed | tf_op | source)
XLA Modules:
  0.0 158.4 jit_solution(9023203456853669657)
XLA Ops:
  0.6 151.3 %shard_map.94 = (bf16[8,16,16,128]{3,2,1,0:T(8,128)(2,1)}, bf16[8,16,16,128]{3,2,1,0:T(8,128)(2,1)}, bf16[8,16,16,128]{3,2,1,0:T(8,128)(2,1)}, bf16[8,16,16,128]...) custom-call(s32[16]{0:T(128)} %refs_0_.1, bf16[4,128,512]{2,1,0:T(8,128)(2,1)} %refs_1_.1, ...), custom_call_target="tpu_custom_call" | custom-call | tf_op jit(solution)/shard_map/pallas_call | solution.py:740
  152.0 4.8 %shard_map.95 = (f32[512,2048]{1,0:T(8,128)}, f32[512,512]{1,0:T(8,128)}) custom-call(bf16[2,4,16,16,128]{4,3,2,1,0:T(8,128)(2,1)} %bitcast.7, bf16[2,4,16,16,128]{4,3,2,1,0:T(8,128)(2,1)} %bitcast.8, bf16[2,4,16,16,128]{4,3,2,1,0:T(8,128)(2,1)} %bitcast.9, bf16[2,4,16,16,128]{4,3,2,1,0:T(8,128)(2,1)} %bitcast.10, bf16[2,4,16,16,128]{4,3,2,1,0:T(8,128)(2,1)} %bitcast.11), custom_call_target="tpu_custom_call" | custom-call | tf_op jit(solution)/shard_map/pallas_call | solution.py:752

commit v6 on v5

--- a/solution.py
+++ b/solution.py
@@ -83,12 +83,12 @@
 
 def cover(first, count, body):
     done = 0
-    for tiles in (4, 2, 1):
+    for tiles in (4, 2):
         n = count // tiles if tiles == 4 else lax.rem(count // tiles, 2)
 
         @pl.loop(0, n)
         def _(at, done=done, tiles=tiles):
-            body((first + done + at * tiles) * TILE, tiles * TILE)
+            body(first + done + at * tiles, tiles)
 
         done = done + n * tiles
 
@@ -216,8 +216,9 @@
             rows = aligned(i * BLOCK, BLOCK)
             pos = i * BLOCK + lax.broadcasted_iota(jnp.int32, (BLOCK, 2 * HEAD), 0)
             kv = jnp.where(pos < seq_len, r.got[i, :BLOCK].astype(F32), 0.0)
-            r.k0[rows] = jnp.where(low_block, 0.5 * kv, 0.0).astype(BF16)
-            r.v0[rows] = jnp.where(low_block, 0.0, kv).astype(BF16)
+            tile, at = i // (TILE // BLOCK), lax.rem(i, TILE // BLOCK) * BLOCK
+            r.kv0[tile, aligned(at, BLOCK)] = jnp.where(low_block, 0.5 * kv, 0.0).astype(BF16)
+            r.kv0[tile, aligned(TILE + at, BLOCK)] = jnp.where(low_block, 0.0, kv).astype(BF16)
             r.kt[:, rows] = jnp.transpose(kv)[:HEAD].astype(BF16)
             q = r.got[i, BLOCK:].astype(F32)
             r.qa[rows] = jnp.concatenate(
@@ -240,22 +241,31 @@
         q = r.qa[aligned(c * FQ, FQ)]
 
         def piece(start, size, masked):
-            rows = pl.ds(pl.multiple_of(start, TILE), size)
-            half = dot_nt(q, r.k0[rows])
+            rows = pl.ds(start, size)
+            size = size * TILE
+            half = dot_nt(q, r.kv0[rows, :TILE].reshape(size, 2 * HEAD))
             if masked:
                 ahead = lax.broadcasted_iota(jnp.int32, (FQ, size), 1) - lax.broadcasted_iota(
                     jnp.int32, (FQ, size), 0
                 )
-                half = jnp.where(ahead <= 0, half, 0.0)
+                half = jnp.where(ahead <= size - FQ, half, 0.0)
             probs = (half + half * jnp.tanh(half)).astype(BF16)
-            return dot_nn(probs, r.v0[rows])
-
-        r.acc[...] = piece(c * FQ, FQ, True)
+            return dot_nn(probs, r.kv0[rows, TILE:].reshape(size, 2 * HEAD))
+
+        odd = lax.rem(c, 2)
+
+        @pl.when(odd == 0)
+        def _():
+            r.acc[...] = piece(c, 1, True)
+
+        @pl.when(odd == 1)
+        def _():
+            r.acc[...] = piece(c - 1, 2, True)
 
         def more(start, size):
             r.acc[...] += piece(start, size, False)
 
-        cover(0, c, more)
+        cover(0, c - odd, more)
         for u in range(f_per):
             out = r.acc[u * BLOCK:(u + 1) * BLOCK] * inv_len
             top, bottom = out[:HEAD], out[HEAD:]
@@ -331,11 +341,14 @@
                 to = lax.rem(across + step, 16)
                 copy_to(source(to), target, *sems, chip(axis, along, to))
 
-        def scatter(grad):
-            for half in range(4):
-                block = grad[:, half * BLOCK:(half + 1) * BLOCK].astype(BF16)
-                low, first = half % 2 * 8, half // 2 * 4
-                part[first:first + 4, low:low + 8] = block.reshape(4, 8, 16, BLOCK)
+        def scatter(*grads):
+            for which, grad in enumerate(grads):
+                for half in range(4):
+                    block = grad[:, half * BLOCK:(half + 1) * BLOCK].astype(BF16)
+                    low, first = half % 2 * 8, half // 2 * 4
+                    part[first:first + 4, low:low + 8, which * 16:which * 16 + 16] = block.reshape(
+                        4, 8, 16, BLOCK
+                    )
             along_axis(lambda to: part.at[to], got.at[mine], (send[0], recv[0]))
 
         def plane():
@@ -364,9 +377,8 @@
 
         return types.SimpleNamespace(scatter=scatter, plane=plane, gather=gather, spread=spread, finish=finish)
 
-    early = [reduction("u", "x", 0), reduction("o", "y", 1)]
-    early[0].scatter(dot_nn(r.xnt[...], r.d_pre[:, :WIDTH]))
-    early[1].scatter(r.grad_out[...])
+    early = reduction("e", "x", 0)
+    early.scatter(dot_nn(r.xnt[...], r.d_pre[:, :WIDTH]), r.grad_out[...])
     copy_to(r.loss, r.loss_core, r.loss_sem.at[0], r.loss_sem.at[1], mate)
 
     def loss_along(axis, value, at):
@@ -434,10 +446,11 @@
         low_tile = low_lanes((BM, 2 * HEAD))
 
         def piece(start, size, masked):
-            t_rows = pl.ds(pl.multiple_of(start, TILE), size)
+            size = size * TILE
+            t_rows = pl.ds(pl.multiple_of(start * TILE, TILE), size)
             qa = r.qa[t_rows]
-            half = dot_nt(r.k0[m_rows], qa)
-            d_probs = dot_nt(r.v0[m_rows], qa)
+            products = dot_nt(r.kv0[c], qa)
+            half, d_probs = products[:TILE], products[TILE:]
             if masked:
                 ahead = lax.broadcasted_iota(jnp.int32, (BM, size), 0) - lax.broadcasted_iota(
                     jnp.int32, (BM, size), 1
@@ -450,12 +463,20 @@
             r.dq[:, t_rows] += dot_nn(r.kt[:, m_rows], d_scores)
             return jnp.where(low_tile, dot_nn(d_scores, qa), dot_nn(probs.astype(BF16), qa))
 
-        r.dkv[...] = piece(c * BM, BM, True)
+        odd = lax.rem(b_tiles - 1 - c, 2)
+
+        @pl.when(odd == 0)
+        def _():
+            r.dkv[...] = piece(c, 1, True)
+
+        @pl.when(odd == 1)
+        def _():
+            r.dkv[...] = piece(c, 2, True)
 
         def more(start, size):
             r.dkv[...] += piece(start, size, False)
 
-        cover(c + 1, b_tiles - 1 - c, more)
+        cover(c + 1 + odd, b_tiles - 1 - c - odd, more)
         for u in range(b_per):
             r.grad_send[c * b_per + u, :BLOCK] = (
                 r.dkv[u * BLOCK:(u + 1) * BLOCK] * kv_scale
@@ -480,8 +501,7 @@
             @pl.when(step == 2 * at + 1)
             def _(at=at, stage=stage):
                 if stage:
-                    for one in early:
-                        getattr(one, stage)()
+                    getattr(early, stage)()
                 if at == 0:
                     await_bytes(r.loss_core, r.loss_sem.at[1])
                     loss_along("x", r.loss[...] + r.loss_core[...], 0)
@@ -503,7 +523,7 @@
         def _():
             send_d_q(end, b_tiles)
 
-    late = [reduction("v", "x", 2), reduction("k", "y", 3), reduction("q", "z", 4)]
+    late = [reduction("v", "x", 1), reduction("k", "y", 2), reduction("q", "z", 3)]
     await_bytes(r.grad_got.at[others, pl.ds(0, BLOCK)], r.grad_sem.at[0])
 
     @pl.loop(0, n_here)
@@ -538,7 +558,7 @@
         for one in late:
             getattr(one, stage)()
 
-    for one in early + late:
+    for one in [early] + late:
         one.finish()
 
     await_bytes(r.first, r.send_sem.at[1])
@@ -688,14 +708,15 @@
 
 def widen(*refs):
     *blocks, joined, out = refs
-    for at, block in enumerate(blocks):
-        for half in range(4):
-            low = half % 2 * 8
-            values = block[half // 2, 0, low:low + 8].reshape(BLOCK, BLOCK).astype(F32)
-            if at < 4:
-                joined[:, at * WIDTH + half * BLOCK:at * WIDTH + (half + 1) * BLOCK] = values
-            else:
-                out[:, half * BLOCK:(half + 1) * BLOCK] = values
+    for half in range(4):
+        low = half % 2 * 8
+
+        def taken(block, first):
+            return block[half // 2, 0, low:low + 8, first:first + 16].reshape(BLOCK, BLOCK).astype(F32)
+
+        for at, block in enumerate(blocks):
+            joined[:, at * WIDTH + half * BLOCK:at * WIDTH + (half + 1) * BLOCK] = taken(block, 0)
+        out[:, half * BLOCK:(half + 1) * BLOCK] = taken(blocks[0], 16)
 
 
 def local(inputs, history, lengths, w_joined, w_out, neg_emb, neg_ids):
@@ -716,7 +737,7 @@
         first=((n_here, 16, width), BF16), ids=((2 * n_here, block), jnp.int32),
         next_ids=((2 * n_here, block), jnp.int32), negs=((4, n_neg, width), BF16),
         all_ids=((4, 2 * n_here, block), jnp.int32),
-        k0=((length, lanes), BF16), v0=((length, lanes), BF16), qa=((length, lanes), BF16),
+        kv0=((length // TILE, 2 * TILE, lanes), BF16), qa=((length, lanes), BF16),
         kt=((HEAD, length), BF16), acc=((FQ, lanes), F32), dq=((HEAD, length), F32), dkv=((BM, lanes), F32),
         att=((2 * block, width), F32), exps=((2 * block, 4 * n_neg), F32), grad_out=((width, width), F32),
         loss=((8, block), F32), loss_core=((8, block), F32), loss_sum=((3, 8, block), F32),
@@ -725,43 +746,47 @@
         history=((n_here, block), jnp.int32), neg_ids=((n_here, block), jnp.int32),
     )
     wide = (8, 16, 16, block)
-    for name in "uovkq":
-        buffers[name + "_part"] = buffers[name + "_got"] = (wide, BF16)
-        buffers[name + "_sum"] = buffers[name + "_got2"] = (wide[1:], BF16)
-        buffers[name + "_red"] = (wide[2:], BF16)
+    shapes = dict(e=(8, 16, 32, block), v=wide, k=wide, q=wide)
+    for name, shape in shapes.items():
+        buffers[name + "_part"] = buffers[name + "_got"] = (shape, BF16)
+        buffers[name + "_sum"] = buffers[name + "_got2"] = (shape[1:], BF16)
+        buffers[name + "_red"] = (shape[2:], BF16)
     sems = dict(
         send_sem=13, one_sem=8, got_sem=n_seq, att_sem=n_seq, datt_sem=n_seq, grad_sem=2, loss_sem=8,
-        red_send=20, red_recv=20, load_sem=6,
+        red_send=16, red_recv=16, load_sem=6,
     )
     takes = ("lens", "x_in", "history_in", "neg_ids_in", "w_joined_in", "w_out_in", "neg_emb_in")
-    gives = {name + "_full": (wide, BF16) for name in "uvqko"}
+    gives = {name + "_full": (shapes[name], BF16) for name in "evqk"}
     gives["loss_out"] = ((1,), F32)
     names = takes + tuple(gives) + tuple(buffers) + tuple(sems)
     *grads, loss = pl.pallas_call(
         functools.partial(kernel, n_seq, names),
         out_shape=[jax.ShapeDtypeStruct(*kind) for kind in gives.values()],
         in_specs=[SMEM] + [pl.BlockSpec(memory_space=pl.ANY)] * (len(takes) - 1),
-        out_specs=[VMEM] * 5 + [SMEM],
+        out_specs=[VMEM] * 4 + [SMEM],
         scratch_shapes=[pltpu.VMEM(*kind) for kind in buffers.values()]
         + [dma((count,)) for count in sems.values()],
         compiler_params=pltpu.CompilerParams(
             collective_id=0, has_side_effects=True, vmem_limit_bytes=60 * 1024 * 1024
         ),
     )(lengths, inputs, history, neg_ids.reshape(-1, block), w_joined, w_out, neg_emb)
-    taken = pl.BlockSpec((2, 1) + wide[1:], lambda at: (0, at, 0, 0, 0))
+    grads = [grad.reshape((2, 4) + grad.shape[1:]) for grad in grads]
+    taken = [
+        pl.BlockSpec((2, 1) + grad.shape[2:], lambda at: (0, at, 0, 0, 0)) for grad in grads
+    ]
     joined, out = pl.pallas_call(
         widen,
         grid=(4,),
         out_shape=[
             jax.ShapeDtypeStruct((width, 4 * width), F32), jax.ShapeDtypeStruct((width, width), F32)
         ],
-        in_specs=[taken] * 5,
+        in_specs=taken,
         out_specs=[
             pl.BlockSpec((width // 4, 4 * width), lambda at: (at, 0)),
             pl.BlockSpec((width // 4, width), lambda at: (at, 0)),
         ],
         compiler_params=pltpu.CompilerParams(vmem_limit_bytes=60 * 1024 * 1024),
-    )(*(grad.reshape((2, 4) + wide[1:]) for grad in grads))
+    )(*grads)
     return (joined, out, loss.reshape(()))
 
 

time: 159 us -> 163 us (1.025)
  Pallas kernels: 156 us -> 161 us
    pallas_call x1, Pallas kernels: 151 us -> 156 us  [local(): pl.pallas_call(functools.partial(kernel, n_seq, names), out_shape=[jax.Sh...]
where the time goes in v6:
time: 163 us
  Pallas kernels  161 us (99%)
  between operations  2.33 us (1%)
    pallas_call x1, Pallas kernels, local(): pl.pallas_call(functools.partial(kernel, n_seq, names), out_shape=[jax.Sh...  156 us
    pallas_call x1, Pallas kernels, local(): pl.pallas_call(widen, grid=(4,), out_shape=[jax.ShapeDtypeStruct((width,...  4.79 us

profile of v6, /device:TPU:1, one launch (start us, length us, event | category | flops | bytes accessed | tf_op | source)
XLA Modules:
  0.0 163.3 jit_solution(9251029762577622393)
XLA Ops:
  0.6 156.2 %shard_map.94 = (bf16[8,16,32,128]{3,2,1,0:T(8,128)(2,1)}, bf16[8,16,16,128]{3,2,1,0:T(8,128)(2,1)}, bf16[8,16,16,128]{3,2,1,0:T(8,128)(2,1)}, bf16[8,16,16,128]{3,2,1,0:T(8,128)(2,1)}, f32[1]{0:T(128)}) custom-call(s32[16]{0:T(128)} %refs_0_.1, bf16[4,128,512]{2,1,0:T(8,128)(2,1)} %refs_1_.1, s32[4,128]{1,0:T(4,128)} %refs_2_.1, s32[4,128]{1,0:T(4,128)} %bitcast.10, ...), custom_call_target="tpu_custom_call" | custom-call | tf_op jit(solution)/shard_map/pallas_call | solution.py:762
  156.8 4.8 %shard_map.95 = (f32[512,2048]{1,0:T(8,128)}, f32[512,512]{1,0:T(8,128)}) custom-call(bf16[2,4,16,32,128]{4,3,2,1,0:T(8,128)(2,1)} %bitcast.6, bf16[2,4,16,16,128]{4,3,2,1,0:T(8,128)(2,1)} %bitcast.7, bf16[2,4,16,16,128]{4,3,2,1,0:T(8,128)(2,1)} %bitcast.8, bf16[2,4,16,16,128]{4,3,2,1,0:T(8,128)(2,1)} %bitcast.9), custom_call_target="tpu_custom_call" | custom-call | tf_op jit(solution)/shard_map/pallas_call | solution.py:777

commit v7 on v5

--- a/solution.py
+++ b/solution.py
@@ -83,12 +83,12 @@
 
 def cover(first, count, body):
     done = 0
-    for tiles in (4, 2, 1):
+    for tiles in (4, 2):
         n = count // tiles if tiles == 4 else lax.rem(count // tiles, 2)
 
         @pl.loop(0, n)
         def _(at, done=done, tiles=tiles):
-            body((first + done + at * tiles) * TILE, tiles * TILE)
+            body(first + done + at * tiles, tiles)
 
         done = done + n * tiles
 
@@ -216,8 +216,9 @@
             rows = aligned(i * BLOCK, BLOCK)
             pos = i * BLOCK + lax.broadcasted_iota(jnp.int32, (BLOCK, 2 * HEAD), 0)
             kv = jnp.where(pos < seq_len, r.got[i, :BLOCK].astype(F32), 0.0)
-            r.k0[rows] = jnp.where(low_block, 0.5 * kv, 0.0).astype(BF16)
-            r.v0[rows] = jnp.where(low_block, 0.0, kv).astype(BF16)
+            tile, at = i // (TILE // BLOCK), lax.rem(i, TILE // BLOCK) * BLOCK
+            r.kv0[tile, aligned(at, BLOCK)] = jnp.where(low_block, 0.5 * kv, 0.0).astype(BF16)
+            r.kv0[tile, aligned(TILE + at, BLOCK)] = jnp.where(low_block, 0.0, kv).astype(BF16)
             r.kt[:, rows] = jnp.transpose(kv)[:HEAD].astype(BF16)
             q = r.got[i, BLOCK:].astype(F32)
             r.qa[rows] = jnp.concatenate(
@@ -240,22 +241,31 @@
         q = r.qa[aligned(c * FQ, FQ)]
 
         def piece(start, size, masked):
-            rows = pl.ds(pl.multiple_of(start, TILE), size)
-            half = dot_nt(q, r.k0[rows])
+            rows = pl.ds(start, size)
+            size = size * TILE
+            half = dot_nt(q, r.kv0[rows, :TILE].reshape(size, 2 * HEAD))
             if masked:
                 ahead = lax.broadcasted_iota(jnp.int32, (FQ, size), 1) - lax.broadcasted_iota(
                     jnp.int32, (FQ, size), 0
                 )
-                half = jnp.where(ahead <= 0, half, 0.0)
+                half = jnp.where(ahead <= size - FQ, half, 0.0)
             probs = (half + half * jnp.tanh(half)).astype(BF16)
-            return dot_nn(probs, r.v0[rows])
-
-        r.acc[...] = piece(c * FQ, FQ, True)
+            return dot_nn(probs, r.kv0[rows, TILE:].reshape(size, 2 * HEAD))
+
+        odd = lax.rem(c, 2)
+
+        @pl.when(odd == 0)
+        def _():
+            r.acc[...] = piece(c, 1, True)
+
+        @pl.when(odd == 1)
+        def _():
+            r.acc[...] = piece(c - 1, 2, True)
 
         def more(start, size):
             r.acc[...] += piece(start, size, False)
 
-        cover(0, c, more)
+        cover(0, c - odd, more)
         for u in range(f_per):
             out = r.acc[u * BLOCK:(u + 1) * BLOCK] * inv_len
             top, bottom = out[:HEAD], out[HEAD:]
@@ -365,8 +375,6 @@
         return types.SimpleNamespace(scatter=scatter, plane=plane, gather=gather, spread=spread, finish=finish)
 
     early = [reduction("u", "x", 0), reduction("o", "y", 1)]
-    early[0].scatter(dot_nn(r.xnt[...], r.d_pre[:, :WIDTH]))
-    early[1].scatter(r.grad_out[...])
     copy_to(r.loss, r.loss_core, r.loss_sem.at[0], r.loss_sem.at[1], mate)
 
     def loss_along(axis, value, at):
@@ -400,6 +408,9 @@
             low_block, qa, jnp.concatenate([turned(d_att), d_att], axis=0)
         ).astype(BF16)
 
+    early[0].scatter(dot_nn(r.xnt[...], r.d_pre[:, :WIDTH]))
+    early[1].scatter(r.grad_out[...])
+
     r.dq[...] = jnp.zeros_like(r.dq)
     b_tiles = length // BM
     b_per = BM // BLOCK
@@ -434,10 +445,11 @@
         low_tile = low_lanes((BM, 2 * HEAD))
 
         def piece(start, size, masked):
-            t_rows = pl.ds(pl.multiple_of(start, TILE), size)
+            size = size * TILE
+            t_rows = pl.ds(pl.multiple_of(start * TILE, TILE), size)
             qa = r.qa[t_rows]
-            half = dot_nt(r.k0[m_rows], qa)
-            d_probs = dot_nt(r.v0[m_rows], qa)
+            products = dot_nt(r.kv0[c], qa)
+            half, d_probs = products[:TILE], products[TILE:]
             if masked:
                 ahead = lax.broadcasted_iota(jnp.int32, (BM, size), 0) - lax.broadcasted_iota(
                     jnp.int32, (BM, size), 1
@@ -450,12 +462,20 @@
             r.dq[:, t_rows] += dot_nn(r.kt[:, m_rows], d_scores)
             return jnp.where(low_tile, dot_nn(d_scores, qa), dot_nn(probs.astype(BF16), qa))
 
-        r.dkv[...] = piece(c * BM, BM, True)
+        odd = lax.rem(b_tiles - 1 - c, 2)
+
+        @pl.when(odd == 0)
+        def _():
+            r.dkv[...] = piece(c, 1, True)
+
+        @pl.when(odd == 1)
+        def _():
+            r.dkv[...] = piece(c, 2, True)
 
         def more(start, size):
             r.dkv[...] += piece(start, size, False)
 
-        cover(c + 1, b_tiles - 1 - c, more)
+        cover(c + 1 + odd, b_tiles - 1 - c - odd, more)
         for u in range(b_per):
             r.grad_send[c * b_per + u, :BLOCK] = (
                 r.dkv[u * BLOCK:(u + 1) * BLOCK] * kv_scale
@@ -716,7 +736,7 @@
         first=((n_here, 16, width), BF16), ids=((2 * n_here, block), jnp.int32),
         next_ids=((2 * n_here, block), jnp.int32), negs=((4, n_neg, width), BF16),
         all_ids=((4, 2 * n_here, block), jnp.int32),
-        k0=((length, lanes), BF16), v0=((length, lanes), BF16), qa=((length, lanes), BF16),
+        kv0=((length // TILE, 2 * TILE, lanes), BF16), qa=((length, lanes), BF16),
         kt=((HEAD, length), BF16), acc=((FQ, lanes), F32), dq=((HEAD, length), F32), dkv=((BM, lanes), F32),
         att=((2 * block, width), F32), exps=((2 * block, 4 * n_neg), F32), grad_out=((width, width), F32),
         loss=((8, block), F32), loss_core=((8, block), F32), loss_sum=((3, 8, block), F32),

time: 159 us -> 157 us (0.987)
  Pallas kernels: 156 us -> 154 us
    pallas_call x1, Pallas kernels: 151 us -> 149 us  [local(): pl.pallas_call(functools.partial(kernel, n_seq, names), out_shape=[jax.Sh...]
where the time goes in v7:
time: 157 us
  Pallas kernels  154 us (98%)
  between operations  2.33 us (1%)
    pallas_call x1, Pallas kernels, local(): pl.pallas_call(functools.partial(kernel, n_seq, names), out_shape=[jax.Sh...  149 us
    pallas_call x1, Pallas kernels, local(): pl.pallas_call(widen, grid=(4,), out_shape=[jax.ShapeDtypeStruct((width,...  4.77 us

profile of v7, /device:TPU:1, one launch (start us, length us, event | category | flops | bytes accessed | tf_op | source)
XLA Modules:
  0.0 156.5 jit_solution(5066469396349126411)
XLA Ops:
  0.6 149.4 %shard_map.94 = (bf16[8,16,16,128]{3,2,1,0:T(8,128)(2,1)}, bf16[8,16,16,128]{3,2,1,0:T(8,128)(2,1)}, bf16[8,16,16,128]{3,2,1,0:T(8,128)(2,1)}, bf16[8,16,16,128]...) custom-call(s32[16]{0:T(128)} %refs_0_.1, bf16[4,128,512]{2,1,0:T(8,128)(2,1)} %refs_1_.1, ...), custom_call_target="tpu_custom_call" | custom-call | tf_op jit(solution)/shard_map/pallas_call | solution.py:760
  150.1 4.8 %shard_map.95 = (f32[512,2048]{1,0:T(8,128)}, f32[512,512]{1,0:T(8,128)}) custom-call(bf16[2,4,16,16,128]{4,3,2,1,0:T(8,128)(2,1)} %bitcast.7, bf16[2,4,16,16,128]{4,3,2,1,0:T(8,128)(2,1)} %bitcast.8, bf16[2,4,16,16,128]{4,3,2,1,0:T(8,128)(2,1)} %bitcast.9, bf16[2,4,16,16,128]{4,3,2,1,0:T(8,128)(2,1)} %bitcast.10, bf16[2,4,16,16,128]{4,3,2,1,0:T(8,128)(2,1)} %bitcast.11), custom_call_target="tpu_custom_call" | custom-call | tf_op jit(solution)/shard_map/pallas_call | solution.py:772

commit v8 on v7

--- a/solution.py
+++ b/solution.py
@@ -330,22 +330,24 @@
         seven, fifteen = pl.ds(0, 7), pl.ds(0, 15)
 
         def along_axis(source, target, sems):
-            @pl.loop(1, 8)
+            @pl.loop(1, 8, unroll=7)
             def _(step):
                 to = lax.rem(mine + step, 8)
                 copy_to(source(to), target, *sems, chip(axis, lax.rem(to, 4), across, to // 4))
 
         def over_plane(source, target, sems):
-            @pl.loop(1, 16)
+            @pl.loop(1, 16, unroll=5)
             def _(step):
                 to = lax.rem(across + step, 16)
                 copy_to(source(to), target, *sems, chip(axis, along, to))
 
-        def scatter(grad):
+        def pack(grad):
             for half in range(4):
                 block = grad[:, half * BLOCK:(half + 1) * BLOCK].astype(BF16)
                 low, first = half % 2 * 8, half // 2 * 4
                 part[first:first + 4, low:low + 8] = block.reshape(4, 8, 16, BLOCK)
+
+        def scatter():
             along_axis(lambda to: part.at[to], got.at[mine], (send[0], recv[0]))
 
         def plane():
@@ -372,9 +374,12 @@
             await_bytes(got2.at[fifteen], send[2])
             await_bytes(got.at[seven], send[3])
 
-        return types.SimpleNamespace(scatter=scatter, plane=plane, gather=gather, spread=spread, finish=finish)
+        return types.SimpleNamespace(
+            pack=pack, scatter=scatter, plane=plane, gather=gather, spread=spread, finish=finish)
 
     early = [reduction("u", "x", 0), reduction("o", "y", 1)]
+    early[0].pack(dot_nn(r.xnt[...], r.d_pre[:, :WIDTH]))
+    early[1].pack(r.grad_out[...])
     copy_to(r.loss, r.loss_core, r.loss_sem.at[0], r.loss_sem.at[1], mate)
 
     def loss_along(axis, value, at):
@@ -408,8 +413,8 @@
             low_block, qa, jnp.concatenate([turned(d_att), d_att], axis=0)
         ).astype(BF16)
 
-    early[0].scatter(dot_nn(r.xnt[...], r.d_pre[:, :WIDTH]))
-    early[1].scatter(r.grad_out[...])
+    early[0].scatter()
+    early[1].scatter()
 
     r.dq[...] = jnp.zeros_like(r.dq)
     b_tiles = length // BM
@@ -456,9 +461,10 @@
                 )
                 half = jnp.where(ahead <= 0, half, 0.0)
                 d_probs = jnp.where(ahead <= 0, d_probs, 0.0)
-            up = 1.0 + jnp.tanh(half)
+            th = jnp.tanh(half)
+            up = 1.0 + th
             probs = half * up
-            d_scores = (d_probs * up * (1.0 + (half + half) - probs)).astype(BF16)
+            d_scores = (d_probs * up * (1.0 + half * (1.0 - th))).astype(BF16)
             r.dq[:, t_rows] += dot_nn(r.kt[:, m_rows], d_scores)
             return jnp.where(low_tile, dot_nn(d_scores, qa), dot_nn(probs.astype(BF16), qa))
 
@@ -537,8 +543,10 @@
                 slope = r.slope[b, :, at:at + 2 * HEAD].astype(F32)
                 r.d_pre[rows, at:at + 2 * HEAD] = (grad * slope).astype(BF16)
 
-    late[0].scatter(dot_nn(r.xnt[...], r.d_pre[:, WIDTH:2 * WIDTH]))
-    late[1].scatter(dot_nn(r.xnt[...], r.d_pre[:, 3 * WIDTH:]))
+    late[0].pack(dot_nn(r.xnt[...], r.d_pre[:, WIDTH:2 * WIDTH]))
+    late[0].scatter()
+    late[1].pack(dot_nn(r.xnt[...], r.d_pre[:, 3 * WIDTH:]))
+    late[1].scatter()
     await_bytes(r.grad_got.at[others, pl.ds(BLOCK, HEAD)], r.grad_sem.at[1])
 
     @pl.loop(0, n_here)
@@ -553,7 +561,8 @@
             slope = r.slope[b, :, at:at + 2 * HEAD].astype(F32)
             r.d_pre[rows, at:at + 2 * HEAD] = (grad * slope).astype(BF16)
 
-    late[2].scatter(dot_nn(r.xnt[...], r.d_pre[:, 2 * WIDTH:3 * WIDTH]))
+    late[2].pack(dot_nn(r.xnt[...], r.d_pre[:, 2 * WIDTH:3 * WIDTH]))
+    late[2].scatter()
     for stage in ("plane", "gather", "spread"):
         for one in late:
             getattr(one, stage)()
@@ -710,8 +719,7 @@
     *blocks, joined, out = refs
     for at, block in enumerate(blocks):
         for half in range(4):
-            low = half % 2 * 8
-            values = block[half // 2, 0, low:low + 8].reshape(BLOCK, BLOCK).astype(F32)
+            values = block[half // 2, 0, half % 2].reshape(HEAD, BLOCK).astype(F32)
             if at < 4:
                 joined[:, at * WIDTH + half * BLOCK:at * WIDTH + (half + 1) * BLOCK] = values
             else:
@@ -768,20 +776,20 @@
             collective_id=0, has_side_effects=True, vmem_limit_bytes=60 * 1024 * 1024
         ),
     )(lengths, inputs, history, neg_ids.reshape(-1, block), w_joined, w_out, neg_emb)
-    taken = pl.BlockSpec((2, 1) + wide[1:], lambda at: (0, at, 0, 0, 0))
+    taken = pl.BlockSpec((2, 1, 2, 4, 16, block), lambda at: (0, at // 2, 0, at % 2, 0, 0))
     joined, out = pl.pallas_call(
         widen,
-        grid=(4,),
+        grid=(8,),
         out_shape=[
             jax.ShapeDtypeStruct((width, 4 * width), F32), jax.ShapeDtypeStruct((width, width), F32)
         ],
         in_specs=[taken] * 5,
         out_specs=[
-            pl.BlockSpec((width // 4, 4 * width), lambda at: (at, 0)),
-            pl.BlockSpec((width // 4, width), lambda at: (at, 0)),
+            pl.BlockSpec((width // 8, 4 * width), lambda at: (at, 0)),
+            pl.BlockSpec((width // 8, width), lambda at: (at, 0)),
         ],
         compiler_params=pltpu.CompilerParams(vmem_limit_bytes=60 * 1024 * 1024),
-    )(*(grad.reshape((2, 4) + wide[1:]) for grad in grads))
+    )(*(grad.reshape((2, 4, 2, 8) + wide[2:]) for grad in grads))
     return (joined, out, loss.reshape(()))
 
 

time: 157 us -> 157 us (level)
    pallas_call x1, Pallas kernels: 149 us -> 148 us  [local(): pl.pallas_call(functools.partial(kernel, n_seq, names), out_shape=[jax.Sh...]
    pallas_call x1, Pallas kernels: 4.77 us -> 6.46 us  [local(): pl.pallas_call(widen, grid=(8,), out_shape=[jax.ShapeDtypeStruct((width,...]
where the time goes in v8:
time: 157 us; the launch traced here: 156 us
  Pallas kernels  154 us (98%)
  between operations  2.33 us (1%)
    pallas_call x1, Pallas kernels, local(): pl.pallas_call(functools.partial(kernel, n_seq, names), out_shape=[jax.Sh...  148 us
    pallas_call x1, Pallas kernels, local(): pl.pallas_call(widen, grid=(8,), out_shape=[jax.ShapeDtypeStruct((width,...  6.46 us

profile of v8, /device:TPU:1, one launch (start us, length us, event | category | flops | bytes accessed | tf_op | source)
XLA Modules:
  0.0 156.5 jit_solution(13004451427262852412)
XLA Ops:
  0.6 147.7 %shard_map.94 = (bf16[8,16,16,128]{3,2,1,0:T(8,128)(2,1)}, bf16[8,16,16,128]{3,2,1,0:T(8,128)(2,1)}, bf16[8,16,16,128]{3,2,1,0:T(8,128)(2,1)}, bf16[8,16,16,128]...) custom-call(s32[16]{0:T(128)} %refs_0_.1, bf16[4,128,512]{2,1,0:T(8,128)(2,1)} %refs_1_.1, ...), custom_call_target="tpu_custom_call" | custom-call | tf_op jit(solution)/shard_map/pallas_call | solution.py:768
  148.3 6.5 %shard_map.95 = (f32[512,2048]{1,0:T(8,128)}, f32[512,512]{1,0:T(8,128)}) custom-call(bf16[2,4,2,8,16,128]{5,4,3,2,1,0:T(8,128)(2,1)} %bitcast.7, bf16[2,4,2,8,16,128]{5,4,3,2,1,0:T(8,128)(2,1)} %bitcast.8, bf16[2,4,2,8,16,128]{5,4,3,2,1,0:T(8,128)(2,1)} %bitcast.9, bf16[2,4,2,8,16,128]{5,4,3,2,1,0:T(8,128)(2,1)} %bitcast.10, ...), custom_call_target="tpu_custom_call" | custom-call | tf_op jit(solution)/shard_map/pallas_call | solution.py:780

commit v9 on v8

--- a/solution.py
+++ b/solution.py
@@ -502,12 +502,9 @@
             def _():
                 r.grad_got[me, :BLOCK] = r.grad_send[me, :BLOCK]
 
-        for at, stage in enumerate(("plane", "gather", "spread", "")):
+        for at in range(4):
             @pl.when(step == 2 * at + 1)
-            def _(at=at, stage=stage):
-                if stage:
-                    for one in early:
-                        getattr(one, stage)()
+            def _(at=at):
                 if at == 0:
                     await_bytes(r.loss_core, r.loss_sem.at[1])
                     loss_along("x", r.loss[...] + r.loss_core[...], 0)
@@ -530,6 +527,8 @@
             send_d_q(end, b_tiles)
 
     late = [reduction("v", "x", 2), reduction("k", "y", 3), reduction("q", "z", 4)]
+    for one in early:
+        one.plane()
     await_bytes(r.grad_got.at[others, pl.ds(0, BLOCK)], r.grad_sem.at[0])
 
     @pl.loop(0, n_here)
@@ -563,9 +562,16 @@
 
     late[2].pack(dot_nn(r.xnt[...], r.d_pre[:, 2 * WIDTH:3 * WIDTH]))
     late[2].scatter()
-    for stage in ("plane", "gather", "spread"):
-        for one in late:
-            getattr(one, stage)()
+    for one in early:
+        one.gather()
+    for one in late:
+        one.plane()
+    for one in early:
+        one.spread()
+    for one in late:
+        one.gather()
+    for one in late:
+        one.spread()
 
     for one in early + late:
         one.finish()

time: 157 us -> 156 us (level)
  no operation moved by 1% of the time
where the time goes in v9:
time: 156 us
  Pallas kernels  153 us (98%)
  between operations  2.33 us (1%)
    pallas_call x1, Pallas kernels, local(): pl.pallas_call(functools.partial(kernel, n_seq, names), out_shape=[jax.Sh...  147 us
    pallas_call x1, Pallas kernels, local(): pl.pallas_call(widen, grid=(8,), out_shape=[jax.ShapeDtypeStruct((width,...  6.46 us

profile of v9, /device:TPU:1, one launch (start us, length us, event | category | flops | bytes accessed | tf_op | source)
XLA Modules:
  0.0 155.8 jit_solution(6915324146169979514)
XLA Ops:
  0.6 147.0 %shard_map.94 = (bf16[8,16,16,128]{3,2,1,0:T(8,128)(2,1)}, bf16[8,16,16,128]{3,2,1,0:T(8,128)(2,1)}, bf16[8,16,16,128]{3,2,1,0:T(8,128)(2,1)}, bf16[8,16,16,128]...) custom-call(s32[16]{0:T(128)} %refs_0_.1, bf16[4,128,512]{2,1,0:T(8,128)(2,1)} %refs_1_.1, ...), custom_call_target="tpu_custom_call" | custom-call | tf_op jit(solution)/shard_map/pallas_call | solution.py:774
  147.7 6.5 %shard_map.95 = (f32[512,2048]{1,0:T(8,128)}, f32[512,512]{1,0:T(8,128)}) custom-call(bf16[2,4,2,8,16,128]{5,4,3,2,1,0:T(8,128)(2,1)} %bitcast.7, bf16[2,4,2,8,16,128]{5,4,3,2,1,0:T(8,128)(2,1)} %bitcast.8, bf16[2,4,2,8,16,128]{5,4,3,2,1,0:T(8,128)(2,1)} %bitcast.9, bf16[2,4,2,8,16,128]{5,4,3,2,1,0:T(8,128)(2,1)} %bitcast.10, ...), custom_call_target="tpu_custom_call" | custom-call | tf_op jit(solution)/shard_map/pallas_call | solution.py:786

commit v10 on v8

--- a/solution.py
+++ b/solution.py
@@ -237,7 +237,7 @@
 
     @pl.loop(0, f_tiles)
     def _(step):
-        c = tile_at(me // f_per, f_tiles - 1 - step, f_tiles)
+        c = tile_at(me // f_per, step, f_tiles)
         q = r.qa[aligned(c * FQ, FQ)]
 
         def piece(start, size, masked):

time: 157 us -> 156 us (level)
  no operation moved by 1% of the time
where the time goes in v10:
time: 156 us
  Pallas kernels  154 us (99%)
  between operations  2.33 us (1%)
    pallas_call x1, Pallas kernels, local(): pl.pallas_call(functools.partial(kernel, n_seq, names), out_shape=[jax.Sh...  147 us
    pallas_call x1, Pallas kernels, local(): pl.pallas_call(widen, grid=(8,), out_shape=[jax.ShapeDtypeStruct((width,...  6.46 us

profile of v10, /device:TPU:1, one launch (start us, length us, event | category | flops | bytes accessed | tf_op | source)
XLA Modules:
  0.0 155.9 jit_solution(11733402541707977424)
XLA Ops:
  0.6 147.1 %shard_map.94 = (bf16[8,16,16,128]{3,2,1,0:T(8,128)(2,1)}, bf16[8,16,16,128]{3,2,1,0:T(8,128)(2,1)}, bf16[8,16,16,128]{3,2,1,0:T(8,128)(2,1)}, bf16[8,16,16,128]...) custom-call(s32[16]{0:T(128)} %refs_0_.1, bf16[4,128,512]{2,1,0:T(8,128)(2,1)} %refs_1_.1, ...), custom_call_target="tpu_custom_call" | custom-call | tf_op jit(solution)/shard_map/pallas_call | solution.py:768
  147.7 6.5 %shard_map.95 = (f32[512,2048]{1,0:T(8,128)}, f32[512,512]{1,0:T(8,128)}) custom-call(bf16[2,4,2,8,16,128]{5,4,3,2,1,0:T(8,128)(2,1)} %bitcast.7, bf16[2,4,2,8,16,128]{5,4,3,2,1,0:T(8,128)(2,1)} %bitcast.8, bf16[2,4,2,8,16,128]{5,4,3,2,1,0:T(8,128)(2,1)} %bitcast.9, bf16[2,4,2,8,16,128]{5,4,3,2,1,0:T(8,128)(2,1)} %bitcast.10, ...), custom_call_target="tpu_custom_call" | custom-call | tf_op jit(solution)/shard_map/pallas_call | solution.py:780
